TPU v7x, 32 devices: a whole 2x2x4 slice. The times are simulated.
32 devices in a mesh: group: 4 (over y, core), dp: 8 (over z, x).
Axes of the slice: x: 2, y: 2, z: 4, core: 2. Of those that a mesh axis runs over, the one named last changes fastest.
Arguments:
- pixels: bfloat16 [4, 96, 64, 12, 256], P('group', 'dp'), may hold values from -6 to 6
- patch_index: int32 [4, 96, 64], P('group', 'dp'), may hold values from 0 to 195, as said below
- kept_count: int32 [4, 96], P('group', 'dp'), may hold values from 21 to 64, as said below
- wavelength: int32 [4, 12], P('group'), may hold values from 400 to 2499
- weight_tokens: bfloat16 [128, 128], replicated, may hold values from -6 to 6
- bias_token: bfloat16 [128], replicated, may hold values from -6 to 6
- hyper_project: bfloat16 [128, 384], replicated, may hold values from -0.5 to 0.5
- hyper_output: bfloat16 [128, 128], replicated, may hold values from -0.5 to 0.5
- hyper_gains: bfloat16 [2, 128], replicated, may hold values from 0.5 to 1.5
- hyper_shifts: bfloat16 [2, 128], replicated, may hold values from -3 to 3
- hyper_up: bfloat16 [128, 2048], replicated, may hold values from -0.5 to 0.5
- hyper_down: bfloat16 [2048, 128], replicated, may hold values from -0.125 to 0.125
- kernel_weight: bfloat16 [128, 256, 768], P(None, 'dp'), may hold values from -0.5 to 0.5
- kernel_bias: bfloat16 [256, 768], P('dp'), may hold values from -6 to 6
- bias_weight: bfloat16 [128, 768], replicated, may hold values from -2 to 2
- bias_shift: bfloat16 [768], replicated, may hold values from -120 to 120
- attention_in: bfloat16 [768, 2304], P('dp'), may hold values from -0.21875 to 0.21875
- attention_out: bfloat16 [768, 768], P('dp'), may hold values from -0.625 to 0.625
- expand_weight: bfloat16 [768, 3072], P('dp'), may hold values from -0.21875 to 0.21875
- reduce_weight: bfloat16 [3072, 768], P('dp'), may hold values from -0.15625 to 0.15625
- norm_gains: bfloat16 [2, 768], replicated, may hold values from 0.5 to 1.5
- norm_shifts: bfloat16 [2, 768], replicated, may hold values from -3 to 3
- attention_bias: bfloat16 [2, 768], replicated, may hold values from -3 to 3
- output_bias: bfloat16 [768], replicated, may hold values from -3 to 3
- expand_bias: bfloat16 [3072], replicated, may hold values from -3 to 3
- reduce_bias: bfloat16 [768], replicated, may hold values from -3 to 3
- cotangent: bfloat16 [4, 96, 64, 768], P('group', 'dp'), may hold values from -6 to 6
Outputs:
- encoded: bfloat16 [4, 96, 64, 768], P('group', 'dp')
- pixel_grad: bfloat16 [4, 96, 64, 12, 256], P('group', 'dp')
- weight_tokens_grad: float32 [128, 128], replicated
- bias_token_grad: float32 [128], replicated
- hyper_project_grad: float32 [128, 384], replicated
- hyper_output_grad: float32 [128, 128], replicated
- hyper_gains_grad: float32 [2, 128], replicated
- hyper_shifts_grad: float32 [2, 128], replicated
- hyper_up_grad: float32 [128, 2048], replicated
- hyper_down_grad: float32 [2048, 128], replicated
- kernel_weight_grad: float32 [128, 256, 768], P(None, 'dp')
- kernel_bias_grad: float32 [256, 768], P('dp')
- bias_weight_grad: float32 [128, 768], replicated
- bias_shift_grad: float32 [768], replicated
- attention_in_grad: float32 [768, 2304], P('dp')
- attention_out_grad: float32 [768, 768], P('dp')
- expand_weight_grad: float32 [768, 3072], P('dp')
- reduce_weight_grad: float32 [3072, 768], P('dp')
- norm_gains_grad: float32 [2, 768], replicated
- norm_shifts_grad: float32 [2, 768], replicated
- attention_bias_grad: float32 [2, 768], replicated
- output_bias_grad: float32 [768], replicated
- expand_bias_grad: float32 [3072], replicated
- reduce_bias_grad: float32 [768], replicated
Inputs may be any that keep to these rules, and one draw needn't show every extreme that they name: `patch_index`: within an image the 64 entries are distinct patch numbers; slots at or past the image's kept_count are padding. `kept_count`: in every group at least one image keeps all 64 slots.
All inputs are finite; a program needn't handle non-finite values.
Results may differ from a plain program's by a relative error of at most 0.019.
Values may be sent and summed in bfloat16 or wider, within the bound.
No kernel may reach another device: no remote copies, remote signals or barrier semaphores. Data moves between devices by JAX's collectives and lax.ppermute only.
A program may use at most 256 MiB of HBM per device.

v0:
```python
from functools import partial

import jax
import jax.numpy as jnp
from jax import lax
from jax.sharding import PartitionSpec as P

HEADS = 12
HE = 128
HH = 4
SIDE = 14


scaler = 0.01
highest = lax.Precision.HIGHEST


def layer_norm(values, gain_row, shift_row, epsilon):
    center = values - jnp.mean(values, -1, keepdims=True)
    scaled = center * lax.rsqrt(jnp.mean(center * center, -1, keepdims=True) + epsilon)
    return scaled * gain_row + shift_row


def norm_parts(values, epsilon):
    center = values - jnp.mean(values, -1, keepdims=True)
    inverse = lax.rsqrt(jnp.mean(center * center, -1, keepdims=True) + epsilon)
    return (center * inverse, inverse)


def norm_back(grad_rows, normed, inverse, gain_row):
    scaled = grad_rows * gain_row
    return inverse * (
        scaled
        - jnp.mean(scaled, -1, keepdims=True)
        - normed * jnp.mean(scaled * normed, -1, keepdims=True)
    )


def contract_rows(operand, partner):
    return lax.dot_general(
        operand, partner, (((0,), (0,)), ((), ())), preferred_element_type=jnp.float32
    )


def contract_last(operand, partner):
    return lax.dot_general(
        operand, partner, (((1,), (1,)), ((), ())), preferred_element_type=jnp.float32
    )


def wave_embed(wave_ids):
    half_width = HE // 2
    frequency = 1.0 / 10000.0 ** (jnp.arange(half_width, dtype=jnp.float32) / half_width)
    angles = wave_ids.astype(jnp.float32)[:, None] * frequency
    return jnp.concatenate([jnp.sin(angles), jnp.cos(angles)], -1)


def place_embed(patch_ids, model_width):
    quarter = model_width // 4
    frequency = 1.0 / 10000.0 ** (jnp.arange(quarter, dtype=jnp.float32) / quarter)
    row_angle = (patch_ids // SIDE).astype(jnp.float32)[..., None] * frequency
    col_angle = (patch_ids % SIDE).astype(jnp.float32)[..., None] * frequency
    return jnp.concatenate(
        [jnp.sin(row_angle), jnp.cos(row_angle), jnp.sin(col_angle), jnp.cos(col_angle)], -1
    )


def hyper_core(
    wave_rows,
    weight_tokens,
    bias_token,
    hyper_project,
    hyper_output,
    hyper_gains,
    hyper_shifts,
    hyper_up,
    hyper_down,
):
    token_count = weight_tokens.shape[0]
    band_count = wave_rows.shape[0]
    sequence = jnp.concatenate([weight_tokens, wave_rows, bias_token[None, :]], 0)
    length = sequence.shape[0]
    project = jnp.dot(sequence, hyper_project, precision=highest)
    split_heads = project.reshape(length, 3, HH, -1)
    queries = split_heads[:, 0]
    keys_all = split_heads[:, 1]
    values_all = split_heads[:, 2]
    scores = jnp.einsum("qhd,khd->hqk", queries, keys_all, precision=highest) * queries.shape[
        -1
    ] ** (-0.5)
    weights = jax.nn.softmax(scores, -1)
    mixed_rows = jnp.einsum("hqk,khd->qhd", weights, values_all, precision=highest).reshape(
        length, -1
    )
    hidden = layer_norm(
        sequence + jnp.dot(mixed_rows, hyper_output, precision=highest),
        hyper_gains[0],
        hyper_shifts[0],
        1e-05,
    )
    expanded = jax.nn.gelu(jnp.dot(hidden, hyper_up, precision=highest), approximate=False)
    hidden = layer_norm(
        hidden + jnp.dot(expanded, hyper_down, precision=highest),
        hyper_gains[1],
        hyper_shifts[1],
        1e-05,
    )
    band_feats = hidden[token_count : token_count + band_count] + wave_rows
    return (band_feats, hidden[length - 1])


def masked_scores(queries, keys_all, valid_mask, score_scale):
    scores = (
        jnp.einsum("iqhd,ikhd->ihqk", queries, keys_all, preferred_element_type=jnp.float32)
        * score_scale
    )
    return jnp.where(valid_mask[:, None, None, :], scores, -1000000000.0)


def on_device(
    pixels,
    patch_index,
    kept_count,
    wavelength,
    weight_tokens,
    bias_token,
    hyper_project,
    hyper_output,
    hyper_gains,
    hyper_shifts,
    hyper_up,
    hyper_down,
    kernel_weight,
    kernel_bias,
    bias_weight,
    bias_shift,
    attention_in,
    attention_out,
    expand_weight,
    reduce_weight,
    norm_gains,
    norm_shifts,
    attention_bias,
    output_bias,
    expand_bias,
    reduce_bias,
    cotangent,
):
    floaty = jnp.float32
    lowtype = jnp.bfloat16
    image_count, slot_count, band_count, pixel_count = pixels.shape[1:]
    model_width = cotangent.shape[-1]
    row_count = image_count * slot_count
    head_count = HEADS
    head_size = model_width // head_count
    score_scale = head_size ** (-0.5)
    pixel_rows = pixels.reshape(row_count, band_count, pixel_count)
    valid_mask = (
        lax.broadcasted_iota(jnp.int32, (image_count, slot_count), 1) < kept_count[0][:, None]
    )
    valid_rows = valid_mask.reshape(row_count, 1).astype(floaty)
    wave_rows = wave_embed(wavelength[0])
    hyper_params = tuple(
        (
            member.astype(floaty)
            for member in (
                weight_tokens,
                bias_token,
                hyper_project,
                hyper_output,
                hyper_gains,
                hyper_shifts,
                hyper_up,
                hyper_down,
            )
        )
    )
    (band_feats, bias_feat), hyper_back = jax.vjp(partial(hyper_core, wave_rows), *hyper_params)
    shard_weight = kernel_weight.astype(floaty)
    shard_bias = kernel_bias.astype(floaty)
    kernel_part = (
        scaler
        * (
            jnp.einsum("bh,hpd->pbd", band_feats, shard_weight, precision=highest)
            + shard_bias[:, None, :]
        )
    ).astype(lowtype)
    bias_matrix = bias_weight.astype(floaty)
    conv_bias = scaler * (
        jnp.dot(bias_feat, bias_matrix, precision=highest) + bias_shift.astype(floaty)
    )
    window = pixel_rows
    conv_out = jnp.einsum(
        "rbp,pbd->rd",
        window,
        lax.all_gather(kernel_part, "dp", axis=0, tiled=True),
        preferred_element_type=floaty,
    )
    start = conv_out + conv_bias + place_embed(patch_index[0].reshape(row_count), model_width)
    wide_in, wide_out, wide_up, wide_down = (
        lax.all_gather(attention_in, "dp", axis=0, tiled=True),
        lax.all_gather(attention_out, "dp", axis=0, tiled=True),
        lax.all_gather(expand_weight, "dp", axis=0, tiled=True),
        lax.all_gather(reduce_weight, "dp", axis=0, tiled=True),
    )
    gains = norm_gains.astype(floaty)
    shifts = norm_shifts.astype(floaty)
    normed_one, inverse_one = norm_parts(start, 1e-06)
    hidden_one = (normed_one * gains[0] + shifts[0]).astype(lowtype)
    bias_full = jnp.concatenate(
        [
            attention_bias[0].astype(floaty),
            jnp.zeros((model_width,), floaty),
            attention_bias[1].astype(floaty),
        ]
    )
    project = (jnp.dot(hidden_one, wide_in, preferred_element_type=floaty) + bias_full).astype(
        lowtype
    )
    split_heads = project.reshape(image_count, slot_count, 3, head_count, head_size)
    queries = split_heads[:, :, 0]
    keys_all = split_heads[:, :, 1]
    values_all = split_heads[:, :, 2]
    masked = masked_scores(queries, keys_all, valid_mask, score_scale)
    row_peak = jnp.max(masked, -1, keepdims=True)
    log_total = row_peak + jnp.log(jnp.sum(jnp.exp(masked - row_peak), -1, keepdims=True))
    probs_low = jnp.exp(masked - log_total).astype(lowtype)
    mixed_rows = (
        jnp.einsum("ihqk,ikhd->iqhd", probs_low, values_all, preferred_element_type=floaty)
        .astype(lowtype)
        .reshape(row_count, model_width)
    )
    middle = (
        start
        + jnp.dot(mixed_rows, wide_out, preferred_element_type=floaty)
        + output_bias.astype(floaty)
    )
    normed_two, inverse_two = norm_parts(middle, 1e-06)
    hidden_two = (normed_two * gains[1] + shifts[1]).astype(lowtype)
    expand_pre = jnp.dot(hidden_two, wide_up, preferred_element_type=floaty) + expand_bias.astype(
        floaty
    )
    activated = jax.nn.gelu(expand_pre, approximate=False).astype(lowtype)
    final_rows = (
        middle
        + jnp.dot(activated, wide_down, preferred_element_type=floaty)
        + reduce_bias.astype(floaty)
    ) * valid_rows
    encoded = final_rows.astype(lowtype).reshape(cotangent.shape)
    out_grad = cotangent.reshape(row_count, model_width).astype(floaty) * valid_rows
    out_low = out_grad.astype(lowtype)
    grad_down = contract_rows(activated, out_low)
    act_grad = contract_last(out_low, wide_down)
    gelu_part, gelu_back = jax.vjp(partial(jax.nn.gelu, approximate=False), expand_pre)
    pre_grad = gelu_back(act_grad)[0]
    pre_low = pre_grad.astype(lowtype)
    grad_up = contract_rows(hidden_two, pre_low)
    hidden_two_grad = contract_last(pre_low, wide_up)
    middle_grad = out_grad + norm_back(hidden_two_grad, normed_two, inverse_two, gains[1])
    middle_low = middle_grad.astype(lowtype)
    grad_out = contract_rows(mixed_rows, middle_low)
    mixed_low = (
        contract_last(middle_low, wide_out)
        .astype(lowtype)
        .reshape(image_count, slot_count, head_count, head_size)
    )
    masked = masked_scores(queries, keys_all, valid_mask, score_scale)
    probs_full = jnp.exp(masked - log_total)
    probs_again = probs_full.astype(lowtype)
    value_grad = jnp.einsum(
        "ihqk,iqhd->ikhd", probs_again, mixed_low, preferred_element_type=floaty
    )
    prob_grad = jnp.einsum("iqhd,ikhd->ihqk", mixed_low, values_all, preferred_element_type=floaty)
    score_grad = probs_full * (prob_grad - jnp.sum(prob_grad * probs_full, -1, keepdims=True))
    score_low = score_grad.astype(lowtype)
    query_grad = (
        jnp.einsum("ihqk,ikhd->iqhd", score_low, keys_all, preferred_element_type=floaty)
        * score_scale
    )
    key_grad = (
        jnp.einsum("ihqk,iqhd->ikhd", score_low, queries, preferred_element_type=floaty)
        * score_scale
    )
    project_low = (
        jnp.stack([query_grad, key_grad, value_grad], 2)
        .reshape(row_count, 3 * model_width)
        .astype(lowtype)
    )
    grad_in = contract_rows(hidden_one, project_low)
    project_wide = project_low.astype(floaty)
    hidden_one_grad = contract_last(project_low, wide_in)
    start_grad = middle_grad + norm_back(hidden_one_grad, normed_one, inverse_one, gains[0])
    conv_low = start_grad.astype(lowtype)
    small_grads = lax.psum(
        (
            jnp.stack(
                [jnp.sum(hidden_one_grad * normed_one, 0), jnp.sum(hidden_two_grad * normed_two, 0)]
            ),
            jnp.stack([jnp.sum(hidden_one_grad, 0), jnp.sum(hidden_two_grad, 0)]),
            jnp.stack(
                [
                    jnp.sum(project_wide[:, :model_width], 0),
                    jnp.sum(project_wide[:, 2 * model_width :], 0),
                ]
            ),
            jnp.sum(middle_grad, 0),
            jnp.sum(pre_grad, 0),
            jnp.sum(out_grad, 0),
        ),
        ("group", "dp"),
    )
    window = pixel_rows
    kernel_grad = lax.psum_scatter(
        jnp.einsum("rbp,rd->pbd", window, conv_low, preferred_element_type=floaty),
        "dp",
        scatter_dimension=0,
        tiled=True,
    )
    pixel_grad = jnp.einsum(
        "rd,pbd->rbp",
        conv_low,
        lax.all_gather(kernel_part, "dp", axis=0, tiled=True),
        preferred_element_type=floaty,
    )
    pixel_grad = pixel_grad.astype(lowtype).reshape(pixels.shape)
    feats_part = scaler * jnp.einsum("pbd,hpd->bh", kernel_grad, shard_weight, precision=highest)
    feats_grad, conv_bias_grad = lax.psum((feats_part, jnp.sum(start_grad, 0)), "dp")
    weight_shard_grad = scaler * jnp.einsum(
        "bh,pbd->hpd", band_feats, kernel_grad, precision=highest
    )
    bias_shard_grad = scaler * jnp.sum(kernel_grad, 1)
    bias_weight_grad = scaler * bias_feat[:, None] * conv_bias_grad[None, :]
    bias_shift_grad = scaler * conv_bias_grad
    bias_feat_grad = scaler * jnp.dot(bias_matrix, conv_bias_grad, precision=highest)
    hyper_grad = hyper_back((feats_grad, bias_feat_grad))
    summed = (
        lax.psum(hyper_grad[0].astype(jnp.bfloat16), "group").astype(jnp.float32),
        lax.psum(hyper_grad[1].astype(jnp.bfloat16), "group").astype(jnp.float32),
        lax.psum(hyper_grad[2].astype(jnp.bfloat16), "group").astype(jnp.float32),
        lax.psum(hyper_grad[3].astype(jnp.bfloat16), "group").astype(jnp.float32),
        lax.psum(hyper_grad[4].astype(jnp.bfloat16), "group").astype(jnp.float32),
        lax.psum(hyper_grad[5].astype(jnp.bfloat16), "group").astype(jnp.float32),
        lax.psum(hyper_grad[6].astype(jnp.bfloat16), "group").astype(jnp.float32),
        lax.psum(hyper_grad[7].astype(jnp.bfloat16), "group").astype(jnp.float32),
        lax.psum(weight_shard_grad.astype(jnp.bfloat16), "group").astype(jnp.float32),
        lax.psum(bias_shard_grad.astype(jnp.bfloat16), "group").astype(jnp.float32),
        lax.psum(bias_weight_grad.astype(jnp.bfloat16), "group").astype(jnp.float32),
        lax.psum(bias_shift_grad.astype(jnp.bfloat16), "group").astype(jnp.float32),
    )
    block_shards = (
        lax.psum_scatter(grad_in, "dp", scatter_dimension=0, tiled=True),
        lax.psum_scatter(grad_out, "dp", scatter_dimension=0, tiled=True),
        lax.psum_scatter(grad_up, "dp", scatter_dimension=0, tiled=True),
        lax.psum_scatter(grad_down, "dp", scatter_dimension=0, tiled=True),
    )
    block_shards = (
        lax.psum(block_shards[0].astype(jnp.bfloat16), "group").astype(jnp.float32),
        lax.psum(block_shards[1].astype(jnp.bfloat16), "group").astype(jnp.float32),
        lax.psum(block_shards[2].astype(jnp.bfloat16), "group").astype(jnp.float32),
        lax.psum(block_shards[3].astype(jnp.bfloat16), "group").astype(jnp.float32),
    )
    return (
        encoded,
        pixel_grad,
        summed[0],
        summed[1],
        summed[2],
        summed[3],
        summed[4],
        summed[5],
        summed[6],
        summed[7],
        summed[8],
        summed[9],
        summed[10],
        summed[11],
        block_shards[0],
        block_shards[1],
        block_shards[2],
        block_shards[3],
        small_grads[0],
        small_grads[1],
        small_grads[2],
        small_grads[3],
        small_grads[4],
        small_grads[5],
    )


def solution(mesh):
    placed = (
        P("group", "dp", None, None, None),
        P("group", "dp", None),
        P("group", "dp"),
        P("group", None),
        P(),
        P(),
        P(),
        P(),
        P(),
        P(),
        P(),
        P(),
        P(None, "dp", None),
        P("dp", None),
        P(),
        P(),
        P("dp", None),
        P("dp", None),
        P("dp", None),
        P("dp", None),
        P(),
        P(),
        P(),
        P(),
        P(),
        P(),
        P("group", "dp", None, None),
    )
    return jax.shard_map(
        on_device,
        mesh=mesh,
        in_specs=placed,
        out_specs=(
            P("group", "dp", None, None),
            P("group", "dp", None, None, None),
            P(),
            P(),
            P(),
            P(),
            P(),
            P(),
            P(),
            P(),
            P(None, "dp", None),
            P("dp", None),
            P(),
            P(),
            P("dp", None),
            P("dp", None),
            P("dp", None),
            P("dp", None),
            P(),
            P(),
            P(),
            P(),
            P(),
            P(),
        ),
        check_vma=False,
    )
```

profile of v0, /device:TPU:0, one launch (start us, length us, event | category | flops | bytes accessed | tf_op | source)
XLA Modules:
  0.0 1419.0 jit_solution(18022485400869557949)
XLA Ops:
  21.4 20.3 %fusion.28 = bf16[32,12,768]{2,1,0:T(8,128)(2,1)S(1)} fusion(bf16[128,32,768]{2,1,0:T(8,128)(2,1)S(1)} %bitcast.192, f32[32,768]{1,0:T(8,128)S(1)} %convert_element_type.258, f32[141,128]{1,0:T(8,128)S(1)} %multiply_add_fusion.4, f32[12,64]{1,0:T(8,128)S(1)} %get-tuple-element.168, f32[12,64]{1,0:T(8,128)S(1)} %get-tuple-element.167), kind=kOutput, calls=%fused_computation.78 | convolution fusion | flops 453872640 | bytes 7004160 | tf_op jit(solution)/shard_map/bh,hpd->pbd/dot_general | solution.py:184
  53.2 7.0 multiply_sine_fusion.1
  60.2 65.5 %all-gather.6.cloned.1.call-done = bf16[256,12,768]{2,0,1:T(8,128)(2,1)} async-done(((bf16[32,12,768]{2,0,1:T(8,128)(2,1)}), bf16[256,12,768]{2,0,1:T(8,128)(2,1)}) %all-gather.6.cloned.1.call-update) | async-done | bytes 4718608 | tf_op jit(solution)/shard_map/all_gather | solution.py:196
  125.7 8.6 fusion.112
  134.7 56.5 %all-gather.8.cloned.1.call-done = bf16[768,2304]{1,0:T(8,128)(2,1)} async-done(((bf16[96,2304]{1,0:T(8,128)(2,1)}), bf16[768,2304]{1,0:T(8,128)(2,1)}) %all-gather.8.cloned.1.call-update) | async-done | bytes 3538960 | tf_op jit(solution)/shard_map/all_gather | solution.py:201
  197.9 11.5 reshape.331
  209.4 6.7 fusion.108
  246.7 67.0 %all-gather.12.cloned.1.call-done = bf16[768,3072]{1,0:T(8,128)(2,1)} async-done(((bf16[96,3072]{1,0:T(8,128)(2,1)}), bf16[768,3072]{1,0:T(8,128)(2,1)}) %all-gather.12.cloned.1.call-update) | async-done | bytes 4718608 | tf_op jit(solution)/shard_map/all_gather | solution.py:203
  313.7 10.6 fusion.102
  324.3 69.5 %all-gather.14.cloned.1.call-done = bf16[3072,768]{1,0:T(8,128)(2,1)} async-done(((bf16[384,768]{1,0:T(8,128)(2,1)}), bf16[3072,768]{1,0:T(8,128)(2,1)}) %all-gather.14.cloned.1.call-update) | async-done | bytes 4718608 | tf_op jit(solution)/shard_map/all_gather | solution.py:204
  393.8 30.8 %fusion.103 = (f32[3072]{0:T(1024)}, bf16[768,3072]{1,0:T(8,128)(2,1)S(1)}, f32[768,3072]{1,0:T(8,128)}) fusion(f32[768,3072]{1,0:T(8,128)} %fusion.102, f32[3072]{0:T(1024)S(1)} %convert_element_type.277, bf16[768,768]{1,0:T(8,128)(2,1)} %fusion.22, bf16[3072,768]{1,0:T(8,128)(2,1)} %all-gather.14.cloned.1.call-done), kind=kOutput, calls=%fused_computation.240 | convolution fusion | flops 3798463488 | bytes 29515776 | tf_op jit(solution)/shard_map/dot_general | solution.py:46
  466.9 12.3 copy.138
  479.2 12.2 convert_element_type.290
  491.3 7.3 fusion.101
  498.7 7.3 multiply_reduce_fusion.3
  508.2 8.5 convolution_bitcast_fusion
  516.8 11.7 copy.141
  530.2 9.0 fusion.18
  539.3 11.4 multiply_convert_fusion.1
  550.7 10.3 fusion.114
  564.5 69.7 %reduce-scatter.8.cloned.1.call-done = f32[96,2304]{1,0:T(8,128)} async-done(((f32[768,2304]{1,0:T(8,128)}), f32[96,2304]{1,0:T(8,128)}) %reduce-scatter.8.cloned.1.call-update) | async-done | bytes 884752 | tf_op jit(solution)/shard_map/reduce_scatter | solution.py:351
  636.1 209.0 %reduce-scatter.6.cloned.1.call-done = f32[32,12,768]{2,1,0:T(8,128)} async-done(((f32[256,12,768]{2,1,0:T(8,128)}), f32[32,12,768]{2,1,0:T(8,128)}) %reduce-scatter.6.cloned.1.call-update) | async-done | bytes 1179664 | tf_op jit(solution)/shard_map/reduce_scatter | solution.py:313
  845.2 10.6 fusion.43
  855.9 37.8 %all-reduce.10 = (f32[12,128]{1,0:T(8,128)S(1)}, f32[768]{0:T(1024)S(1)}) all-reduce(f32[12,128]{1,0:T(8,128)S(1)} %fusion.43, f32[768]{0:T(1024)S(1)} %get-tuple-element.152), channel_id=1, replica_groups=mesh['group'=4,'dp'=8] {'dp'}, use_global_device_ids=true, to_apply=%region_20.21 | all-reduce | flops 2304 | bytes 18432 | tf_op jit(solution)/shard_map/psum | solution.py:327
  920.4 14.2 multiply_convert_fusion
  935.4 76.3 %reduce-scatter.12.cloned.1.call-done = f32[96,3072]{1,0:T(8,128)} async-done(((f32[768,3072]{1,0:T(8,128)}), f32[96,3072]{1,0:T(8,128)}) %reduce-scatter.12.cloned.1.call-update) | async-done | bytes 1179664 | tf_op jit(solution)/shard_map/reduce_scatter | solution.py:353
  1013.9 164.2 %reduce-scatter.14.cloned.1.call-done = f32[384,768]{1,0:T(8,128)} async-done(((f32[3072,768]{1,0:T(8,128)}), f32[384,768]{1,0:T(8,128)}) %reduce-scatter.14.cloned.1.call-update) | async-done | bytes 1179664 | tf_op jit(solution)/shard_map/reduce_scatter | solution.py:354
  1188.2 7.8 convert_bitcast_fusion
  1210.7 41.6 %all-reduce.9 = (f32[2,768]{1,0:T(2,128)}, f32[2,768]{1,0:T(2,128)}, f32[2,768]{1,0:T(2,128)}, f32[768]{0:T(1024)}, f32[3072]{0:T(1024)}, /*index=5*/f32[768]{0:T(1024)}) all-reduce(f32[2,768]{1,0:T(2,128)S(1)} %pad_maximum_fusion.3, f32[2,768]{1,0:T(2,128)S(1)} %pad_maximum_fusion.4, ...), channel_id=1, replica_groups=mesh['group'=4,'dp'=8] {'group','dp'}, use_global_device_ids=true, to_apply=%region_53.54 | all-reduce | flops 9216 | bytes 73728 | tf_op jit(solution)/shard_map/psum | solution.py:294
  1252.3 8.6 multiply_convert_fusion.5
  1270.1 122.0 %all-reduce.18.cloned.1.call-done = (bf16[128,32,768]{2,0,1:T(8,128)(2,1)}, bf16[128,384]{1,0:T(8,128)(2,1)}, bf16[128,2048]{1,0:T(8,128)(2,1)}, bf16[2048,128]{...) async-done(((bf16[128,32,768]{2,0,1:T(8,128)(2,1)}, ...) | async-done | bytes 9404432 | tf_op jit(solution)/shard_map/psum | solution.py:345
  1403.5 8.4 copy.149
  (407 shorter events, 189.0 us)
Async XLA Ops:
  7.2 118.5 %all-gather.6.cloned.1.call-start = ((), (), s32[]{:S(2)}) async-start(), calls=%async_computation.5 | async-start | bytes 5308416 | tf_op jit(solution)/shard_map/all_gather | solution.py:196
  21.4 30.2 %copy-start.63 = (f32[141,128]{1,0:T(8,128)}, f32[141,128]{1,0:T(8,128)S(1)}, u32[]{:S(2)}) copy-start(f32[141,128]{1,0:T(8,128)S(1)} %multiply_add_fusion.4) | copy-start | bytes 216580
  42.9 148.3 %all-gather.8.cloned.1.call-start = ((), (), s32[]{:S(2)}) async-start(), calls=%async_computation.6 | async-start | bytes 3981312 | tf_op jit(solution)/shard_map/all_gather | solution.py:201
  43.6 198.3 %all-gather.10.cloned.1.call-start = ((), (), s32[]{:S(2)}) async-start(), calls=%async_computation.7 | async-start | bytes 1327104 | tf_op jit(solution)/shard_map/all_gather | solution.py:202
  44.4 269.3 %all-gather.12.cloned.1.call-start = ((), (), s32[]{:S(2)}) async-start(), calls=%async_computation.8 | async-start | bytes 5308416 | tf_op jit(solution)/shard_map/all_gather | solution.py:203
  45.0 348.8 %all-gather.14.cloned.1.call-start = ((), (), s32[]{:S(2)}) async-start(), calls=%async_computation.9 | async-start | bytes 5308416 | tf_op jit(solution)/shard_map/all_gather | solution.py:204
  45.5 517.3 %reduce-scatter.10.cloned.1.call-start = ((), (), s32[]{:S(2)}) async-start(), calls=%async_computation.12 | async-start | bytes 2654208 | tf_op jit(solution)/shard_map/reduce_scatter | solution.py:352
  45.8 181.4 %copy-start.66 = (pred[12,64]{1,0:T(8,128)(4,1)}, pred[12,64]{1,0:T(8,128)(4,1)S(1)}, u32[]{:S(2)}) copy-start(pred[12,64]{1,0:T(8,128)(4,1)S(1)} %get-tuple-element.172) | copy-start | bytes 2308
  51.6 139.6 %copy-start.53 = (f32[768]{0:T(1024)}, f32[768]{0:T(1024)S(1)}, u32[]{:S(2)}) copy-start(f32[768]{0:T(1024)S(1)} %get-tuple-element.114) | copy-start | bytes 9220
  51.7 139.5 %copy-start.57 = (f32[768]{0:T(1024)}, f32[768]{0:T(1024)S(1)}, u32[]{:S(2)}) copy-start(f32[768]{0:T(1024)S(1)} %get-tuple-element.116) | copy-start | bytes 9220
  51.7 262.0 %copy-start.59 = (f32[768]{0:T(1024)}, f32[768]{0:T(1024)S(1)}, u32[]{:S(2)}) copy-start(f32[768]{0:T(1024)S(1)} %get-tuple-element.115) | copy-start | bytes 9220
  134.3 107.6 %copy-start.2 = (f32[768,768]{1,0:T(8,128)}, f32[768,768]{1,0:T(8,128)S(1)}, u32[]{:S(2)}) copy-start(f32[768,768]{1,0:T(8,128)S(1)} %get-tuple-element.182) | copy-start | bytes 7077892
  134.3 63.6 %copy-start.47 = (f32[768]{0:T(1024)}, f32[768]{0:T(1024)S(1)}, u32[]{:S(2)}) copy-start(f32[768]{0:T(1024)S(1)} %broadcast_multiply_fusion.5) | copy-start | bytes 9220
  134.7 63.2 %copy-start.55 = (f32[768]{0:T(1024)}, f32[768]{0:T(1024)S(1)}, u32[]{:S(2)}) copy-start(f32[768]{0:T(1024)S(1)} %add_rsqrt_fusion.1) | copy-start | bytes 9220
  324.3 100.3 %copy-start.5 = (f32[768,768]{1,0:T(8,128)S(1)}, f32[768,768]{1,0:T(8,128)}, u32[]{:S(2)}) copy-start(f32[768,768]{1,0:T(8,128)} %copy-done.4) | copy-start | bytes 7077892
  393.8 30.8 %copy-start.111 = (bf16[768,3072]{1,0:T(8,128)(2,1)S(1)}, bf16[768,3072]{1,0:T(8,128)(2,1)}, u32[]{:S(2)}) copy-start(bf16[768,3072]{1,0:T(8,128)(2,1)} %all-gather.12.cloned.1.call-done) | copy-start | bytes 14155780
  435.1 199.1 %reduce-scatter.8.cloned.1.call-start = ((), (), s32[]{:S(2)}) async-start(), calls=%async_computation.11 | async-start | bytes 7962624 | tf_op jit(solution)/shard_map/reduce_scatter | solution.py:351
  479.1 12.2 copy-start.48
  479.1 12.2 copy-start.54
  479.1 12.2 copy-start.56
  479.2 12.2 copy-start.58
  498.7 346.5 %reduce-scatter.6.cloned.1.call-start = ((), (), s32[]{:S(2)}) async-start(), calls=%async_computation.10 | async-start | bytes 14155776 | tf_op jit(solution)/shard_map/reduce_scatter | solution.py:313
  528.5 483.2 %reduce-scatter.12.cloned.1.call-start = ((), (), s32[]{:S(2)}) async-start(), calls=%async_computation.13 | async-start | bytes 10616832 | tf_op jit(solution)/shard_map/reduce_scatter | solution.py:353
  539.2 638.8 %reduce-scatter.14.cloned.1.call-start = ((), (), s32[]{:S(2)}) async-start(), calls=%async_computation.14 | async-start | bytes 10616832 | tf_op jit(solution)/shard_map/reduce_scatter | solution.py:354
  561.0 699.9 %all-reduce.16.cloned.1.call-start = ((), (), s32[]{:S(2)}) async-start(), calls=%async_computation.15 | async-start | bytes 531456 | tf_op jit(solution)/shard_map/psum | solution.py:346
  855.8 40.9 %copy-start.26 = (f32[141,128]{1,0:T(8,128)S(1)}, f32[141,128]{1,0:T(8,128)}, u32[]{:S(2)}) copy-start(f32[141,128]{1,0:T(8,128)} %copy-done.25) | copy-start | bytes 216580
  855.8 40.9 %copy-start.69 = (f32[141]{0:T(256)S(1)}, f32[141]{0:T(256)}, u32[]{:S(2)}) copy-start(f32[141]{0:T(256)} %copy-done.68) | copy-start | bytes 1696
  855.8 40.9 %copy-start.82 = (f32[128]{0:T(128)S(1)}, f32[128]{0:T(128)}, u32[]{:S(2)}) copy-start(f32[128]{0:T(128)} %copy-done.81) | copy-start | bytes 1540
  855.8 41.1 %copy-start.94 = (f32[141]{0:T(256)S(1)}, f32[141]{0:T(256)}, u32[]{:S(2)}) copy-start(f32[141]{0:T(256)} %copy-done.93) | copy-start | bytes 1696
  855.8 41.1 %copy-start.79 = (f32[141]{0:T(256)S(1)}, f32[141]{0:T(256)}, u32[]{:S(2)}) copy-start(f32[141]{0:T(256)} %copy-done.78) | copy-start | bytes 1696
  920.4 14.2 %copy-start.109 = (f32[128]{0:T(128)S(1)}, f32[128]{0:T(128)}, u32[]{:S(2)}) copy-start(f32[128]{0:T(128)} %bitcast_multiply_fusion.1) | copy-start | bytes 1540
  920.4 471.7 %all-reduce.18.cloned.1.call-start = ((), (), s32[]{:S(2)}) async-start(), calls=%async_computation.16 | async-start | bytes 18808832 | tf_op jit(solution)/shard_map/psum | solution.py:345
  (96 other events, 375.5 us)
Sparse Core Ops, SparseCore 0:
  43.0 82.6 all-gather.5
  127.9 63.3 all-gather.7
  193.4 39.5 all-gather.9
  235.0 78.6 all-gather.11
  315.7 78.0 all-gather.13
  435.2 67.1 reduce-scatter.9
  506.0 128.0 reduce-scatter.7
  638.7 206.4 reduce-scatter.5
  849.2 162.4 reduce-scatter.11
  1015.6 162.3 reduce-scatter.13
  1182.2 30.8 all-reduce.15
  1217.9 174.1 all-reduce.17
where the time goes:
time: 1430 us; the launch traced here: 1420 us
  waiting for transfers between devices  902 us (63%)
  matrix products  218 us (15%)
  local copies, waits for them, and re-layouts  123 us (9%)
  other arithmetic  80.3 us (6%)
  blocking collectives  79.3 us (6%)
  between operations  16 us (1%)
    reduce_scatter x1, waiting for transfers between devices, on_device(): lax.psum_scatter(jnp.einsum('rbp,rd->pbd', window, conv_low, preferred_el...  209 us
    reduce_scatter x1, waiting for transfers between devices, on_device(): lax.psum_scatter(grad_down, 'dp', scatter_dimension=0, tiled=True)  164 us
    psum x1, waiting for transfers between devices, on_device(): lax.psum(weight_shard_grad.astype(jnp.bfloat16), 'group')  122 us
    reduce_scatter x1, waiting for transfers between devices, on_device(): lax.psum_scatter(grad_up, 'dp', scatter_dimension=0, tiled=True)  76.3 us
    reduce_scatter x1, waiting for transfers between devices, on_device(): lax.psum_scatter(grad_in, 'dp', scatter_dimension=0, tiled=True)  69.7 us
    all_gather x1, waiting for transfers between devices, on_device(): lax.all_gather(reduce_weight, 'dp', axis=0, tiled=True)  69.5 us
    all_gather x1, waiting for transfers between devices, on_device(): lax.all_gather(expand_weight, 'dp', axis=0, tiled=True)  67 us
    all_gather x1, waiting for transfers between devices, on_device(): lax.all_gather(kernel_part, 'dp', axis=0, tiled=True)  65.5 us
  transfers between devices with their start and end apart: 12, of which 9 were waited for; matrix products, arithmetic and copies ran while one was open for 22% of the time, Pallas kernels for 0%

commit v1 on v0

v1 whole, which is shorter than its diff:
```python
from functools import partial

import jax
import jax.numpy as jnp
import numpy as np
from jax import lax
from jax.experimental import pallas as pl
from jax.experimental.pallas import tpu as pltpu
from jax.sharding import PartitionSpec as P

HE = 128
HH = 4
SIDE = 14


scaler = 0.01
highest = lax.Precision.HIGHEST


def contract_rows(operand, partner):
    return lax.dot_general(
        operand, partner, (((0,), (0,)), ((), ())), preferred_element_type=jnp.float32
    )


def wave_embed(wave_ids):
    half_width = HE // 2
    frequency = 1.0 / 10000.0 ** (jnp.arange(half_width, dtype=jnp.float32) / half_width)
    angles = wave_ids.astype(jnp.float32)[:, None] * frequency
    return jnp.concatenate([jnp.sin(angles), jnp.cos(angles)], -1)


def place_table(model_width):
    quarter = model_width // 4
    frequency = 1.0 / 10000.0 ** (jnp.arange(quarter, dtype=jnp.float32) / quarter)
    angle = jnp.arange(SIDE, dtype=jnp.float32)[:, None] * frequency
    waves = jnp.concatenate([jnp.sin(angle), jnp.cos(angle)], -1)
    blank = jnp.zeros_like(waves)
    return jnp.concatenate(
        [jnp.concatenate([waves, blank], -1), jnp.concatenate([blank, waves], -1)], 0
    )


def place_spots(patch_ids, copies):
    lanes = jnp.arange(128, dtype=jnp.int32)[None, :]
    spot = lanes % (2 * SIDE + 1)
    row_id = (patch_ids // SIDE)[:, None]
    col_id = (patch_ids % SIDE)[:, None] + SIDE
    hit = (spot == row_id) | (spot == col_id) | (spot == 2 * SIDE)
    return (hit & (lanes < copies * (2 * SIDE + 1))).astype(jnp.bfloat16)


def split_low(values, count, axis):
    pieces = []
    for _ in range(count):
        piece = values.astype(jnp.bfloat16)
        pieces.append(piece)
        values = values - piece.astype(jnp.float32)
    return jnp.concatenate(pieces, axis)


def stage(*values):
    return lax.optimization_barrier(values)


class Links:
    def __init__(self, group_size, dp_size):
        self.group_size = group_size
        self.dp_size = dp_size
        group_id = lax.axis_index("group")
        dp_id = lax.axis_index("dp")
        self.y = group_id // 2
        self.c = group_id % 2
        self.x = dp_id % 2
        self.digits = []
        stride = 2
        while stride < dp_size:
            size = min(4, dp_size // stride)
            self.digits.insert(0, (size, stride, dp_id // stride % size))
            stride *= size
        self.line = dp_size // 2
        self.z = dp_id // 2

    def core(self, block):
        return lax.ppermute(block, "group", [(i, i ^ 1) for i in range(self.group_size)])

    def yside(self, block):
        return lax.ppermute(block, "group", [(i, i ^ 2) for i in range(self.group_size)])

    def xside(self, block):
        return lax.ppermute(block, "dp", [(i, i ^ 1) for i in range(self.dp_size)])

    def zside(self, block, step):
        return lax.ppermute(block, "dp", [(i, i ^ step) for i in range(self.dp_size)])

    def owner_pairs(self, target_of):
        pairs = []
        for group_id in range(self.group_size):
            for dp_id in range(self.dp_size):
                target = target_of(group_id, dp_id)
                if target is not None:
                    pairs.append(
                        (group_id * self.dp_size + dp_id, target[0] * self.dp_size + target[1])
                    )
        return pairs

    def owner_line(self, block):
        top = self.dp_size // 2
        pairs = self.owner_pairs(lambda g, d: (g, d ^ top) if d // top != g % 2 else None)
        return lax.ppermute(block, ("group", "dp"), pairs)

    def owner_core(self, block):
        top = self.dp_size // 2
        pairs = self.owner_pairs(lambda g, d: (g ^ 1, d) if d // top == g % 2 else None)
        return lax.ppermute(block, ("group", "dp"), pairs)


def pick(block, index, axis, count=1):
    return lax.dynamic_slice_in_dim(block, index, count, axis)


def add_low(one, two):
    return (one.astype(jnp.float32) + two.astype(jnp.float32)).astype(jnp.bfloat16)


def pair_up(block, other, bit, axis):
    return jnp.where(
        bit == 0,
        jnp.concatenate([block, other], axis),
        jnp.concatenate([other, block], axis),
    )


def place_digit(block, received, me, axis):
    size = len(received) + 1
    shape = block.shape[:axis] + (size,) + block.shape[axis + 1 :]
    out = jnp.zeros(shape, block.dtype)
    for step, piece in zip(range(size), [block] + received):
        at = tuple(me ^ step if i == axis else 0 for i in range(len(shape)))
        out = lax.dynamic_update_slice(out, piece, at)
    return out


def gather_line(links, piece, axis):
    lead, tail = piece.shape[:axis], piece.shape[axis + 1 :]
    count = len(links.digits)
    block = piece.reshape(lead + (1,) * count + tail)
    for place, (size, stride, me) in reversed(list(enumerate(links.digits))):
        received = [links.zside(block, stride * step) for step in range(1, size)]
        block = place_digit(block, received, me, axis + place)
    return block.reshape(lead + (links.line,) + tail)


def reduce_line(links, block, axis, sender):
    lead, tail = block.shape[:axis], block.shape[axis + 1 :]
    block = block.reshape(lead + tuple(size for size, _, _ in links.digits) + tail)
    for place, (size, stride, me) in enumerate(links.digits):
        if place:
            block = block.astype(jnp.bfloat16)
        received = [
            sender(pick(block, me ^ step, axis + place), stride * step) for step in range(1, size)
        ]
        block = pick(block, me, axis + place).astype(jnp.float32)
        for piece in received:
            block = block + piece.astype(jnp.float32)
    return block.reshape(lead + tail)


def attention_piece(links, attention_in, attention_out):
    width = attention_out.shape[1]
    thirds = [attention_in[:, i * width : (i + 1) * width] for i in range(3)]
    return lax.dynamic_index_in_dim(
        jnp.stack(thirds + [attention_out]), lax.axis_index("group"), 0, False
    )


def gather_feed(links, expand_weight, reduce_weight):
    width = reduce_weight.shape[1]
    count = links.group_size
    group_id = lax.axis_index("group")
    up = pick(expand_weight, group_id * width, 1, width)
    rows = reduce_weight.shape[0] // count
    down = pick(reduce_weight, group_id * rows, 0, rows)
    wide = lax.all_gather(jnp.stack([up, down]), ("dp", "group"), axis=0)
    wide = wide.reshape(links.dp_size, count, 2, rows, width)
    if rows % 16:
        up = wide[:, :, 0].transpose(1, 0, 2, 3).reshape(count, 8, width // 8, width)
        down = wide[:, :, 1].reshape(8, count, width // 8, width)
        wide = jnp.stack([up.transpose(1, 0, 2, 3), down], 2)
    return wide


def spread_group(links, piece):
    piece = piece.reshape((1, 1) + piece.shape)
    piece = pair_up(piece, links.yside(piece), links.y, 0)
    piece = pair_up(piece, links.core(piece), links.c, 1)
    return piece.reshape((-1,) + piece.shape[2:])


def sum_dp(links, values):
    step = 1
    while step < links.dp_size:
        values = values + links.zside(values, step)
        step *= 2
    return values


VMEM_BYTES = 60 * 1024 * 1024


def kernel_params():
    return pltpu.CompilerParams(vmem_limit_bytes=VMEM_BYTES)


def whole_spec(shape):
    return pl.BlockSpec(shape, lambda *_: (0,) * len(shape))


def norm_rows(values, epsilon):
    center = values - jnp.mean(values, -1, keepdims=True)
    inverse = lax.rsqrt(jnp.mean(center * center, -1, keepdims=True) + epsilon)
    return center * inverse, inverse


def dot_nn(one, two):
    return lax.dot_general(one, two, (((1,), (0,)), ((), ())), preferred_element_type=jnp.float32)


def dot_nt(one, two):
    return lax.dot_general(one, two, (((1,), (1,)), ((), ())), preferred_element_type=jnp.float32)


def dot_tn(one, two):
    return lax.dot_general(one, two, (((0,), (0,)), ((), ())), preferred_element_type=jnp.float32)


def embed_body(part_ref, pixel_ref, kernel_ref, norm_ref, start_ref, hidden_ref):
    start = part_ref[...] + dot_nn(pixel_ref[...], kernel_ref[...])
    start_ref[...] = start
    normed, _ = norm_rows(start, 1e-06)
    hidden_ref[...] = (normed * norm_ref[0:1, :] + norm_ref[1:2, :]).astype(jnp.bfloat16)


def embed_rows(part, pixel_rows, wide_kernel, norm_one, block_rows):
    rows = part.shape[0]
    depth = wide_kernel.shape[0]
    last = pixel_rows.shape[1] // depth - 1
    width = wide_kernel.shape[1]
    row_spec = lambda cols: pl.BlockSpec((block_rows, cols), lambda i: (i, 0))
    return pl.pallas_call(
        embed_body,
        grid=(rows // block_rows,),
        in_specs=[
            row_spec(width),
            pl.BlockSpec((block_rows, depth), lambda i: (i, last)),
            whole_spec(wide_kernel.shape),
            whole_spec(norm_one.shape),
        ],
        out_specs=[row_spec(width), row_spec(width)],
        out_shape=[
            jax.ShapeDtypeStruct((rows, width), jnp.float32),
            jax.ShapeDtypeStruct((rows, width), jnp.bfloat16),
        ],
        compiler_params=kernel_params(),
        cost_estimate=pl.CostEstimate(
            flops=2 * rows * depth * width,
            bytes_accessed=2 * (rows * depth + depth * width) + 6 * rows * width,
            transcendentals=0,
        ),
        name="embed_rows",
    )(part, pixel_rows, wide_kernel, norm_one)


def pair_stack(block, low_half):
    zero = jnp.zeros_like(block)
    return jnp.concatenate(
        [jnp.where(low_half, block, zero), jnp.where(low_half, zero, block)], 0
    )


def half_reduce(values, low_half, reducer, filler):
    first = reducer(jnp.where(low_half, values, filler), -1, keepdims=True)
    second = reducer(jnp.where(low_half, filler, values), -1, keepdims=True)
    return jnp.where(low_half, first, second)


def attend_body(
    first,
    count_ref,
    hidden_ref,
    start_ref,
    weight_ref,
    bias_ref,
    rows_ref,
    project_ref,
    probs_ref,
    mixed_ref,
    middle_ref,
    hidden_two_ref,
):
    block_rows, width = hidden_ref.shape
    slots = 64
    images = block_rows // slots
    base = (pl.program_id(0) + first) * images
    for third in range(3):
        at = third * width
        weight = weight_ref[:, third].reshape(width, width)
        project_ref[:, at : at + width] = (
            dot_nn(hidden_ref[...], weight) + bias_ref[:, at : at + width]
        ).astype(jnp.bfloat16)
    lanes = lax.broadcasted_iota(jnp.int32, (slots, 128), 1)
    low_half = lanes < 64
    key_id = jnp.where(low_half, lanes, lanes - 64)
    for image in range(images):
        count = count_ref[base + image]
        keep = key_id < count
        here = slice(image * slots, (image + 1) * slots)
        for pair in range(width // 128):
            at = pair * 128
            queries = project_ref[here, at : at + 128]
            keys = pair_stack(project_ref[here, width + at : width + at + 128], low_half)
            values = pair_stack(project_ref[here, 2 * width + at : 2 * width + at + 128], low_half)
            scores = jnp.where(keep, dot_nt(queries, keys) * 0.125, -1000000000.0)
            peak = half_reduce(scores, low_half, jnp.max, -3e38)
            probs = jnp.exp(scores - peak)
            total = half_reduce(probs, low_half, jnp.sum, 0.0)
            probs_low = (probs / total).astype(jnp.bfloat16)
            probs_ref[here, at : at + 128] = probs_low
            mixed_ref[here, at : at + 128] = dot_nn(probs_low, values).astype(jnp.bfloat16)
    middle = start_ref[...] + dot_nn(mixed_ref[...], weight_ref[:, 3].reshape(width, width)) + rows_ref[0:1, :]
    middle_ref[...] = middle
    normed, _ = norm_rows(middle, 1e-06)
    hidden_two_ref[...] = (normed * rows_ref[1:2, :] + rows_ref[2:3, :]).astype(jnp.bfloat16)


def attend_rows(first, steps, earlier, counts, hidden_one, start, weights, bias_full, rows_in):
    rows, width = hidden_one.shape
    block_rows = 128
    row_spec = lambda cols: pl.BlockSpec((block_rows, cols), lambda i, *_: (i + first, 0))
    low = jnp.bfloat16
    keep = list(earlier or ())

    def body(count_ref, *refs):
        refs = refs[:5] + refs[5 + len(keep) :]
        attend_body(first, count_ref, *refs)

    return pl.pallas_call(
        body,
        grid_spec=pltpu.PrefetchScalarGridSpec(
            num_scalar_prefetch=1,
            grid=(steps,),
            in_specs=[
                row_spec(width),
                row_spec(width),
                whole_spec(weights.shape),
                whole_spec(bias_full.shape),
                whole_spec(rows_in.shape),
                *(pl.BlockSpec(memory_space=pl.ANY) for _ in keep),
            ],
            out_specs=[
                row_spec(3 * width),
                row_spec(width),
                row_spec(width),
                row_spec(width),
                row_spec(width),
            ],
        ),
        out_shape=[
            jax.ShapeDtypeStruct((rows, 3 * width), low),
            jax.ShapeDtypeStruct((rows, width), low),
            jax.ShapeDtypeStruct((rows, width), low),
            jax.ShapeDtypeStruct((rows, width), jnp.float32),
            jax.ShapeDtypeStruct((rows, width), low),
        ],
        input_output_aliases={6 + i: i for i in range(len(keep))},
        compiler_params=kernel_params(),
        cost_estimate=pl.CostEstimate(
            flops=16 * steps * block_rows * width * width,
            bytes_accessed=8 * width * width + 20 * steps * block_rows * width,
            transcendentals=rows * width,
        ),
        name="attend_rows",
    )(counts, hidden_one, start, weights, bias_full, rows_in, *keep)


def expand_step(hidden_ref, turned_ref, out_ref, up_ref, bias_ref, down_ref):
    low = jnp.bfloat16
    out_low = out_ref[...]
    width = out_low.shape[1]
    up = up_ref[...].reshape(width, -1)
    down = down_ref[...].reshape(-1, width)
    pre = dot_nn(hidden_ref[...], up) + bias_ref[...]
    cumulative = 0.5 + 0.5 * lax.erf(pre * 0.7071067811865476)
    slope = cumulative + pre * (jnp.exp(pre * pre * -0.5) * 0.3989422804014327)
    activated = (pre * cumulative).astype(low)
    pre_grad = dot_nt(out_low, down) * slope
    pre_low = pre_grad.astype(low)
    return (
        jnp.sum(pre_grad, 0, keepdims=True),
        dot_nn(activated, down),
        dot_nt(pre_low, up),
        dot_nn(turned_ref[...], pre_low),
        dot_tn(activated, out_low),
    )


def accumulate(ref, part):
    @pl.when(pl.program_id(0) == 0)
    def _():
        ref[...] = part

    @pl.when(pl.program_id(0) > 0)
    def _():
        ref[...] += part


def first_body(
    half_ref,
    hidden_ref,
    out_ref,
    up_ref,
    bias_ref,
    down_ref,
    grad_up_ref,
    grad_down_ref,
    bias_grad_ref,
    forward_ref,
    back_ref,
    turned_ref,
):
    @pl.when(pl.program_id(0) == 0)
    def _():
        turned_ref[...] = hidden_ref[...].T

    bias_grad, forward_part, back_part, grad_up, grad_down = expand_step(
        hidden_ref, turned_ref, out_ref, up_ref, bias_ref, down_ref
    )
    bias_grad_ref[...] = bias_grad
    grad_up_ref[...] = grad_up.astype(jnp.bfloat16)
    grad_down_ref[...] = grad_down.astype(jnp.bfloat16)
    accumulate(forward_ref, forward_part)
    accumulate(back_ref, back_part)


def second_body(
    half_ref,
    hidden_ref,
    out_ref,
    up_ref,
    bias_ref,
    down_ref,
    forward_ref,
    back_ref,
    middle_ref,
    valid_ref,
    rows_ref,
    grad_up_ref,
    grad_down_ref,
    bias_grad_ref,
    encoded_ref,
    middle_grad_ref,
    middle_low_ref,
    sums_ref,
    forward_acc,
    back_acc,
    turned_ref,
):
    step = pl.program_id(0)
    low = jnp.bfloat16

    @pl.when(step == 0)
    def _():
        turned_ref[...] = hidden_ref[...].T
        forward_acc[...] = forward_ref[...]
        back_acc[...] = back_ref[...]

    bias_grad, forward_part, back_part, grad_up, grad_down = expand_step(
        hidden_ref, turned_ref, out_ref, up_ref, bias_ref, down_ref
    )
    bias_grad_ref[...] = bias_grad
    grad_up_ref[...] = grad_up.astype(low)
    grad_down_ref[...] = grad_down.astype(low)
    forward_acc[...] += forward_part
    back_acc[...] += back_part

    @pl.when(step == pl.num_programs(0) - 1)
    def _():
        middle = middle_ref[...]
        encoded_ref[...] = (
            (middle + forward_acc[...] + rows_ref[0:1, :]) * valid_ref[...]
        ).astype(low)
        normed, inverse = norm_rows(middle, 1e-06)
        grad = back_acc[...]
        out_grad = out_ref[...].astype(jnp.float32)
        scaled = grad * rows_ref[1:2, :]
        middle_grad = out_grad + inverse * (
            scaled
            - jnp.mean(scaled, -1, keepdims=True)
            - normed * jnp.mean(scaled * normed, -1, keepdims=True)
        )
        middle_grad_ref[...] = middle_grad
        middle_low_ref[...] = middle_grad.astype(low)
        sums_ref[0:1, :] = jnp.sum(grad * normed, 0, keepdims=True)
        sums_ref[1:2, :] = jnp.sum(grad, 0, keepdims=True)
        sums_ref[2:3, :] = jnp.sum(middle_grad, 0, keepdims=True)
        sums_ref[3:4, :] = jnp.sum(out_grad, 0, keepdims=True)


def expand_call(name, body, half, rows, width, ins, extra_ins, extra_outs, scratch):
    packed = ins[2].shape
    low = jnp.bfloat16
    steps = packed[1] // 2
    full = whole_spec((rows, width))
    place = lambda i, half: steps * half[0] + i
    return pl.pallas_call(
        body,
        grid_spec=pltpu.PrefetchScalarGridSpec(
            num_scalar_prefetch=1,
            grid=(steps,),
            in_specs=[
                full,
                full,
                pl.BlockSpec(
                    (packed[0], 1, 1) + packed[3:], lambda i, half: (0, place(i, half), 0, 0, 0)
                ),
                pl.BlockSpec((1, width), lambda i, half: (0, place(i, half))),
                pl.BlockSpec(
                    (packed[0] // packed[1], packed[1], 1) + packed[3:],
                    lambda i, half: (place(i, half), 0, 1, 0, 0),
                ),
                *extra_ins,
            ],
            out_specs=[
                pl.BlockSpec((width, width), lambda i, half: (0, i)),
                pl.BlockSpec((width, width), lambda i, half: (i, 0)),
                pl.BlockSpec((1, width), lambda i, half: (0, i)),
                *(whole_spec(item.shape) for item in extra_outs),
            ],
            scratch_shapes=scratch,
        ),
        out_shape=[
            jax.ShapeDtypeStruct((width, steps * width), low),
            jax.ShapeDtypeStruct((steps * width, width), low),
            jax.ShapeDtypeStruct((1, steps * width), jnp.float32),
            *extra_outs,
        ],
        compiler_params=kernel_params(),
        cost_estimate=pl.CostEstimate(
            flops=12 * rows * width * width * steps,
            bytes_accessed=8 * width * width * steps + 16 * rows * width,
            transcendentals=2 * rows * width * steps,
        ),
        name=name,
    )(half, *ins)


def expand_first(half, hidden_two, out_low, packed, bias):
    rows, width = hidden_two.shape
    total = jax.ShapeDtypeStruct((rows, width), jnp.float32)
    return expand_call(
        "expand_first",
        first_body,
        half,
        rows,
        width,
        (hidden_two, out_low, packed, bias, packed),
        [],
        [total, total],
        [pltpu.VMEM((width, rows), jnp.bfloat16)],
    )


def expand_second(
    half,
    hidden_two,
    out_low,
    packed,
    bias,
    forward_part,
    back_part,
    middle,
    valid_rows,
    rows_in,
):
    rows, width = hidden_two.shape
    full = whole_spec((rows, width))
    total = pltpu.VMEM((rows, width), jnp.float32)
    return expand_call(
        "expand_second",
        second_body,
        half,
        rows,
        width,
        (
            hidden_two,
            out_low,
            packed,
            bias,
            packed,
            forward_part,
            back_part,
            middle,
            valid_rows,
            rows_in,
        ),
        [full, full, full, whole_spec(valid_rows.shape), whole_spec(rows_in.shape)],
        [
            jax.ShapeDtypeStruct((rows, width), jnp.bfloat16),
            jax.ShapeDtypeStruct((rows, width), jnp.float32),
            jax.ShapeDtypeStruct((rows, width), jnp.bfloat16),
            jax.ShapeDtypeStruct((4, width), jnp.float32),
        ],
        [total, total, pltpu.VMEM((width, rows), jnp.bfloat16)],
    )


def attend_back_body(
    project_ref,
    probs_ref,
    start_ref,
    middle_grad_ref,
    middle_low_ref,
    weight_ref,
    rows_ref,
    project_low_ref,
    conv_low_ref,
    sums_ref,
    third_ref,
    mixed_low,
):
    block_rows, width = start_ref.shape
    slots = 64
    low = jnp.bfloat16
    wide_out = weight_ref[:, 3].reshape(width, width)
    mixed_low[...] = dot_nt(middle_low_ref[...], wide_out).astype(low)
    lanes = lax.broadcasted_iota(jnp.int32, (slots, 128), 1)
    low_half = lanes < 64

    def fold(block):
        return jnp.where(low_half, block[:slots], block[slots:])

    for image in range(block_rows // slots):
        here = slice(image * slots, (image + 1) * slots)
        for pair in range(width // 128):
            at = pair * 128
            queries = project_ref[here, at : at + 128]
            keys = pair_stack(project_ref[here, width + at : width + at + 128], low_half)
            values = pair_stack(project_ref[here, 2 * width + at : 2 * width + at + 128], low_half)
            probs_low = probs_ref[here, at : at + 128]
            mixed = mixed_low[here, at : at + 128]
            probs = probs_low.astype(jnp.float32)
            prob_grad = dot_nt(mixed, values)
            value_grad = fold(dot_tn(probs_low, mixed))
            centre = half_reduce(prob_grad * probs, low_half, jnp.sum, 0.0)
            score_low = (probs * (prob_grad - centre)).astype(low)
            project_low_ref[here, at : at + 128] = (dot_nn(score_low, keys) * 0.125).astype(low)
            project_low_ref[here, width + at : width + at + 128] = (
                fold(dot_tn(score_low, queries)) * 0.125
            ).astype(low)
            project_low_ref[here, 2 * width + at : 2 * width + at + 128] = value_grad.astype(low)
    project_low = project_low_ref[...]
    grad = dot_nt(project_low[:, :width], weight_ref[:, 0].reshape(width, width))
    for third in (1, 2):
        at = third * width
        weight = weight_ref[:, third].reshape(width, width)
        grad = grad + dot_nt(project_low[:, at : at + width], weight)
    normed, inverse = norm_rows(start_ref[...], 1e-06)
    scaled = grad * rows_ref[0:1, :]
    start_grad = middle_grad_ref[...] + inverse * (
        scaled
        - jnp.mean(scaled, -1, keepdims=True)
        - normed * jnp.mean(scaled * normed, -1, keepdims=True)
    )
    conv_low_ref[...] = start_grad.astype(low)
    sums = jnp.concatenate(
        [
            jnp.sum(grad * normed, 0, keepdims=True),
            jnp.sum(grad, 0, keepdims=True),
            jnp.sum(start_grad, 0, keepdims=True),
        ],
        0,
    )
    third = jnp.sum(project_low.astype(jnp.float32), 0, keepdims=True)

    @pl.when(pl.program_id(0) == 0)
    def _():
        sums_ref[...] = sums
        third_ref[...] = third

    @pl.when(pl.program_id(0) > 0)
    def _():
        sums_ref[...] += sums
        third_ref[...] += third


def attend_back(
    project, probs_low, start, middle_grad, middle_low, weights, rows_in, block_rows
):
    rows, width = start.shape
    row_spec = lambda cols: pl.BlockSpec((block_rows, cols), lambda i: (i, 0))
    low = jnp.bfloat16
    return pl.pallas_call(
        attend_back_body,
        grid=(rows // block_rows,),
        in_specs=[
            row_spec(3 * width),
            row_spec(width),
            row_spec(width),
            row_spec(width),
            row_spec(width),
            whole_spec(weights.shape),
            whole_spec(rows_in.shape),
        ],
        out_specs=[
            row_spec(3 * width),
            row_spec(width),
            whole_spec((3, width)),
            whole_spec((1, 3 * width)),
        ],
        out_shape=[
            jax.ShapeDtypeStruct((rows, 3 * width), low),
            jax.ShapeDtypeStruct((rows, width), low),
            jax.ShapeDtypeStruct((3, width), jnp.float32),
            jax.ShapeDtypeStruct((1, 3 * width), jnp.float32),
        ],
        scratch_shapes=[pltpu.VMEM((block_rows, width), low)],
        compiler_params=kernel_params(),
        cost_estimate=pl.CostEstimate(
            flops=24 * rows * width * width,
            bytes_accessed=8 * width * width + 30 * rows * width,
            transcendentals=0,
        ),
        name="attend_back",
    )(project, probs_low, start, middle_grad, middle_low, weights, rows_in)


def dot_full(one, two, dims):
    return lax.dot_general(
        one, two, (dims, ((), ())), precision=highest, preferred_element_type=jnp.float32
    )


def hyper_rows(
    pick_rows,
    bias_mask,
    key_rows,
    hyper_project,
    hyper_output,
    hyper_gains,
    hyper_shifts,
    hyper_up,
    hyper_down,
):
    width = key_rows.shape[1]
    query_rows = dot_full(pick_rows, key_rows, ((1,), (0,)))
    queries = dot_full(query_rows, hyper_project[:, :width], ((1,), (0,)))
    keys_all = dot_full(key_rows, hyper_project[:, width : 2 * width], ((1,), (0,)))
    values_all = dot_full(key_rows, hyper_project[:, 2 * width :], ((1,), (0,)))
    head_size = width // HH
    head_of = lax.broadcasted_iota(jnp.int32, (1, width), 1) // head_size
    mixed_rows = jnp.zeros_like(query_rows)
    for head in range(HH):
        here = (head_of == head).astype(jnp.float32)
        scores = dot_full(queries * here, keys_all, ((1,), (1,))) * head_size ** (-0.5) + bias_mask
        peak = lax.stop_gradient(jnp.max(scores, -1, keepdims=True))
        weights = jnp.exp(scores - peak)
        weights = weights / jnp.sum(weights, -1, keepdims=True)
        mixed_rows = mixed_rows + dot_full(weights, values_all * here, ((1,), (0,)))

    def norm(values, index):
        center = values - jnp.mean(values, -1, keepdims=True)
        inverse = lax.rsqrt(jnp.mean(center * center, -1, keepdims=True) + 1e-05)
        gain = hyper_gains[index : index + 1, :]
        return center * inverse * gain + hyper_shifts[index : index + 1, :]

    hidden = norm(query_rows + dot_full(mixed_rows, hyper_output, ((1,), (0,))), 0)
    expand = dot_full(hidden, hyper_up, ((1,), (0,)))
    expanded = expand * (0.5 + 0.5 * lax.erf(expand * 0.7071067811865476))
    return norm(hidden + dot_full(expanded, hyper_down, ((1,), (0,))), 1)


def hyper_forward_body(*refs):
    refs[-1][...] = hyper_rows(*(ref[...].astype(jnp.float32) for ref in refs[:-1]))


def hyper_forward(pick_rows, bias_mask, key_rows, params):
    return pl.pallas_call(
        hyper_forward_body,
        out_shape=jax.ShapeDtypeStruct((pick_rows.shape[0], key_rows.shape[1]), jnp.float32),
        compiler_params=kernel_params(),
        name="hyper_forward",
    )(pick_rows, bias_mask, key_rows, *params)


def hyper_backward_body(count, pick_ref, mask_ref, key_ref, *refs):
    params = [ref[...].astype(jnp.float32) for ref in refs[:6]]
    feats_ref, conv_ref, matrix_ref = refs[6:9]
    key_out, *param_outs = refs[9:16]
    matrix_out, shift_out = refs[16:]
    conv = conv_ref[...] * scaler
    hidden, pull = jax.vjp(
        lambda *items: hyper_rows(pick_ref[...], mask_ref[...], *items), key_ref[...], *params
    )
    rows = count + conv.shape[0]
    bias_grad = dot_full(conv, matrix_ref[...].astype(jnp.float32), ((1,), (1,)))
    blank = jnp.zeros((hidden.shape[0] - rows, hidden.shape[1]), jnp.float32)
    grads = pull(jnp.concatenate([feats_ref[...], bias_grad, blank], 0))
    key_out[...] = grads[0]
    for out, grad in zip(param_outs, grads[1:]):
        out[...] = grad
    matrix_out[...] = dot_full(hidden[count:rows], conv, ((0,), (0,)))
    shift_out[...] = jnp.sum(conv, 0, keepdims=True)


def hyper_backward(pick_rows, bias_mask, key_rows, params, feats_grad, conv_grad, bias_weight):
    out = lambda item: jax.ShapeDtypeStruct(item.shape, jnp.float32)
    return pl.pallas_call(
        partial(hyper_backward_body, feats_grad.shape[0]),
        out_shape=[
            out(key_rows),
            *(out(item) for item in params),
            out(bias_weight),
            jax.ShapeDtypeStruct((1, bias_weight.shape[1]), jnp.float32),
        ],
        compiler_params=kernel_params(),
        name="hyper_backward",
    )(pick_rows, bias_mask, key_rows, *params, feats_grad, conv_grad, bias_weight)


def hyper_layout(weight_tokens, bias_token, wave_rows):
    group_count, band_count, width = wave_rows.shape
    tokens = weight_tokens.shape[0]
    waves = group_count * band_count
    key_count = -(-(tokens + waves + 1) // 16) * 16
    query_count = -(-(waves + group_count) // 8) * 8
    key_rows = jnp.concatenate(
        [
            weight_tokens.astype(jnp.float32),
            wave_rows.reshape(waves, width),
            bias_token.astype(jnp.float32)[None, :],
            jnp.zeros((key_count - tokens - waves - 1, width), jnp.float32),
        ],
        0,
    )
    query_id = np.arange(query_count)[:, None]
    key_id = np.arange(key_count)[None, :]
    source = np.where(query_id < waves, tokens + query_id, tokens + waves)
    pick_rows = (key_id == source) & (query_id < waves + group_count)
    query_group = np.where(query_id < waves, query_id // band_count, query_id - waves)
    key_group = (key_id - tokens) // band_count
    allowed = (
        (key_id < tokens)
        | (key_id == tokens + waves)
        | ((key_id < tokens + waves) & (key_group == query_group))
    )
    return (
        jnp.asarray(pick_rows.astype(np.float32)),
        jnp.asarray(np.where(allowed, 0.0, -1e30).astype(np.float32)),
        key_rows,
    )


def spread_eye(rows, copies):
    count, width = rows.shape
    iota = lambda shape, axis: lax.broadcasted_iota(jnp.int32, shape, axis)
    wide = (iota((width, width * copies), 1) // copies == iota((width, width * copies), 0)).astype(
        jnp.bfloat16
    )
    tall = (iota((count * copies, count), 0) // copies == iota((count * copies, count), 1)).astype(
        jnp.bfloat16
    )
    spread = dot_nn(tall, dot_nn(rows, wide).astype(jnp.bfloat16))
    same = iota(spread.shape, 0) % copies == iota(spread.shape, 1) % copies
    return jnp.where(same, spread, 0.0).astype(jnp.bfloat16)


def make_kernel_body(feats_ref, weight_ref, bias_ref, part_ref, spread_ref):
    bands, block, width = part_ref.shape
    hidden = weight_ref.shape[0]

    @pl.when(pl.program_id(0) == 0)
    def _():
        spread_ref[...] = spread_eye(feats_ref[...], block)

    product = dot_nn(spread_ref[...], weight_ref[...].reshape(hidden * block, width))
    product = product.reshape(-1, bands, block, width)
    bias = bias_ref[...].astype(jnp.float32)
    part_ref[...] = (scaler * (product[0] + product[1] + bias[None])).astype(part_ref.dtype)


def make_kernel(band_feats, kernel_weight, kernel_bias):
    bands = band_feats.shape[0]
    hidden, rows, width = kernel_weight.shape
    block = 16
    feats = split_low(band_feats, 2, 0)
    if rows % block:
        product = jnp.einsum(
            "sh,hpd->spd", feats, kernel_weight, preferred_element_type=jnp.float32
        )
        total = jnp.sum(product.reshape(2, bands, rows, width), 0)
        return (scaler * (total + kernel_bias.astype(jnp.float32))).astype(jnp.bfloat16)
    return pl.pallas_call(
        make_kernel_body,
        grid=(rows // block,),
        in_specs=[
            whole_spec(feats.shape),
            pl.BlockSpec((hidden, block, width), lambda i: (0, i, 0)),
            pl.BlockSpec((block, width), lambda i: (i, 0)),
        ],
        out_specs=pl.BlockSpec((bands, block, width), lambda i: (0, i, 0)),
        out_shape=jax.ShapeDtypeStruct((bands, rows, width), jnp.bfloat16),
        scratch_shapes=[pltpu.VMEM((2 * bands * block, hidden * block), jnp.bfloat16)],
        compiler_params=kernel_params(),
        name="make_kernel",
    )(feats, kernel_weight, kernel_bias)


def weight_grad_body(feats_ref, grad_ref, out_ref, spread_ref):
    hidden, block, width = out_ref.shape

    @pl.when(pl.program_id(0) == 0)
    def _():
        spread_ref[...] = spread_eye(feats_ref[...], block)

    grad = grad_ref[...].reshape(-1, width)
    out_ref[...] = dot_nn(spread_ref[...], grad).reshape(hidden, block, width)


def weight_grad(feats, kernel_all):
    count, rows, width = kernel_all.shape
    hidden = feats.shape[1]
    block = 16
    feats = (scaler * feats).astype(jnp.bfloat16)
    if rows % block:
        return jnp.einsum("sh,spd->hpd", feats, kernel_all, preferred_element_type=jnp.float32)
    table = feats.T
    return pl.pallas_call(
        weight_grad_body,
        grid=(rows // block,),
        in_specs=[
            whole_spec(table.shape),
            pl.BlockSpec((count, block, width), lambda i: (0, i, 0)),
        ],
        out_specs=pl.BlockSpec((hidden, block, width), lambda i: (0, i, 0)),
        out_shape=jax.ShapeDtypeStruct((hidden, rows, width), jnp.float32),
        scratch_shapes=[pltpu.VMEM((hidden * block, count * block), jnp.bfloat16)],
        compiler_params=kernel_params(),
        name="weight_grad",
    )(table, kernel_all)


def on_device(
    group_size,
    dp_size,
    pixels,
    patch_index,
    kept_count,
    wavelength,
    weight_tokens,
    bias_token,
    hyper_project,
    hyper_output,
    hyper_gains,
    hyper_shifts,
    hyper_up,
    hyper_down,
    kernel_weight,
    kernel_bias,
    bias_weight,
    bias_shift,
    attention_in,
    attention_out,
    expand_weight,
    reduce_weight,
    norm_gains,
    norm_shifts,
    attention_bias,
    output_bias,
    expand_bias,
    reduce_bias,
    cotangent,
):
    floaty = jnp.float32
    low = jnp.bfloat16
    links = Links(group_size, dp_size)
    image_count, slot_count, band_count, pixel_count = pixels.shape[1:]
    model_width = cotangent.shape[-1]
    row_count = image_count * slot_count
    widen = lambda item: item.astype(floaty)
    hyper_params = (
        hyper_project,
        hyper_output,
        hyper_gains,
        hyper_shifts,
        hyper_up,
        hyper_down,
    )

    feed = gather_feed(links, expand_weight, reduce_weight)
    piece = attention_piece(links, attention_in, attention_out)
    piece = piece.reshape((1, 1, 1, 1) + piece.shape)
    block = gather_line(links, piece, 0)
    wave_rows = wave_embed(wavelength[0])
    own_hidden = hyper_forward(
        *hyper_layout(weight_tokens, bias_token, wave_rows[None]), hyper_params
    )
    band_feats = own_hidden[:band_count] + wave_rows
    bias_feat = own_hidden[band_count]
    kernel_part = make_kernel(band_feats, kernel_weight, kernel_bias)
    chunk_count = 3
    chunk_bands = band_count // chunk_count
    depth = chunk_bands * pixel_count
    kernel_part, block, wavelength, bias_feat = stage(kernel_part, block, wavelength, bias_feat)
    chunks = [
        kernel_part[i * chunk_bands : (i + 1) * chunk_bands][:, None, None]
        for i in range(chunk_count)
    ]

    line_one = gather_line(links, chunks[0], 1)
    other = links.xside(block)
    all_waves = spread_group(links, wavelength[0])
    line_one, other, chunks, pixels, all_waves = stage(line_one, other, chunks, pixels, all_waves)
    block = pair_up(block, other, links.x, 1)

    line_one, block, chunks = stage(line_one, block, chunks)
    line_two = gather_line(links, chunks[1], 1)
    other_one = links.xside(line_one)
    other = links.yside(block)
    pixel_rows = pixels.reshape(row_count, band_count * pixel_count)
    line_two, other_one, other, chunks, pixel_rows, all_waves, bias_feat = stage(
        line_two, other_one, other, chunks, pixel_rows, all_waves, bias_feat
    )
    kernel_one = pair_up(line_one, other_one, links.x, 2).reshape(depth, model_width)
    block = pair_up(block, other, links.y, 2)

    line_two, block, kernel_one, chunks = stage(line_two, block, kernel_one, chunks)
    line_three = gather_line(links, chunks[2], 1)
    other_two = links.xside(line_two)
    other = links.core(block)
    valid_rows = (
        lax.broadcasted_iota(jnp.int32, (image_count, slot_count), 1) < kept_count[0][:, None]
    )
    valid_rows = valid_rows.reshape(row_count, 1).astype(floaty)
    out_low = cotangent.reshape(row_count, model_width) * valid_rows.astype(low)
    conv_bias = scaler * (
        jnp.dot(bias_feat, widen(bias_weight), precision=highest) + widen(bias_shift)
    )
    spots = place_spots(patch_index[0].reshape(row_count), 3)
    table = split_low(jnp.concatenate([place_table(model_width), conv_bias[None, :]], 0), 3, 0)
    table = jnp.pad(table, ((0, 128 - table.shape[0]), (0, 0)))
    embed_part = dot_nn(spots, table) + dot_nn(pixel_rows[:, :depth], kernel_one)
    line_three, other_two, other, embed_part, out_low, all_waves = stage(
        line_three, other_two, other, embed_part, out_low, all_waves
    )
    kernel_two = pair_up(line_two, other_two, links.x, 2).reshape(depth, model_width)
    weights = pair_up(block, other, links.c, 3).reshape(8, 4, -1, model_width)

    line_three, weights, kernel_two, all_waves = stage(line_three, weights, kernel_two, all_waves)
    other_three = links.xside(line_three)
    embed_part = embed_part + dot_nn(pixel_rows[:, depth : 2 * depth], kernel_two)
    wave_all = jax.vmap(wave_embed)(all_waves)
    pick_rows, bias_mask, key_rows = hyper_layout(weight_tokens, bias_token, wave_all)
    all_hidden = hyper_forward(pick_rows, bias_mask, key_rows, hyper_params)
    wave_count = group_size * band_count
    feats_all = all_hidden[:wave_count] + wave_all.reshape(wave_count, HE)
    other_three, embed_part, weights, feats_all = stage(
        other_three, embed_part, weights, feats_all
    )
    kernel_three = pair_up(line_three, other_three, links.x, 2).reshape(depth, model_width)

    gains = widen(norm_gains)
    shifts = widen(norm_shifts)
    start, hidden_one = embed_rows(
        embed_part, pixel_rows, kernel_three, jnp.stack([gains[0], shifts[0]]), 256
    )
    bias_full = jnp.concatenate(
        [widen(attention_bias[0]), jnp.zeros((model_width,), floaty), widen(attention_bias[1])]
    )[None, :]
    attended = attend_rows(
        0,
        6,
        None,
        kept_count[0],
        hidden_one,
        start,
        weights,
        bias_full,
        jnp.stack([widen(output_bias), gains[1], shifts[1]]),
    )
    project, probs_low, mixed_rows, middle, hidden_two = attended

    half_other = (1 - links.c).reshape(1)
    half_own = links.c.reshape(1)
    wide_bias = widen(expand_bias)[None, :]
    up_other, down_other, bias_other, forward_part, back_part = expand_first(
        half_other, hidden_two, out_low, feed, wide_bias
    )
    up_other, down_other, forward_part = stage(up_other, down_other, forward_part)
    up_other = links.core(up_other)
    down_other = links.core(down_other)
    up_own, down_own, bias_own, encoded, middle_grad, middle_low, sums_two = expand_second(
        half_own,
        hidden_two,
        out_low,
        feed,
        wide_bias,
        forward_part,
        back_part,
        middle,
        valid_rows,
        jnp.stack([widen(reduce_bias), gains[1]]),
    )
    encoded = encoded.reshape(cotangent.shape)
    up_other, down_other, up_own, down_own, middle_low = stage(
        up_other, down_other, up_own, down_own, middle_low
    )
    shard_rows = model_width // dp_size
    down_rows = reduce_weight.shape[0]
    up_shape = (links.line, 2, shard_rows, up_own.shape[1])
    up_sum = add_low(up_own.reshape(up_shape), up_other.reshape(up_shape))
    down_shape = (-1, 2, down_rows // 2, model_width)
    down_sum = add_low(down_own.reshape(down_shape), down_other.reshape(down_shape))

    send_up = pick(up_sum, 1 - links.x, 1)
    send_down = pick(down_sum, 1 - links.y, 1)
    send_up, send_down, middle_low = stage(send_up, send_down, middle_low)
    other_up = links.xside(send_up)
    other_down = links.yside(send_down)
    project_low, conv_low, sums_one, third_sums = attend_back(
        project, probs_low, start, middle_grad, middle_low, weights, gains[0:1], 256
    )
    other_up, other_down, conv_low, project_low = stage(
        other_up, other_down, conv_low, project_low
    )
    up_sum = add_low(pick(up_sum, links.x, 1), other_up).reshape(
        links.line, 2, shard_rows // 2, -1
    )
    down_sum = add_low(pick(down_sum, links.y, 1), other_down)

    send_up = pick(up_sum, 1 - links.y, 1)
    down_sum = down_sum.reshape(-1, 2, down_rows // 2, model_width)
    send_down = pick(down_sum, 1 - links.x, 1)
    send_up, send_down, conv_low = stage(send_up, send_down, conv_low)
    other_up = links.yside(send_up)
    other_down = links.xside(send_down)
    kernel_grad = contract_rows(pixel_rows, conv_low).astype(low)
    kernel_grad = kernel_grad.reshape(band_count, links.line, 2, -1, model_width)
    piece_count = 2
    piece_pixels = kernel_grad.shape[3] // piece_count
    piece_of = lambda i, side: pick(
        kernel_grad[:, :, :, i * piece_pixels : (i + 1) * piece_pixels], side, 2
    )
    sends = [piece_of(i, 1 - links.x) for i in range(piece_count)]
    small = jnp.concatenate(
        [
            sums_one[0:1],
            sums_two[0:1],
            sums_one[1:2],
            sums_two[1:2],
            third_sums[:, :model_width],
            third_sums[:, 2 * model_width :],
            sums_two[2:4],
            pair_up(bias_own, bias_other, links.c, 1).reshape(-1, model_width),
            sums_one[2:3],
        ],
        0,
    )
    other_up, other_down, sends, kernel_grad, small = stage(
        other_up, other_down, sends, kernel_grad, small
    )
    up_sum = add_low(pick(up_sum, links.y, 1), other_up)
    down_sum = add_low(pick(down_sum, links.x, 1), other_down)
    line_parts = lambda block: block.reshape(band_count, links.line, -1, model_width)
    finish_piece = lambda total: total.astype(low).reshape(band_count, -1, model_width)

    up_sum, sends, project_low, middle_low = stage(up_sum, sends, project_low, middle_low)
    other = links.xside(sends[0])
    up_total = reduce_line(links, up_sum, 0, links.zside).astype(low)
    grad_units = [
        contract_rows(hidden_one, project_low[:, i * model_width : (i + 1) * model_width])
        for i in range(3)
    ] + [contract_rows(mixed_rows, middle_low)]
    grad_units = [unit.astype(low) for unit in grad_units]
    units_of = lambda side: jnp.stack(
        [
            jnp.where(side == 0, grad_units[0], grad_units[1]),
            jnp.where(side == 0, grad_units[2], grad_units[3]),
        ]
    )
    send_units = units_of(1 - links.c)
    keep_units = units_of(links.c)
    other, up_total, send_units, keep_units, sends, small = stage(
        other, up_total, send_units, keep_units, sends, small
    )
    ready = line_parts(add_low(piece_of(0, links.x), other))

    ready, send_units, sends, small = stage(ready, send_units, sends, small)
    other = links.xside(sends[1])
    total_one = reduce_line(links, ready, 1, links.zside)
    other_units = links.core(send_units)
    small = small + links.zside(small, 1)
    wide_kernel = jnp.concatenate([kernel_one, kernel_two, kernel_three], 0)
    pixel_grad = dot_nt(conv_low, wide_kernel).astype(low)
    other, total_one, other_units, small, pixel_grad = stage(
        other, total_one, other_units, small, pixel_grad
    )
    units = add_low(keep_units, other_units)
    ready = line_parts(add_low(piece_of(1, links.x), other))
    pixel_grad = pixel_grad.reshape(pixels.shape)

    send_units = pick(units, 1 - links.y, 0)
    ready, send_units, down_sum, small = stage(ready, send_units, down_sum, small)
    total_two = reduce_line(links, ready, 1, links.zside)
    other_units = links.yside(send_units)
    step = 2
    while step < dp_size:
        small = small + links.zside(small, step)
        step *= 2
    total_two, other_units, small, down_sum = stage(total_two, other_units, small, down_sum)
    units = add_low(pick(units, links.y, 0), other_units)
    units = units.reshape(links.line, 2, shard_rows, model_width)
    kernel_low = jnp.concatenate([finish_piece(total) for total in (total_one, total_two)], 1)
    feats_part = scaler * jnp.einsum(
        "spd,hpd->sh", kernel_low, kernel_weight, preferred_element_type=floaty
    )

    send_units = pick(units, 1 - links.x, 1)
    send_units, down_sum, feats_part, kernel_low, small = stage(
        send_units, down_sum, feats_part, kernel_low, small
    )
    kernel_all = spread_group(links, kernel_low)
    other_units = links.xside(send_units)
    stride = 2
    while stride < dp_size // 2:
        bit = lax.axis_index("dp") // stride % 2
        down_sum = down_sum.reshape(-1, 2, down_rows // 2, model_width)
        other_down = links.zside(pick(down_sum, 1 - bit, 1), stride)
        down_sum = add_low(pick(down_sum, bit, 1), other_down)
        stride *= 2
    down_sum = down_sum.reshape(down_rows // 2, model_width)
    down_total = add_low(down_sum, links.owner_line(down_sum))
    conv_all = spread_group(links, small[-1:])
    small = small[:-1]
    small = small + links.core(small)
    small = small + links.yside(small)
    feats_grad = spread_group(links, sum_dp(links, feats_part)).reshape(-1, HE)
    units = add_low(pick(units, links.x, 1), other_units).reshape(links.line, shard_rows, -1)
    unit_total = reduce_line(links, units, 0, links.zside).astype(low)
    key_grad, *param_grads, bias_weight_grad, bias_shift_grad = hyper_backward(
        pick_rows,
        bias_mask,
        key_rows,
        hyper_params,
        feats_grad,
        conv_all.reshape(group_size, model_width),
        bias_weight,
    )
    token_count = weight_tokens.shape[0]
    kernel_all = kernel_all.reshape((wave_count,) + kernel_low.shape[1:])
    weight_shard_grad = weight_grad(feats_all, kernel_all)
    bias_shard_grad = scaler * jnp.sum(kernel_all.astype(floaty), 0)
    up_total = up_total.reshape(1, shard_rows // 2, -1)
    up_total = pair_up(up_total, links.yside(up_total), links.y, 0).reshape(shard_rows, -1)
    up_total = pair_up(up_total, links.core(up_total), links.c, 1)
    down_total = down_total.reshape(1, down_rows // 2, model_width)
    down_total = pair_up(down_total, links.yside(down_total), links.y, 0)
    down_other = links.owner_core(down_total)
    is_owner = lax.axis_index("dp") // (dp_size // 2) == links.c
    down_total = jnp.where(is_owner, down_total, down_other)
    unit_all = spread_group(links, unit_total.reshape(shard_rows, model_width))
    block_shards = (
        widen(jnp.concatenate([unit_all[i] for i in range(3)], 1)),
        widen(unit_all[3]),
        widen(up_total),
        widen(down_total.reshape(down_rows, model_width)),
    )
    return (
        encoded,
        pixel_grad,
        key_grad[:token_count],
        key_grad[token_count + wave_count],
        *param_grads,
        weight_shard_grad,
        bias_shard_grad,
        bias_weight_grad,
        bias_shift_grad.reshape(-1),
        *block_shards,
        small[0:2],
        small[2:4],
        small[4:6],
        small[6],
        small[8:].reshape(-1),
        small[7],
    )


def solution(mesh):
    placed = (
        P("group", "dp", None, None, None),
        P("group", "dp", None),
        P("group", "dp"),
        P("group", None),
        P(),
        P(),
        P(),
        P(),
        P(),
        P(),
        P(),
        P(),
        P(None, "dp", None),
        P("dp", None),
        P(),
        P(),
        P("dp", None),
        P("dp", None),
        P("dp", None),
        P("dp", None),
        P(),
        P(),
        P(),
        P(),
        P(),
        P(),
        P("group", "dp", None, None),
    )
    return jax.shard_map(
        partial(on_device, mesh.shape["group"], mesh.shape["dp"]),
        mesh=mesh,
        in_specs=placed,
        out_specs=(
            P("group", "dp", None, None),
            P("group", "dp", None, None, None),
            P(),
            P(),
            P(),
            P(),
            P(),
            P(),
            P(),
            P(),
            P(None, "dp", None),
            P("dp", None),
            P(),
            P(),
            P("dp", None),
            P("dp", None),
            P("dp", None),
            P("dp", None),
            P(),
            P(),
            P(),
            P(),
            P(),
            P(),
        ),
        check_vma=False,
    )
```

time: 1430 us -> 564 us (0.39)
  waiting for transfers between devices: 902 us -> 148 us
  matrix products: 218 us -> 48.4 us
  Pallas kernels: 0 us -> 151 us
  blocking collectives: 79.3 us -> 0 us
  starting transfers between devices: 0.48 us -> 74.4 us
  local copies, waits for them, and re-layouts: 123 us -> 67.3 us
  other arithmetic: 80.3 us -> 52.9 us
    reduce_scatter x5 -> x0, waiting for transfers between devices: 519 us -> none  [the longest x1 209 us: on_device(): lax.psum_scatter(jnp.einsum('rbp,rd->pbd', window, conv_low, preferred_el...]
    all_gather x5 -> x1, waiting for transfers between devices: 258 us -> 0.01 us  [gather_feed(): wide = lax.all_gather(jnp.stack([up, down]), ('dp', 'group'), axis=0)]
    dot_general x40 -> x6, matrix products: 189 us -> 36.6 us  [the longest x1 20.4 us: dot_nt(): lax.dot_general(one, two, (((1,), (1,)), ((), ())), preferred_element_typ...]
    pallas_call x0 -> x10, Pallas kernels: none -> 151 us  [the longest x2 40.7 us: expand_call(): pl.pallas_call(body, grid_spec=pltpu.PrefetchScalarGridSpec(num_scalar_pr...]
    ppermute x0 -> x65, waiting for transfers between devices: none -> 148 us  [the longest x31 102 us: zside(): lax.ppermute(block, 'dp', [(i, i ^ step) for i in range(self.dp_size)])]
    psum x2 -> x0, waiting for transfers between devices: 122 us -> none  [the longest x1 122 us: on_device(): lax.psum(weight_shard_grad.astype(jnp.bfloat16), 'group')]
    psum x2 -> x0, blocking collectives: 79.3 us -> none  [the longest x1 41.6 us: on_device(): lax.psum((jnp.stack([jnp.sum(hidden_one_grad * normed_one, 0), jnp.sum(hi...]
    ppermute x0 -> x65, starting transfers between devices: none -> 74.4 us  [the longest x31 41.8 us: zside(): lax.ppermute(block, 'dp', [(i, i ^ step) for i in range(self.dp_size)])]
  transfers between devices with their start and end apart: 12 -> 66, of which waited for: 9 -> 25; matrix products, arithmetic and copies ran while one was open for 22% -> 22% of each run, Pallas kernels for 0% -> 22%
where the time goes in v1:
time: 564 us; the launch traced here: 558 us
  Pallas kernels  151 us (27%)
  waiting for transfers between devices  148 us (26%)
  starting transfers between devices  74.4 us (13%)
  local copies, waits for them, and re-layouts  67.3 us (12%)
  other arithmetic  52.9 us (9%)
  matrix products  48.4 us (9%)
  between operations  15.9 us (3%)
    ppermute x31, waiting for transfers between devices, zside(): lax.ppermute(block, 'dp', [(i, i ^ step) for i in range(self.dp_size)])  102 us
    ppermute x31, starting transfers between devices, zside(): lax.ppermute(block, 'dp', [(i, i ^ step) for i in range(self.dp_size)])  41.8 us
    pallas_call x2, Pallas kernels, expand_call(): pl.pallas_call(body, grid_spec=pltpu.PrefetchScalarGridSpec(num_scalar_pr...  40.7 us
    pallas_call x1, Pallas kernels, attend_rows(): pl.pallas_call(body, grid_spec=pltpu.PrefetchScalarGridSpec(num_scalar_pr...  31 us
    pallas_call x1, Pallas kernels, attend_back(): pl.pallas_call(attend_back_body, grid=(rows // block_rows,), in_specs=[ro...  29.9 us
    ppermute x9, waiting for transfers between devices, xside(): return lax.ppermute(block, 'dp', [(i, i ^ 1) for i in range(self.dp_size)])  22.4 us
    ppermute x12, waiting for transfers between devices, yside(): lax.ppermute(block, 'group', [(i, i ^ 2) for i in range(self.group_size)])  22 us
    dot_general x1, matrix products, dot_nt(): lax.dot_general(one, two, (((1,), (1,)), ((), ())), preferred_element_typ...  20.4 us
  transfers between devices with their start and end apart: 66, of which 25 were waited for; matrix products, arithmetic and copies ran while one was open for 22% of the time, Pallas kernels for 22%

profile of v1, /device:TPU:0, one launch (start us, length us, event | category | flops | bytes accessed | tf_op | source)
XLA Modules:
  0.0 557.6 jit_solution(7644025167916031500)
XLA Ops:
  10.4 4.1 collective-permute-start.1
  17.6 5.2 hyper_forward.2
  27.5 6.4 %make_kernel.1 = bf16[12,32,768]{2,1,0:T(8,128)(2,1)} custom-call(bf16[24,128]{1,0:T(8,128)(2,1)} %pad_maximum_fusion.8.feats_ref, bf16[128,32,768]{2,1,0:T(8,128)(2,1)} %weight_ref.1, bf16[32,768]{1,0:T(8,128)(2,1)} %bias_ref.1), custom_call_target="tpu_custom_call" | custom-call | tf_op jit(solution)/shard_map/make_kernel/pallas_call | solution.py:902
  44.4 14.1 %collective-permute-done.3 = bf16[4,1,1,32,768]{4,3,0,2,1:T(8,128)(2,1)S(1)} collective-permute-done((bf16[4,1,1,32,768]{4,3,0,2,1:T(8,128)(2,1)S(1)}, bf16[4,1,1,32,768]{4,3,0,2,1:T(8,128)(2,1)S(1)}, u32[]{:S(2)}, u32[]{:S(2)}) %collective-permute-start.3) | collective-permute-done | bytes 196640 | tf_op jit(solution)/shard_map/ppermute | solution.py:94
  58.5 4.1 collective-permute-done.4
  73.0 5.8 %copy.108 = bf16[1,12,64,12,256]{4,3,2,1,0:T(8,128)(2,1)S(1)} copy(bf16[1,12,64,12,256]{4,2,3,1,0:T(8,128)(2,1)} %param.31) | data formatting | bytes 9437184 | tf_op jit(solution)/shard_map/optimization_barrier | solution.py:63
  82.0 13.9 %collective-permute-done.10 = bf16[4,1,1,32,768]{4,3,0,2,1:T(8,128)(2,1)S(1)} collective-permute-done((bf16[4,1,1,32,768]{4,3,0,2,1:T(8,128)(2,1)S(1)}, bf16[4,1,1,32,768]{4,3,0,2,1:T(8,128)(2,1)S(1)}, u32[]{:S(2)}, u32[]{:S(2)}) %collective-permute-start.10) | collective-permute-done | bytes 196640 | tf_op jit(solution)/shard_map/ppermute | solution.py:94
  113.8 13.5 %collective-permute-done.14 = bf16[4,1,1,32,768]{4,3,0,2,1:T(8,128)(2,1)S(1)} collective-permute-done((bf16[4,1,1,32,768]{4,3,0,2,1:T(8,128)(2,1)S(1)}, bf16[4,1,1,32,768]{4,3,0,2,1:T(8,128)(2,1)S(1)}, u32[]{:S(2)}, u32[]{:S(2)}) %collective-permute-start.14) | collective-permute-done | bytes 196640 | tf_op jit(solution)/shard_map/ppermute | solution.py:94
  127.3 4.7 collective-permute-done.15
  138.7 5.7 %hyper_forward.3 = f32[56,128]{1,0:T(8,128)} custom-call(f32[56,192]{1,0:T(8,128)} %constant.160.clone.refs_0_.pick_ref, f32[56,192]{1,0:T(8,128)} %constant.161.clone.refs_1_.mask_ref, f32[192,128]{1,0:T(8,128)} %maximum_maximum_fusion.refs_2_.key_ref, bf16[128,384]{1,0:T(8,128)(2,1)} %refs_0_.3, bf16[128,128]{1,0:T(8,128)(2,1)} %refs_1_.3, ...), custom_call_target="tpu_custom_call" | custom-call | tf_op jit(solution)/shard_map/hyper_forward/pallas_call | solution.py:787
  150.2 5.3 collective-permute-done.19
  158.2 5.7 %embed_rows.1 = (f32[768,768]{1,0:T(8,128)}, bf16[768,768]{1,0:T(8,128)(2,1)}) custom-call(f32[768,768]{1,0:T(8,128)} %add.273.part_ref, bf16[768,3072]{1,0:T(8,128)(2,1)} %bitcast.158, bf16[1024,768]{1,0:T(8,128)(2,1)} %bitcast.169, f32[2,768]{1,0:T(2,128)} %pad_maximum_fusion.9.norm_ref), custom_call_target="tpu_custom_call" | custom-call | flops 1207959552 | bytes 6684672 | tf_op jit(solution)/shard_map/embed_rows/pallas_call | solution.py:250
  163.9 31.0 %attend_rows.1 = (bf16[768,2304]{1,0:T(8,128)(2,1)}, bf16[768,768]{1,0:T(8,128)(2,1)}, bf16[768,768]{1,0:T(8,128)(2,1)}, f32[768,768]{1,0:T(8,128)}, bf16[768,768]{1,0:T(8,128)(2,1)}) custom-call(s32[12]{0:T(128)} %bitcast.193, bf16[768,768]{1,0:T(8,128)(2,1)} %get-tuple-element.188.refs_0_, f32[768,768]{1,0:T(8,128)} %get-tuple-element.189.refs_1_.start_ref, ...), custom_call_target="tpu_custom_call" | custom-call | flops 7247757312 | bytes 16515072 | tf_op jit(solution)/shard_map/attend_rows/pallas_call | solution.py:347
  194.9 18.4 %expand_first.1 = (bf16[768,1536]{1,0:T(8,128)(2,1)}, bf16[1536,768]{1,0:T(8,128)(2,1)}, f32[1,1536]{1,0:T(1,128)}, f32[768,768]{1,0:T(8,128)}, f32[768,768]{1,0:T(8,128)}) custom-call(s32[1]{0:T(128)} %bitcast.38.half_ref, bf16[768,768]{1,0:T(8,128)(2,1)} %get-tuple-element.191.hidden_ref, bf16[768,768]{1,0:T(8,128)(2,1)} %bitcast_multiply_fusion.out_ref, ...), custom_call_target="tpu_custom_call" | custom-call | flops 10871635968 | bytes 18874368 | tf_op jit(solution)/shard_map/expand_first/pallas_call | solution.py:515
  215.5 22.4 %expand_second.1 = (bf16[768,1536]{1,0:T(8,128)(2,1)}, bf16[1536,768]{1,0:T(8,128)(2,1)}, f32[1,1536]{1,0:T(1,128)}, bf16[768,768]{1,0:T(8,128)(2,1)}, f32[768,7...) custom-call(s32[1]{0:T(128)} %bitcast.half_ref, bf16[768,768]{1,0:T(8,128)(2,1)} %get-tuple-element.191.hidden_ref, ...), custom_call_target="tpu_custom_call" | custom-call | flops 10871635968 | bytes 18874368 | tf_op jit(solution)/shard_map/expand_second/pallas_call | solution.py:515
  253.8 29.9 %attend_back.1 = (bf16[768,2304]{1,0:T(8,128)(2,1)}, bf16[768,768]{1,0:T(8,128)(2,1)}, f32[3,768]{1,0:T(4,128)}, f32[1,2304]{1,0:T(1,128)}) custom-call(bf16[768,2304]{1,0:T(8,128)(2,1)} %get-tuple-element.212.project_ref, bf16[768,768]{1,0:T(8,128)(2,1)} %get-tuple-element.213.probs_ref, f32[768,768]{1,0:T(8,128)} %get-tuple-element.189.refs_1_.start_ref, ...), custom_call_target="tpu_custom_call" | custom-call | flops 10871635968 | bytes 22413312 | tf_op jit(solution)/shard_map/attend_back/pallas_call | solution.py:702
  290.5 7.1 %convolution_convert_fusion.1 = bf16[3072,768]{1,0:T(8,128)(2,1)S(1)} fusion(bf16[768,3072]{1,0:T(8,128)(2,1)} %bitcast.159, bf16[768,768]{1,0:T(8,128)(2,1)S(1)} %copy-done.39), kind=kOutput, calls=%fused_computation.4 | convolution fusion | flops 3626237952 | bytes 10616832 | tf_op jit(solution)/shard_map/dot_general | solution.py:21
  301.4 11.0 %collective-permute-done.24 = bf16[4,1,48,1536]{3,2,1,0:T(8,128)(2,1)S(1)} collective-permute-done((bf16[4,1,48,1536]{3,2,1,0:T(8,128)(2,1)S(1)}, bf16[4,1,48,1536]{3,2,1,0:T(8,128)(2,1)S(1)}, u32[]{:S(2)}, u32[]{:S(2)}) %collective-permute-start.24) | collective-permute-done | bytes 589856 | tf_op jit(solution)/shard_map/ppermute | solution.py:88
  332.3 14.0 %collective-permute-done.26 = bf16[12,4,1,16,768]{4,3,2,1,0:T(8,128)(2,1)S(1)} collective-permute-done((bf16[12,4,1,16,768]{4,3,2,1,0:T(8,128)(2,1)S(1)}, bf16[12,4,1,16,768]{4,3,2,1,0:T(8,128)(2,1)S(1)}, u32[]{:S(2)}, u32[]{:S(2)}) %collective-permute-start.26) | collective-permute-done | bytes 1179680 | tf_op jit(solution)/shard_map/ppermute | solution.py:91
  355.3 20.4 %convolution_convert_fusion = bf16[768,3072]{1,0:T(8,128)(2,1)} fusion(bf16[768,768]{1,0:T(8,128)(2,1)} %get-tuple-element.223, bf16[1024,768]{1,0:T(8,128)(2,1)S(1)} %bitcast.170, bf16[1024,768]{1,0:T(8,128)(2,1)} %bitcast.183, bf16[1024,768]{1,0:T(8,128)(2,1)} %bitcast.181), kind=kOutput, calls=%fused_computation.3 | convolution fusion | flops 3640393728 | bytes 10616832 | tf_op jit(solution)/shard_map/dot_general | solution.py:230
  377.3 10.6 %collective-permute-done.32 = bf16[12,1,16,768]{3,0,2,1:T(8,128)(2,1)S(1)} collective-permute-done((bf16[12,1,16,768]{3,0,2,1:T(8,128)(2,1)S(1)}, bf16[12,1,16,768]{3,0,2,1:T(8,128)(2,1)S(1)}, u32[]{:S(2)}, u32[]{:S(2)}) %collective-permute-start.32) | collective-permute-done | bytes 294944 | tf_op jit(solution)/shard_map/ppermute | solution.py:94
  403.8 9.1 %reshape.840 = bf16[1,12,64,12,256]{4,3,2,1,0:T(8,128)(2,1)} reshape(bf16[768,3072]{1,0:T(8,128)(2,1)} %convolution_convert_fusion) | data formatting | bytes 9437184 | tf_op jit(solution)/shard_map/reshape | solution.py:1209
  413.0 6.9 %copy.128 = bf16[1,12,64,12,256]{4,2,3,1,0:T(8,128)(2,1)} copy(bf16[1,12,64,12,256]{4,3,2,1,0:T(8,128)(2,1)} %reshape.840) | data formatting | bytes 9437184
  419.8 16.6 %collective-permute-done.41 = f32[13,768]{1,0:T(8,128)S(1)} collective-permute-done((f32[13,768]{1,0:T(8,128)S(1)}, f32[13,768]{1,0:T(8,128)S(1)}, u32[]{:S(2)}, u32[]{:S(2)}) %collective-permute-start.41) | collective-permute-done | bytes 39968 | tf_op jit(solution)/shard_map/ppermute | solution.py:94
  438.0 9.6 %fusion.22 = f32[12,128]{1,0:T(8,128)S(1)} fusion(bf16[128,32,768]{2,1,0:T(8,128)(2,1)} %weight_ref.1, bf16[12,16,768]{2,0,1:T(8,128)(2,1)S(1)} %add_bitcast_fusion, bf16[12,16,768]{2,0,1:T(8,128)(2,1)S(1)} %add_bitcast_fusion.1), kind=kOutput, calls=%fused_computation.51 | convolution fusion | flops 75793920 | bytes 6887424 | tf_op jit(solution)/shard_map/spd,hpd->sh/dot_general | solution.py:1223
  460.0 4.5 collective-permute-done.44
  466.9 5.0 collective-permute-done.45
  473.9 15.6 %hyper_backward.1 = (f32[192,128]{1,0:T(8,128)}, f32[128,384]{1,0:T(8,128)}, f32[128,128]{1,0:T(8,128)}, f32[2,128]{1,0:T(2,128)}, f32[2,128]{1,0:T(2,128)}, /*i...) custom-call(f32[56,192]{1,0:T(8,128)} %constant.160.clone.refs_0_.pick_ref, ...), custom_call_target="tpu_custom_call" | custom-call | tf_op jit(solution)/shard_map/hyper_backward/pallas_call | solution.py:817
  497.3 4.7 collective-permute-start.54
  504.4 6.2 %collective-permute-done.54 = bf16[1,96,768]{2,1,0:T(8,128)(2,1)S(1)} collective-permute-done((bf16[1,96,768]{2,1,0:T(8,128)(2,1)S(1)}, bf16[1,96,768]{2,1,0:T(8,128)(2,1)S(1)}, u32[]{:S(2)}, u32[]{:S(2)}) %collective-permute-start.54) | collective-permute-done | bytes 147488 | tf_op jit(solution)/shard_map/ppermute | solution.py:94
  510.6 8.9 %collective-permute-done.53 = bf16[1,96,768]{2,1,0:T(8,128)(2,1)S(1)} collective-permute-done((bf16[1,96,768]{2,1,0:T(8,128)(2,1)S(1)}, bf16[1,96,768]{2,1,0:T(8,128)(2,1)S(1)}, u32[]{:S(2)}, u32[]{:S(2)}) %collective-permute-start.53) | collective-permute-done | bytes 147488 | tf_op jit(solution)/shard_map/ppermute | solution.py:94
  539.8 10.5 %weight_grad.1 = f32[128,32,768]{2,1,0:T(8,128)} custom-call(bf16[128,48]{1,0:T(8,128)(2,1)} %fusion.63.feats_ref, bf16[48,32,768]{2,1,0:T(8,128)(2,1)} %bitcast.166), custom_call_target="tpu_custom_call" | custom-call | tf_op jit(solution)/shard_map/weight_grad/pallas_call | solution.py:937
  (377 shorter events, 190.6 us)
Async XLA Ops:
  7.2 187.7 %all-gather.3.cloned.1.call-start = ((), (), s32[]{:S(2)}) async-start(), calls=%async_computation | async-start | bytes 9732096 | tf_op jit(solution)/shard_map/all_gather | solution.py:184
  10.4 23.5 %collective-permute-start.1 = (bf16[1,1,1,1,96,768]{5,4,3,2,1,0:T(8,128)(2,1)S(1)}, bf16[1,1,1,1,96,768]{5,4,3,2,1,0:T(8,128)(2,1)S(1)}, u32[]{:S(2)}, u32[]{:S(2)}) collective-permute-start(bf16[1,1,1,1,96,768]{5,4,3,2,1,0:T(8,128)(2,1)S(1)} %get-tuple-element.361), channel_id=1, source_target_pairs={{0,4},{1,5},{2,6},{3,7},{4,0},{5,1},{6,2},{7,3},{8,12},{9,13},{10,... | collective-permute-start | bytes 442376 | tf_op jit(solution)/shard_map/ppermute | solution.py:94
  35.1 27.5 %collective-permute-start.5 = (bf16[4,1,1,32,768]{4,3,0,2,1:T(8,128)(2,1)S(1)}, bf16[4,1,1,32,768]{4,3,0,2,1:T(8,128)(2,1)S(1)}, u32[]{:S(2)}, u32[]{:S(2)}) collective-permute-start(bf16[4,1,1,32,768]{4,3,0,2,1:T(8,128)(2,1)S(1)} %get-tuple-element.390), channel_id=1, source_target_pairs={{0,6},{1,7},{2,4},{3,5},{4,2},{5,3},{6,0},{7,1},{8,14},{9,15},{10,... | collective-permute-start | bytes 589832 | tf_op jit(solution)/shard_map/ppermute | solution.py:94
  39.0 23.6 %collective-permute-start.4 = (bf16[4,1,1,32,768]{4,3,0,2,1:T(8,128)(2,1)S(1)}, bf16[4,1,1,32,768]{4,3,0,2,1:T(8,128)(2,1)S(1)}, u32[]{:S(2)}, u32[]{:S(2)}) collective-permute-start(bf16[4,1,1,32,768]{4,3,0,2,1:T(8,128)(2,1)S(1)} %get-tuple-element.390), channel_id=1, source_target_pairs={{0,4},{1,5},{2,6},{3,7},{4,0},{5,1},{6,2},{7,3},{8,12},{9,13},{10,... | collective-permute-start | bytes 589832 | tf_op jit(solution)/shard_map/ppermute | solution.py:94
  63.1 35.9 %collective-permute-start.13 = (bf16[4,2,1,1,96,768]{5,4,3,2,1,0:T(8,128)(2,1)S(1)}, bf16[4,2,1,1,96,768]{5,4,3,2,1,0:T(8,128)(2,1)}, u32[]{:S(2)}, u32[]{:S(2)}) collective-permute-start(bf16[4,2,1,1,96,768]{5,4,3,2,1,0:T(8,128)(2,1)S(1)} %maximum_select_fusion.7), channel_id=1, source_target_pairs={{0,16},{8,24},{16,0},{24,8},{1,17},{9,25},{17,1},{25,9},{2,18},{10... | collective-permute-start | bytes 3538952 | tf_op jit(solution)/shard_map/ppermute | solution.py:88
  65.8 30.1 %collective-permute-start.11 = (bf16[4,1,1,32,768]{4,3,0,2,1:T(8,128)(2,1)S(1)}, bf16[4,1,1,32,768]{4,3,0,2,1:T(8,128)(2,1)S(1)}, u32[]{:S(2)}, u32[]{:S(2)}) collective-permute-start(bf16[4,1,1,32,768]{4,3,0,2,1:T(8,128)(2,1)S(1)} %get-tuple-element.159), channel_id=1, source_target_pairs={{0,6},{1,7},{2,4},{3,5},{4,2},{5,3},{6,0},{7,1},{8,14},{9,15},{10,... | collective-permute-start | bytes 589832 | tf_op jit(solution)/shard_map/ppermute | solution.py:94
  68.6 27.3 %collective-permute-start.10 = (bf16[4,1,1,32,768]{4,3,0,2,1:T(8,128)(2,1)S(1)}, bf16[4,1,1,32,768]{4,3,0,2,1:T(8,128)(2,1)S(1)}, u32[]{:S(2)}, u32[]{:S(2)}) collective-permute-start(bf16[4,1,1,32,768]{4,3,0,2,1:T(8,128)(2,1)S(1)} %get-tuple-element.159), channel_id=1, source_target_pairs={{0,4},{1,5},{2,6},{3,7},{4,0},{5,1},{6,2},{7,3},{8,12},{9,13},{10,... | collective-permute-start | bytes 589832 | tf_op jit(solution)/shard_map/ppermute | solution.py:94
  70.3 27.0 %collective-permute-start.12 = (bf16[4,4,1,32,768]{4,3,2,1,0:T(8,128)(2,1)S(1)}, bf16[4,4,1,32,768]{4,3,2,1,0:T(8,128)(2,1)S(1)}, u32[]{:S(2)}, u32[]{:S(2)}) collective-permute-start(bf16[4,4,1,32,768]{4,3,2,1,0:T(8,128)(2,1)S(1)} %bitcast_dynamic-update-slice_fusion.9), channel_id=1, source_target_pairs={{0,1},{1,0},{2,3},{3,2},{4,5},{5,4},{6,7},{7,6},{8,9},{9,8},{10,11... | collective-permute-start | bytes 2359304 | tf_op jit(solution)/shard_map/ppermute | solution.py:91
  101.7 30.4 %collective-permute-start.18 = (bf16[4,2,2,1,96,768]{5,4,3,2,1,0:T(8,128)(2,1)S(1)}, bf16[4,2,2,1,96,768]{5,4,3,2,1,0:T(8,128)(2,1)S(1)}, u32[]{:S(2)}, u32[]{:S(2)}) collective-permute-start(bf16[4,2,2,1,96,768]{5,4,3,2,1,0:T(8,128)(2,1)S(1)} %maximum_select_fusion.2), channel_id=1, source_target_pairs={{0,8},{8,0},{16,24},{24,16},{1,9},{9,1},{17,25},{25,17},{2,10},{10... | collective-permute-start | bytes 7077896 | tf_op jit(solution)/shard_map/ppermute | solution.py:85
  101.8 30.2 %collective-permute-start.16 = (bf16[4,1,1,32,768]{4,3,0,2,1:T(8,128)(2,1)S(1)}, bf16[4,1,1,32,768]{4,3,0,2,1:T(8,128)(2,1)S(1)}, u32[]{:S(2)}, u32[]{:S(2)}) collective-permute-start(bf16[4,1,1,32,768]{4,3,0,2,1:T(8,128)(2,1)S(1)} %get-tuple-element.170), channel_id=1, source_target_pairs={{0,6},{1,7},{2,4},{3,5},{4,2},{5,3},{6,0},{7,1},{8,14},{9,15},{10,... | collective-permute-start | bytes 589832 | tf_op jit(solution)/shard_map/ppermute | solution.py:94
  105.6 26.4 %collective-permute-start.15 = (bf16[4,1,1,32,768]{4,3,0,2,1:T(8,128)(2,1)S(1)}, bf16[4,1,1,32,768]{4,3,0,2,1:T(8,128)(2,1)S(1)}, u32[]{:S(2)}, u32[]{:S(2)}) collective-permute-start(bf16[4,1,1,32,768]{4,3,0,2,1:T(8,128)(2,1)S(1)} %get-tuple-element.170), channel_id=1, source_target_pairs={{0,4},{1,5},{2,6},{3,7},{4,0},{5,1},{6,2},{7,3},{8,12},{9,13},{10,... | collective-permute-start | bytes 589832 | tf_op jit(solution)/shard_map/ppermute | solution.py:94
  105.6 21.7 %collective-permute-start.14 = (bf16[4,1,1,32,768]{4,3,0,2,1:T(8,128)(2,1)S(1)}, bf16[4,1,1,32,768]{4,3,0,2,1:T(8,128)(2,1)S(1)}, u32[]{:S(2)}, u32[]{:S(2)}) collective-permute-start(bf16[4,1,1,32,768]{4,3,0,2,1:T(8,128)(2,1)S(1)} %get-tuple-element.170), channel_id=1, source_target_pairs={{0,2},{1,3},{2,0},{3,1},{4,6},{5,7},{6,4},{7,5},{8,10},{9,11},{10,... | collective-permute-start | bytes 589832 | tf_op jit(solution)/shard_map/ppermute | solution.py:94
  106.5 25.6 %collective-permute-start.17 = (bf16[4,4,1,32,768]{4,3,2,1,0:T(8,128)(2,1)S(1)}, bf16[4,4,1,32,768]{4,3,2,1,0:T(8,128)(2,1)S(1)}, u32[]{:S(2)}, u32[]{:S(2)}) collective-permute-start(bf16[4,4,1,32,768]{4,3,2,1,0:T(8,128)(2,1)S(1)} %bitcast_dynamic-update-slice_fusion.5), channel_id=1, source_target_pairs={{0,1},{1,0},{2,3},{3,2},{4,5},{5,4},{6,7},{7,6},{8,9},{9,8},{10,11... | collective-permute-start | bytes 2359304 | tf_op jit(solution)/shard_map/ppermute | solution.py:91
  213.3 27.0 %collective-permute-start.20 = (bf16[768,1536]{1,0:T(8,128)(2,1)}, bf16[768,1536]{1,0:T(8,128)(2,1)S(1)}, u32[]{:S(2)}, u32[]{:S(2)}) collective-permute-start(bf16[768,1536]{1,0:T(8,128)(2,1)} %get-tuple-element.200), channel_id=1, source_target_pairs={{0,8},{8,0},{16,24},{24,16},{1,9},{9,1},{17,25},{25,17},{2,10},{10... | collective-permute-start | bytes 7077896 | tf_op jit(solution)/shard_map/ppermute | solution.py:85
  213.3 26.9 %collective-permute-start.21 = (bf16[1536,768]{1,0:T(8,128)(2,1)}, bf16[1536,768]{1,0:T(8,128)(2,1)}, u32[]{:S(2)}, u32[]{:S(2)}) collective-permute-start(bf16[1536,768]{1,0:T(8,128)(2,1)} %get-tuple-element.201), channel_id=1, source_target_pairs={{0,8},{8,0},{16,24},{24,16},{1,9},{9,1},{17,25},{25,17},{2,10},{10... | collective-permute-start | bytes 7077896 | tf_op jit(solution)/shard_map/ppermute | solution.py:85
  251.6 34.9 %collective-permute-start.22 = (bf16[4,1,96,1536]{3,2,1,0:T(8,128)(2,1)}, bf16[4,1,96,1536]{3,2,1,0:T(8,128)(2,1)}, u32[]{:S(2)}, u32[]{:S(2)}) collective-permute-start(bf16[4,1,96,1536]{3,2,1,0:T(8,128)(2,1)} %constant_dynamic-slice_fusion.17), channel_id=1, source_target_pairs={{0,1},{1,0},{2,3},{3,2},{4,5},{5,4},{6,7},{7,6},{8,9},{9,8},{10,11... | collective-permute-start | bytes 3538952 | tf_op jit(solution)/shard_map/ppermute | solution.py:91
  253.4 33.1 %collective-permute-start.23 = (bf16[4,1,192,768]{3,2,1,0:T(8,128)(2,1)}, bf16[4,1,192,768]{3,2,1,0:T(8,128)(2,1)}, u32[]{:S(2)}, u32[]{:S(2)}) collective-permute-start(bf16[4,1,192,768]{3,2,1,0:T(8,128)(2,1)} %constant_dynamic-slice_fusion.16), channel_id=1, source_target_pairs={{0,16},{8,24},{16,0},{24,8},{1,17},{9,25},{17,1},{25,9},{2,18},{10... | collective-permute-start | bytes 3538952 | tf_op jit(solution)/shard_map/ppermute | solution.py:88
  321.0 25.3 %collective-permute-start.26 = (bf16[12,4,1,16,768]{4,3,2,1,0:T(8,128)(2,1)S(1)}, bf16[12,4,1,16,768]{4,3,2,1,0:T(8,128)(2,1)S(1)}, u32[]{:S(2)}, u32[]{:S(2)}) collective-permute-start(bf16[12,4,1,16,768]{4,3,2,1,0:T(8,128)(2,1)S(1)} %constant_dynamic-slice_fusion.13), channel_id=1, source_target_pairs={{0,1},{1,0},{2,3},{3,2},{4,5},{5,4},{6,7},{7,6},{8,9},{9,8},{10,11... | collective-permute-start | bytes 3538952 | tf_op jit(solution)/shard_map/ppermute | solution.py:91
  348.4 40.7 %collective-permute-start.34 = (bf16[2,768,768]{2,1,0:T(8,128)(2,1)}, bf16[2,768,768]{2,1,0:T(8,128)(2,1)}, u32[]{:S(2)}, u32[]{:S(2)}) collective-permute-start(bf16[2,768,768]{2,1,0:T(8,128)(2,1)} %pad_maximum_fusion), channel_id=1, source_target_pairs={{0,8},{8,0},{16,24},{24,16},{1,9},{9,1},{17,25},{25,17},{2,10},{10... | collective-permute-start | bytes 7077896 | tf_op jit(solution)/shard_map/ppermute | solution.py:85
  350.1 26.5 %collective-permute-start.31 = (bf16[12,1,16,768]{3,0,2,1:T(8,128)(2,1)S(1)}, bf16[12,1,16,768]{3,0,2,1:T(8,128)(2,1)S(1)}, u32[]{:S(2)}, u32[]{:S(2)}) collective-permute-start(bf16[12,1,16,768]{3,0,2,1:T(8,128)(2,1)S(1)} %get-tuple-element.375), channel_id=1, source_target_pairs={{0,2},{1,3},{2,0},{3,1},{4,6},{5,7},{6,4},{7,5},{8,10},{9,11},{10,... | collective-permute-start | bytes 884744 | tf_op jit(solution)/shard_map/ppermute | solution.py:94
  351.4 25.8 %collective-permute-start.33 = (bf16[12,1,16,768]{3,0,2,1:T(8,128)(2,1)S(1)}, bf16[12,1,16,768]{3,0,2,1:T(8,128)(2,1)S(1)}, u32[]{:S(2)}, u32[]{:S(2)}) collective-permute-start(bf16[12,1,16,768]{3,0,2,1:T(8,128)(2,1)S(1)} %get-tuple-element.376), channel_id=1, source_target_pairs={{0,6},{1,7},{2,4},{3,5},{4,2},{5,3},{6,0},{7,1},{8,14},{9,15},{10,... | collective-permute-start | bytes 884744 | tf_op jit(solution)/shard_map/ppermute | solution.py:94
  352.8 35.0 %collective-permute-start.32 = (bf16[12,1,16,768]{3,0,2,1:T(8,128)(2,1)S(1)}, bf16[12,1,16,768]{3,0,2,1:T(8,128)(2,1)S(1)}, u32[]{:S(2)}, u32[]{:S(2)}) collective-permute-start(bf16[12,1,16,768]{3,0,2,1:T(8,128)(2,1)S(1)} %get-tuple-element.377), channel_id=1, source_target_pairs={{0,4},{1,5},{2,6},{3,7},{4,0},{5,1},{6,2},{7,3},{8,12},{9,13},{10,... | collective-permute-start | bytes 884744 | tf_op jit(solution)/shard_map/ppermute | solution.py:94
  353.7 35.4 %collective-permute-start.30 = (bf16[12,4,1,16,768]{4,3,2,1,0:T(8,128)(2,1)}, bf16[12,4,1,16,768]{4,3,2,1,0:T(8,128)(2,1)S(1)}, u32[]{:S(2)}, u32[]{:S(2)}) collective-permute-start(bf16[12,4,1,16,768]{4,3,2,1,0:T(8,128)(2,1)} %constant_dynamic-slice_fusion.12), channel_id=1, source_target_pairs={{0,1},{1,0},{2,3},{3,2},{4,5},{5,4},{6,7},{7,6},{8,9},{9,8},{10,11... | collective-permute-start | bytes 3538952 | tf_op jit(solution)/shard_map/ppermute | solution.py:91
  393.9 44.0 %collective-permute-start.39 = (bf16[1,768,768]{2,1,0:T(8,128)(2,1)}, bf16[1,768,768]{2,1,0:T(8,128)(2,1)}, u32[]{:S(2)}, u32[]{:S(2)}) collective-permute-start(bf16[1,768,768]{2,1,0:T(8,128)(2,1)} %constant_dynamic-slice_fusion.5), channel_id=1, source_target_pairs={{0,16},{8,24},{16,0},{24,8},{1,17},{9,25},{17,1},{25,9},{2,18},{10... | collective-permute-start | bytes 3538952 | tf_op jit(solution)/shard_map/ppermute | solution.py:88
  396.2 40.3 %collective-permute-start.36 = (bf16[12,1,16,768]{3,0,2,1:T(8,128)(2,1)}, bf16[12,1,16,768]{3,0,2,1:T(8,128)(2,1)}, u32[]{:S(2)}, u32[]{:S(2)}) collective-permute-start(bf16[12,1,16,768]{3,0,2,1:T(8,128)(2,1)} %get-tuple-element.372), channel_id=1, source_target_pairs={{0,2},{1,3},{2,0},{3,1},{4,6},{5,7},{6,4},{7,5},{8,10},{9,11},{10,... | collective-permute-start | bytes 884744 | tf_op jit(solution)/shard_map/ppermute | solution.py:94
  398.2 38.3 %collective-permute-start.38 = (bf16[12,1,16,768]{3,0,2,1:T(8,128)(2,1)}, bf16[12,1,16,768]{3,0,2,1:T(8,128)(2,1)}, u32[]{:S(2)}, u32[]{:S(2)}) collective-permute-start(bf16[12,1,16,768]{3,0,2,1:T(8,128)(2,1)} %get-tuple-element.373), channel_id=1, source_target_pairs={{0,6},{1,7},{2,4},{3,5},{4,2},{5,3},{6,0},{7,1},{8,14},{9,15},{10,... | collective-permute-start | bytes 884744 | tf_op jit(solution)/shard_map/ppermute | solution.py:94
  399.7 36.8 %collective-permute-start.37 = (bf16[12,1,16,768]{3,0,2,1:T(8,128)(2,1)S(1)}, bf16[12,1,16,768]{3,0,2,1:T(8,128)(2,1)}, u32[]{:S(2)}, u32[]{:S(2)}) collective-permute-start(bf16[12,1,16,768]{3,0,2,1:T(8,128)(2,1)S(1)} %get-tuple-element.374), channel_id=1, source_target_pairs={{0,4},{1,5},{2,6},{3,7},{4,0},{5,1},{6,2},{7,3},{8,12},{9,13},{10,... | collective-permute-start | bytes 884744 | tf_op jit(solution)/shard_map/ppermute | solution.py:94
  399.7 36.8 %collective-permute-start.41 = (f32[13,768]{1,0:T(8,128)S(1)}, f32[13,768]{1,0:T(8,128)S(1)}, u32[]{:S(2)}, u32[]{:S(2)}) collective-permute-start(f32[13,768]{1,0:T(8,128)S(1)} %add.300), channel_id=1, source_target_pairs={{0,4},{1,5},{2,6},{3,7},{4,0},{5,1},{6,2},{7,3},{8,12},{9,13},{10,... | collective-permute-start | bytes 119816 | tf_op jit(solution)/shard_map/ppermute | solution.py:94
  453.8 40.5 %collective-permute-start.59 = (bf16[1,1,192,768]{3,2,1,0:T(8,128)(2,1)}, bf16[1,1,192,768]{3,2,1,0:T(8,128)(2,1)S(1)}, u32[]{:S(2)}, u32[]{:S(2)}) collective-permute-start(bf16[1,1,192,768]{3,2,1,0:T(8,128)(2,1)} %constant_dynamic-slice_fusion), channel_id=1, source_target_pairs={{0,2},{1,3},{2,0},{3,1},{4,6},{5,7},{6,4},{7,5},{8,10},{9,11},{10,... | collective-permute-start | bytes 884744 | tf_op jit(solution)/shard_map/ppermute | solution.py:94
  456.8 70.2 %collective-permute-start.49 = (bf16[1,1,12,32,768]{4,3,2,1,0:T(8,128)(2,1)}, bf16[1,1,12,32,768]{4,3,2,1,0:T(8,128)(2,1)}, u32[]{:S(2)}, u32[]{:S(2)}) collective-permute-start(bf16[1,1,12,32,768]{4,3,2,1,0:T(8,128)(2,1)} %copy.121), channel_id=1, source_target_pairs={{0,16},{8,24},{16,0},{24,8},{1,17},{9,25},{17,1},{25,9},{2,18},{10... | collective-permute-start | bytes 1769480 | tf_op jit(solution)/shard_map/ppermute | solution.py:88
  458.3 37.4 %collective-permute-start.51 = (bf16[4,1,96,768]{3,2,1,0:T(8,128)(2,1)S(1)}, bf16[4,1,96,768]{3,2,1,0:T(8,128)(2,1)}, u32[]{:S(2)}, u32[]{:S(2)}) collective-permute-start(bf16[4,1,96,768]{3,2,1,0:T(8,128)(2,1)S(1)} %constant_dynamic-slice_fusion.1), channel_id=1, source_target_pairs={{0,1},{1,0},{2,3},{3,2},{4,5},{5,4},{6,7},{7,6},{8,9},{9,8},{10,11... | collective-permute-start | bytes 1769480 | tf_op jit(solution)/shard_map/ppermute | solution.py:91
  494.4 26.8 %collective-permute-start.60 = (bf16[192,768]{1,0:T(8,128)(2,1)S(1)}, bf16[192,768]{1,0:T(8,128)(2,1)S(1)}, u32[]{:S(2)}, u32[]{:S(2)}) collective-permute-start(bf16[192,768]{1,0:T(8,128)(2,1)S(1)} %fusion.35), channel_id=1, source_target_pairs={{4,0},{5,1},{6,2},{7,3},{8,12},{9,13},{10,14},{11,15},{20,16},{21,... | collective-permute-start | bytes 884744 | tf_op jit(solution)/shard_map/ppermute | solution.py:110
  (74 other events, 714.6 us)
Sparse Core Ops, SparseCore 0:
  11.5 119.3 all-gather.2

commit v2 on v1

--- a/solution.py
+++ b/solution.py
@@ -119,8 +119,11 @@
     return lax.dynamic_slice_in_dim(block, index, count, axis)
 
 
-def add_low(one, two):
-    return (one.astype(jnp.float32) + two.astype(jnp.float32)).astype(jnp.bfloat16)
+def add_low(*items):
+    total = items[0].astype(jnp.float32)
+    for item in items[1:]:
+        total = total + item.astype(jnp.float32)
+    return total.astype(jnp.bfloat16)
 
 
 def pair_up(block, other, bit, axis):
@@ -151,19 +154,16 @@
     return block.reshape(lead + (links.line,) + tail)
 
 
-def reduce_line(links, block, axis, sender):
+def send_line(links, block, axis, sender):
     lead, tail = block.shape[:axis], block.shape[axis + 1 :]
     block = block.reshape(lead + tuple(size for size, _, _ in links.digits) + tail)
     for place, (size, stride, me) in enumerate(links.digits):
         if place:
-            block = block.astype(jnp.bfloat16)
-        received = [
+            block = add_low(*terms)
+        terms = [pick(block, me, axis + place)] + [
             sender(pick(block, me ^ step, axis + place), stride * step) for step in range(1, size)
         ]
-        block = pick(block, me, axis + place).astype(jnp.float32)
-        for piece in received:
-            block = block + piece.astype(jnp.float32)
-    return block.reshape(lead + tail)
+    return [term.reshape(lead + tail) for term in terms]
 
 
 def attention_piece(links, attention_in, attention_out):
@@ -271,6 +271,43 @@
     )(part, pixel_rows, wide_kernel, norm_one)
 
 
+def pixel_grad_body(grad_ref, kernel_ref, out_ref, *wide_refs):
+    rows, bands, depth = out_ref.shape
+    padded = wide_refs[0].shape[0] // rows
+    for band in range(bands):
+        part = dot_nt(grad_ref[...], kernel_ref[band * depth : (band + 1) * depth, :])
+        for place, ref in enumerate(wide_refs):
+            ref[pl.ds(band, rows, stride=padded), :] = part[:, place * 128 : (place + 1) * 128]
+    for place, ref in enumerate(wide_refs):
+        wide = ref[...].reshape(rows, padded, 128)
+        out_ref[:, :, place * 128 : (place + 1) * 128] = wide[:, :bands].astype(out_ref.dtype)
+
+
+def pixel_gradient(conv_low, wide_kernel, bands):
+    rows, width = conv_low.shape
+    depth = wide_kernel.shape[0] // bands
+    block_rows = 128
+    padded = -(-bands // 8) * 8
+    return pl.pallas_call(
+        pixel_grad_body,
+        grid=(rows // block_rows,),
+        in_specs=[
+            pl.BlockSpec((block_rows, width), lambda i: (i, 0)),
+            whole_spec(wide_kernel.shape),
+        ],
+        out_specs=pl.BlockSpec((block_rows, bands, depth), lambda i: (i, 0, 0)),
+        out_shape=jax.ShapeDtypeStruct((rows, bands, depth), jnp.bfloat16),
+        scratch_shapes=[pltpu.VMEM((block_rows * padded, 128), jnp.float32)] * (depth // 128),
+        compiler_params=kernel_params(),
+        cost_estimate=pl.CostEstimate(
+            flops=2 * rows * width * bands * depth,
+            bytes_accessed=4 * bands * depth * (width + rows),
+            transcendentals=0,
+        ),
+        name="pixel_gradient",
+    )(conv_low, wide_kernel)
+
+
 def pair_stack(block, low_half):
     zero = jnp.zeros_like(block)
     return jnp.concatenate(
@@ -297,6 +334,7 @@
     mixed_ref,
     middle_ref,
     hidden_two_ref,
+    score_ref,
 ):
     block_rows, width = hidden_ref.shape
     slots = 64
@@ -311,22 +349,30 @@
     lanes = lax.broadcasted_iota(jnp.int32, (slots, 128), 1)
     low_half = lanes < 64
     key_id = jnp.where(low_half, lanes, lanes - 64)
+    pairs = width // 128
+    blocks = [(image, pair) for image in range(images) for pair in range(pairs)]
+    for place, (image, pair) in enumerate(blocks):
+        here = slice(image * slots, (image + 1) * slots)
+        at = pair * 128
+        queries = project_ref[here, at : at + 128]
+        keys = pair_stack(project_ref[here, width + at : width + at + 128], low_half)
+        keep = key_id < count_ref[base + image]
+        score_ref[place * slots : (place + 1) * slots, :] = jnp.where(
+            keep, dot_nt(queries, keys) * 0.125, -1000000000.0
+        )
     for image in range(images):
-        count = count_ref[base + image]
-        keep = key_id < count
+        here = slice(image * pairs * slots, (image + 1) * pairs * slots)
+        scores = score_ref[here, :]
+        wide_half = lax.broadcasted_iota(jnp.int32, scores.shape, 1) < 64
+        probs = jnp.exp(scores - half_reduce(scores, wide_half, jnp.max, -3e38))
+        score_ref[here, :] = probs / half_reduce(probs, wide_half, jnp.sum, 0.0)
+    for place, (image, pair) in enumerate(blocks):
         here = slice(image * slots, (image + 1) * slots)
-        for pair in range(width // 128):
-            at = pair * 128
-            queries = project_ref[here, at : at + 128]
-            keys = pair_stack(project_ref[here, width + at : width + at + 128], low_half)
-            values = pair_stack(project_ref[here, 2 * width + at : 2 * width + at + 128], low_half)
-            scores = jnp.where(keep, dot_nt(queries, keys) * 0.125, -1000000000.0)
-            peak = half_reduce(scores, low_half, jnp.max, -3e38)
-            probs = jnp.exp(scores - peak)
-            total = half_reduce(probs, low_half, jnp.sum, 0.0)
-            probs_low = (probs / total).astype(jnp.bfloat16)
-            probs_ref[here, at : at + 128] = probs_low
-            mixed_ref[here, at : at + 128] = dot_nn(probs_low, values).astype(jnp.bfloat16)
+        at = pair * 128
+        values = pair_stack(project_ref[here, 2 * width + at : 2 * width + at + 128], low_half)
+        probs_low = score_ref[place * slots : (place + 1) * slots, :].astype(jnp.bfloat16)
+        probs_ref[here, at : at + 128] = probs_low
+        mixed_ref[here, at : at + 128] = dot_nn(probs_low, values).astype(jnp.bfloat16)
     middle = start_ref[...] + dot_nn(mixed_ref[...], weight_ref[:, 3].reshape(width, width)) + rows_ref[0:1, :]
     middle_ref[...] = middle
     normed, _ = norm_rows(middle, 1e-06)
@@ -364,6 +410,7 @@
                 row_spec(width),
                 row_spec(width),
             ],
+            scratch_shapes=[pltpu.VMEM((block_rows * width // 128, 128), jnp.float32)],
         ),
         out_shape=[
             jax.ShapeDtypeStruct((rows, 3 * width), low),
@@ -627,6 +674,7 @@
     sums_ref,
     third_ref,
     mixed_low,
+    grad_ref,
 ):
     block_rows, width = start_ref.shape
     slots = 64
@@ -639,25 +687,38 @@
     def fold(block):
         return jnp.where(low_half, block[:slots], block[slots:])
 
-    for image in range(block_rows // slots):
+    pairs = width // 128
+    images = block_rows // slots
+    blocks = [(image, pair) for image in range(images) for pair in range(pairs)]
+    for place, (image, pair) in enumerate(blocks):
         here = slice(image * slots, (image + 1) * slots)
-        for pair in range(width // 128):
-            at = pair * 128
-            queries = project_ref[here, at : at + 128]
-            keys = pair_stack(project_ref[here, width + at : width + at + 128], low_half)
-            values = pair_stack(project_ref[here, 2 * width + at : 2 * width + at + 128], low_half)
-            probs_low = probs_ref[here, at : at + 128]
-            mixed = mixed_low[here, at : at + 128]
-            probs = probs_low.astype(jnp.float32)
-            prob_grad = dot_nt(mixed, values)
-            value_grad = fold(dot_tn(probs_low, mixed))
-            centre = half_reduce(prob_grad * probs, low_half, jnp.sum, 0.0)
-            score_low = (probs * (prob_grad - centre)).astype(low)
-            project_low_ref[here, at : at + 128] = (dot_nn(score_low, keys) * 0.125).astype(low)
-            project_low_ref[here, width + at : width + at + 128] = (
-                fold(dot_tn(score_low, queries)) * 0.125
-            ).astype(low)
-            project_low_ref[here, 2 * width + at : 2 * width + at + 128] = value_grad.astype(low)
+        at = pair * 128
+        values = pair_stack(project_ref[here, 2 * width + at : 2 * width + at + 128], low_half)
+        mixed = mixed_low[here, at : at + 128]
+        grad_ref[place * slots : (place + 1) * slots, :] = dot_nt(mixed, values)
+        project_low_ref[here, 2 * width + at : 2 * width + at + 128] = fold(
+            dot_tn(probs_ref[here, at : at + 128], mixed)
+        ).astype(low)
+    for image in range(images):
+        rows = slice(image * slots, (image + 1) * slots)
+        probs = jnp.concatenate(
+            [probs_ref[rows, pair * 128 : (pair + 1) * 128] for pair in range(pairs)], 0
+        ).astype(jnp.float32)
+        here = slice(image * pairs * slots, (image + 1) * pairs * slots)
+        prob_grad = grad_ref[here, :]
+        wide_half = lax.broadcasted_iota(jnp.int32, prob_grad.shape, 1) < 64
+        centre = half_reduce(prob_grad * probs, wide_half, jnp.sum, 0.0)
+        grad_ref[here, :] = probs * (prob_grad - centre)
+    for place, (image, pair) in enumerate(blocks):
+        here = slice(image * slots, (image + 1) * slots)
+        at = pair * 128
+        queries = project_ref[here, at : at + 128]
+        keys = pair_stack(project_ref[here, width + at : width + at + 128], low_half)
+        score_low = grad_ref[place * slots : (place + 1) * slots, :].astype(low)
+        project_low_ref[here, at : at + 128] = (dot_nn(score_low, keys) * 0.125).astype(low)
+        project_low_ref[here, width + at : width + at + 128] = (
+            fold(dot_tn(score_low, queries)) * 0.125
+        ).astype(low)
     project_low = project_low_ref[...]
     grad = dot_nt(project_low[:, :width], weight_ref[:, 0].reshape(width, width))
     for third in (1, 2):
@@ -723,7 +784,10 @@
             jax.ShapeDtypeStruct((3, width), jnp.float32),
             jax.ShapeDtypeStruct((1, 3 * width), jnp.float32),
         ],
-        scratch_shapes=[pltpu.VMEM((block_rows, width), low)],
+        scratch_shapes=[
+            pltpu.VMEM((block_rows, width), low),
+            pltpu.VMEM((block_rows * width // 128, 128), jnp.float32),
+        ],
         compiler_params=kernel_params(),
         cost_estimate=pl.CostEstimate(
             flops=24 * rows * width * width,
@@ -734,13 +798,14 @@
     )(project, probs_low, start, middle_grad, middle_low, weights, rows_in)
 
 
-def dot_full(one, two, dims):
+def dot_full(one, two, dims, precision=highest):
     return lax.dot_general(
-        one, two, (dims, ((), ())), precision=highest, preferred_element_type=jnp.float32
+        one, two, (dims, ((), ())), precision=precision, preferred_element_type=jnp.float32
     )
 
 
 def hyper_rows(
+    precision,
     pick_rows,
     bias_mask,
     key_rows,
@@ -753,19 +818,19 @@
 ):
     width = key_rows.shape[1]
     query_rows = dot_full(pick_rows, key_rows, ((1,), (0,)))
-    queries = dot_full(query_rows, hyper_project[:, :width], ((1,), (0,)))
-    keys_all = dot_full(key_rows, hyper_project[:, width : 2 * width], ((1,), (0,)))
-    values_all = dot_full(key_rows, hyper_project[:, 2 * width :], ((1,), (0,)))
+    queries = dot_full(query_rows, hyper_project[:, :width], ((1,), (0,)), precision)
+    keys_all = dot_full(key_rows, hyper_project[:, width : 2 * width], ((1,), (0,)), precision)
+    values_all = dot_full(key_rows, hyper_project[:, 2 * width :], ((1,), (0,)), precision)
     head_size = width // HH
     head_of = lax.broadcasted_iota(jnp.int32, (1, width), 1) // head_size
     mixed_rows = jnp.zeros_like(query_rows)
     for head in range(HH):
         here = (head_of == head).astype(jnp.float32)
-        scores = dot_full(queries * here, keys_all, ((1,), (1,))) * head_size ** (-0.5) + bias_mask
+        scores = dot_full(queries * here, keys_all, ((1,), (1,)), precision) * head_size ** (-0.5) + bias_mask
         peak = lax.stop_gradient(jnp.max(scores, -1, keepdims=True))
         weights = jnp.exp(scores - peak)
         weights = weights / jnp.sum(weights, -1, keepdims=True)
-        mixed_rows = mixed_rows + dot_full(weights, values_all * here, ((1,), (0,)))
+        mixed_rows = mixed_rows + dot_full(weights, values_all * here, ((1,), (0,)), precision)
 
     def norm(values, index):
         center = values - jnp.mean(values, -1, keepdims=True)
@@ -773,14 +838,14 @@
         gain = hyper_gains[index : index + 1, :]
         return center * inverse * gain + hyper_shifts[index : index + 1, :]
 
-    hidden = norm(query_rows + dot_full(mixed_rows, hyper_output, ((1,), (0,))), 0)
-    expand = dot_full(hidden, hyper_up, ((1,), (0,)))
+    hidden = norm(query_rows + dot_full(mixed_rows, hyper_output, ((1,), (0,)), precision), 0)
+    expand = dot_full(hidden, hyper_up, ((1,), (0,)), precision)
     expanded = expand * (0.5 + 0.5 * lax.erf(expand * 0.7071067811865476))
-    return norm(hidden + dot_full(expanded, hyper_down, ((1,), (0,))), 1)
+    return norm(hidden + dot_full(expanded, hyper_down, ((1,), (0,)), precision), 1)
 
 
 def hyper_forward_body(*refs):
-    refs[-1][...] = hyper_rows(*(ref[...].astype(jnp.float32) for ref in refs[:-1]))
+    refs[-1][...] = hyper_rows(highest, *(ref[...].astype(jnp.float32) for ref in refs[:-1]))
 
 
 def hyper_forward(pick_rows, bias_mask, key_rows, params):
@@ -799,7 +864,7 @@
     matrix_out, shift_out = refs[16:]
     conv = conv_ref[...] * scaler
     hidden, pull = jax.vjp(
-        lambda *items: hyper_rows(pick_ref[...], mask_ref[...], *items), key_ref[...], *params
+        lambda *items: hyper_rows(None, pick_ref[...], mask_ref[...], *items), key_ref[...], *params
     )
     rows = count + conv.shape[0]
     bias_grad = dot_full(conv, matrix_ref[...].astype(jnp.float32), ((1,), (1,)))
@@ -915,38 +980,139 @@
     )(feats, kernel_weight, kernel_bias)
 
 
-def weight_grad_body(feats_ref, grad_ref, out_ref, spread_ref):
+def table_body(feats_ref, out_ref):
+    out_ref[...] = spread_eye(feats_ref[...], out_ref.shape[0] // feats_ref.shape[0])
+
+
+def weight_table(feats, block):
+    feats = (scaler * feats).astype(jnp.bfloat16).T
+    if block != 16:
+        return feats
+    return pl.pallas_call(
+        table_body,
+        out_shape=jax.ShapeDtypeStruct(tuple(size * block for size in feats.shape), jnp.bfloat16),
+        compiler_params=kernel_params(),
+        name="weight_table",
+    )(feats)
+
+
+def weight_grad_body(table_ref, grad_ref, *refs):
+    out_ref = refs[-1]
     hidden, block, width = out_ref.shape
-
-    @pl.when(pl.program_id(0) == 0)
-    def _():
-        spread_ref[...] = spread_eye(feats_ref[...], block)
-
     grad = grad_ref[...].reshape(-1, width)
-    out_ref[...] = dot_nn(spread_ref[...], grad).reshape(hidden, block, width)
-
-
-def weight_grad(feats, kernel_all):
-    count, rows, width = kernel_all.shape
-    hidden = feats.shape[1]
-    block = 16
-    feats = (scaler * feats).astype(jnp.bfloat16)
-    if rows % block:
-        return jnp.einsum("sh,spd->hpd", feats, kernel_all, preferred_element_type=jnp.float32)
-    table = feats.T
+    out_ref[...] = dot_nn(table_ref[...], grad).reshape(hidden, block, width)
+
+
+def weight_grad(table, piece, place, rows, out):
+    count, block, width = piece.shape
+    if block != 16:
+        part = jnp.einsum("hs,spd->hpd", table, piece, preferred_element_type=jnp.float32)
+        return part if out is None else jnp.concatenate([out, part], 1)
+    hidden = table.shape[0] // block
+    halves = 2
+    keep = [] if out is None else [out]
     return pl.pallas_call(
         weight_grad_body,
-        grid=(rows // block,),
+        grid=(halves,),
         in_specs=[
-            whole_spec(table.shape),
-            pl.BlockSpec((count, block, width), lambda i: (0, i, 0)),
-        ],
-        out_specs=pl.BlockSpec((hidden, block, width), lambda i: (0, i, 0)),
+            pl.BlockSpec((hidden * block // halves, count * block), lambda i: (i, 0)),
+            whole_spec(piece.shape),
+            *(pl.BlockSpec(memory_space=pl.ANY) for _ in keep),
+        ],
+        out_specs=pl.BlockSpec((hidden // halves, block, width), lambda i: (i, place, 0)),
         out_shape=jax.ShapeDtypeStruct((hidden, rows, width), jnp.float32),
-        scratch_shapes=[pltpu.VMEM((hidden * block, count * block), jnp.bfloat16)],
+        input_output_aliases={2: 0} if keep else {},
         compiler_params=kernel_params(),
         name="weight_grad",
-    )(table, kernel_all)
+    )(table, piece, *keep)
+
+
+def feats_body(grad_ref, weight_ref, out_ref):
+    bands, block, width = grad_ref.shape
+    hidden = weight_ref.shape[0]
+    product = dot_nt(
+        grad_ref[...].reshape(bands * block, width), weight_ref[...].reshape(hidden * block, width)
+    )
+    iota = lambda shape, axis: lax.broadcasted_iota(jnp.int32, shape, axis)
+    same = iota(product.shape, 0) % block == iota(product.shape, 1) % block
+    kept = jnp.sum(jnp.where(same, product, 0.0).reshape(bands, block, hidden * block), 1)
+    fold_shape = (hidden * block, hidden)
+    fold = (iota(fold_shape, 0) // block == iota(fold_shape, 1)).astype(jnp.float32)
+    out_ref[...] = scaler * dot_full(kept, fold, ((1,), (0,)))
+
+
+def feats_piece(piece, kernel_weight, place):
+    bands, block, width = piece.shape
+    hidden = kernel_weight.shape[0]
+    if block != 16:
+        return scaler * jnp.einsum(
+            "spd,hpd->sh",
+            piece,
+            kernel_weight[:, place * block : (place + 1) * block],
+            preferred_element_type=jnp.float32,
+        )
+    return pl.pallas_call(
+        feats_body,
+        grid=(1,),
+        in_specs=[
+            whole_spec(piece.shape),
+            pl.BlockSpec((hidden, block, width), lambda i: (0, place, 0)),
+        ],
+        out_specs=whole_spec((bands, hidden)),
+        out_shape=jax.ShapeDtypeStruct((bands, hidden), jnp.float32),
+        compiler_params=kernel_params(),
+        name="feats_piece",
+    )(piece, kernel_weight)
+
+
+def finish_body(place_ref, own_ref, other_ref, in_ref, out_ref, up_ref, down_ref):
+    rows, width = out_ref.shape
+    half = rows // 2
+    widen = lambda item: item.astype(jnp.float32)
+
+    def emit(first, second):
+        for core, ref in enumerate((first, second)):
+            for y in range(2):
+                for block in range(2):
+                    at = (2 * core + block) * width
+                    up_ref[y * half : (y + 1) * half, at : at + width] = widen(
+                        ref[y, block * half : (block + 1) * half]
+                    )
+        in_ref[:, :width] = widen(first[0, rows : 2 * rows])
+        in_ref[:, width : 2 * width] = widen(second[0, rows : 2 * rows])
+        in_ref[:, 2 * width :] = widen(first[1, rows : 2 * rows])
+        out_ref[...] = widen(second[1, rows : 2 * rows])
+
+    def emit_down(ref):
+        part = down_ref.shape[0] // 2
+        for y in range(2):
+            down_ref[y * part : (y + 1) * part] = widen(ref[y, 2 * rows :])
+
+    pl.when(place_ref[0] == 0)(lambda: emit(own_ref, other_ref))
+    pl.when(place_ref[0] == 1)(lambda: emit(other_ref, own_ref))
+    pl.when(place_ref[1] == 1)(lambda: emit_down(own_ref))
+    pl.when(place_ref[1] == 0)(lambda: emit_down(other_ref))
+
+
+def finish_grads(place, own, other, rows, down_rows):
+    width = own.shape[2]
+    out = lambda *shape: jax.ShapeDtypeStruct(shape, jnp.float32)
+    return pl.pallas_call(
+        finish_body,
+        in_specs=[
+            pl.BlockSpec(memory_space=pltpu.SMEM),
+            pl.BlockSpec(memory_space=pltpu.VMEM),
+            pl.BlockSpec(memory_space=pltpu.VMEM),
+        ],
+        out_shape=[
+            out(rows, 3 * width),
+            out(rows, width),
+            out(rows, 4 * width),
+            out(down_rows, width),
+        ],
+        compiler_params=kernel_params(),
+        name="finish_grads",
+    )(place, own, other)
 
 
 def on_device(
@@ -1063,8 +1229,12 @@
     all_hidden = hyper_forward(pick_rows, bias_mask, key_rows, hyper_params)
     wave_count = group_size * band_count
     feats_all = all_hidden[:wave_count] + wave_all.reshape(wave_count, HE)
-    other_three, embed_part, weights, feats_all = stage(
-        other_three, embed_part, weights, feats_all
+    shard_pixels = kernel_bias.shape[0]
+    piece_count = 2
+    piece_pixels = shard_pixels // piece_count
+    table_all = weight_table(feats_all, piece_pixels)
+    other_three, embed_part, weights, table_all = stage(
+        other_three, embed_part, weights, table_all
     )
     kernel_three = pair_up(line_three, other_three, links.x, 2).reshape(depth, model_width)
 
@@ -1117,40 +1287,30 @@
     shard_rows = model_width // dp_size
     down_rows = reduce_weight.shape[0]
     up_shape = (links.line, 2, shard_rows, up_own.shape[1])
-    up_sum = add_low(up_own.reshape(up_shape), up_other.reshape(up_shape))
+    up_pair = [up_own.reshape(up_shape), up_other.reshape(up_shape)]
     down_shape = (-1, 2, down_rows // 2, model_width)
-    down_sum = add_low(down_own.reshape(down_shape), down_other.reshape(down_shape))
-
-    send_up = pick(up_sum, 1 - links.x, 1)
-    send_down = pick(down_sum, 1 - links.y, 1)
+    down_pair = [down_own.reshape(down_shape), down_other.reshape(down_shape)]
+
+    send_up = add_low(*(pick(item, 1 - links.x, 1) for item in up_pair))
+    send_down = add_low(*(pick(item, 1 - links.y, 1) for item in down_pair))
     send_up, send_down, middle_low = stage(send_up, send_down, middle_low)
     other_up = links.xside(send_up)
     other_down = links.yside(send_down)
     project_low, conv_low, sums_one, third_sums = attend_back(
         project, probs_low, start, middle_grad, middle_low, weights, gains[0:1], 256
     )
-    other_up, other_down, conv_low, project_low = stage(
-        other_up, other_down, conv_low, project_low
-    )
-    up_sum = add_low(pick(up_sum, links.x, 1), other_up).reshape(
-        links.line, 2, shard_rows // 2, -1
-    )
-    down_sum = add_low(pick(down_sum, links.y, 1), other_down)
-
-    send_up = pick(up_sum, 1 - links.y, 1)
-    down_sum = down_sum.reshape(-1, 2, down_rows // 2, model_width)
-    send_down = pick(down_sum, 1 - links.x, 1)
-    send_up, send_down, conv_low = stage(send_up, send_down, conv_low)
-    other_up = links.yside(send_up)
-    other_down = links.xside(send_down)
     kernel_grad = contract_rows(pixel_rows, conv_low).astype(low)
-    kernel_grad = kernel_grad.reshape(band_count, links.line, 2, -1, model_width)
-    piece_count = 2
-    piece_pixels = kernel_grad.shape[3] // piece_count
+    kernel_grad = kernel_grad.reshape(band_count, links.line, 2, shard_pixels, model_width)
     piece_of = lambda i, side: pick(
         kernel_grad[:, :, :, i * piece_pixels : (i + 1) * piece_pixels], side, 2
     )
-    sends = [piece_of(i, 1 - links.x) for i in range(piece_count)]
+    send_one = piece_of(0, 1 - links.x)
+    other_up, other_down, kernel_grad, send_one = stage(
+        other_up, other_down, kernel_grad, send_one
+    )
+    up_sum = add_low(*(pick(item, links.x, 1) for item in up_pair), other_up)
+    up_sum = up_sum.reshape(links.line, 2, shard_rows // 2, -1)
+    down_sum = add_low(*(pick(item, links.y, 1) for item in down_pair), other_down)
     small = jnp.concatenate(
         [
             sums_one[0:1],
@@ -1165,17 +1325,25 @@
         ],
         0,
     )
-    other_up, other_down, sends, kernel_grad, small = stage(
-        other_up, other_down, sends, kernel_grad, small
-    )
-    up_sum = add_low(pick(up_sum, links.y, 1), other_up)
-    down_sum = add_low(pick(down_sum, links.x, 1), other_down)
-    line_parts = lambda block: block.reshape(band_count, links.line, -1, model_width)
-    finish_piece = lambda total: total.astype(low).reshape(band_count, -1, model_width)
-
-    up_sum, sends, project_low, middle_low = stage(up_sum, sends, project_low, middle_low)
-    other = links.xside(sends[0])
-    up_total = reduce_line(links, up_sum, 0, links.zside).astype(low)
+
+    def halve_down(block, stride):
+        block = block.reshape(2, -1, down_rows // 2, model_width)
+        bit = lax.axis_index("dp") // stride % 2
+        return pick(block, 1 - bit, 0), pick(block, bit, 0)
+
+    send_up = pick(up_sum, 1 - links.y, 1)
+    stride = dp_size // 4
+    send_down, keep_down = halve_down(down_sum, stride)
+    other_one = links.xside(send_one)
+    send_up, send_down, keep_down, small, project_low = stage(
+        send_up, send_down, keep_down, small, project_low
+    )
+    other_up = links.yside(send_up)
+    other_down = links.zside(send_down, stride)
+    step = 2
+    while step < dp_size:
+        small = small + links.zside(small, step)
+        step *= 2
     grad_units = [
         contract_rows(hidden_one, project_low[:, i * model_width : (i + 1) * model_width])
         for i in range(3)
@@ -1188,92 +1356,145 @@
         ]
     )
     send_units = units_of(1 - links.c)
-    keep_units = units_of(links.c)
-    other, up_total, send_units, keep_units, sends, small = stage(
-        other, up_total, send_units, keep_units, sends, small
-    )
-    ready = line_parts(add_low(piece_of(0, links.x), other))
-
-    ready, send_units, sends, small = stage(ready, send_units, sends, small)
-    other = links.xside(sends[1])
-    total_one = reduce_line(links, ready, 1, links.zside)
+    send_two = piece_of(1, 1 - links.x)
+    other_one, other_up, other_down, small, send_units, send_two, kernel_grad = stage(
+        other_one, other_up, other_down, small, send_units, send_two, kernel_grad
+    )
+    line_parts = lambda block: block.reshape(band_count, links.line, -1, model_width)
+    finish_piece = lambda terms: add_low(*terms).reshape(band_count, -1, model_width)
+    ready = line_parts(add_low(piece_of(0, links.x), other_one))
+
+    ready, send_two, send_units, conv_low, other_up, other_down = stage(
+        ready, send_two, send_units, conv_low, other_up, other_down
+    )
+    other_two = links.xside(send_two)
+    total_one = send_line(links, ready, 1, links.zside)
     other_units = links.core(send_units)
-    small = small + links.zside(small, 1)
-    wide_kernel = jnp.concatenate([kernel_one, kernel_two, kernel_three], 0)
-    pixel_grad = dot_nt(conv_low, wide_kernel).astype(low)
-    other, total_one, other_units, small, pixel_grad = stage(
-        other, total_one, other_units, small, pixel_grad
-    )
-    units = add_low(keep_units, other_units)
-    ready = line_parts(add_low(piece_of(1, links.x), other))
-    pixel_grad = pixel_grad.reshape(pixels.shape)
+    up_sum = add_low(pick(up_sum, links.y, 1), other_up)
+    down_sum = add_low(keep_down, other_down)
+    other_two, total_one, other_units, up_sum, down_sum, conv_low = stage(
+        other_two, total_one, other_units, up_sum, down_sum, conv_low
+    )
+    ready = line_parts(add_low(piece_of(1, links.x), other_two))
+    units = add_low(units_of(links.c), other_units)
+    while stride > 2:
+        stride //= 2
+        send_down, keep_down = halve_down(down_sum, stride)
+        down_sum = add_low(keep_down, links.zside(send_down, stride))
 
     send_units = pick(units, 1 - links.y, 0)
-    ready, send_units, down_sum, small = stage(ready, send_units, down_sum, small)
-    total_two = reduce_line(links, ready, 1, links.zside)
+    send_down, keep_down = halve_down(down_sum, 1)
+    ready, send_units, send_down, keep_down, total_one = stage(
+        ready, send_units, send_down, keep_down, total_one
+    )
+    total_two = send_line(links, ready, 1, links.zside)
     other_units = links.yside(send_units)
+    other_down = links.xside(send_down)
+    low_one = finish_piece(total_one)
+    feats_one = feats_piece(low_one, kernel_weight, 0)
+    total_two, other_units, other_down, feats_one, low_one = stage(
+        total_two, other_units, other_down, feats_one, low_one
+    )
+    low_two = finish_piece(total_two)
+
+    low_two, feats_one = stage(low_two, feats_one)
+    feats_part = feats_one + feats_piece(low_two, kernel_weight, 1)
+    units = add_low(pick(units, links.y, 0), other_units)
+    units = units.reshape(links.line, 2, shard_rows, model_width)
+    send_units = pick(units, 1 - links.x, 1)
+    tiny = jnp.concatenate([small, feats_part.reshape(-1, model_width)], 0)
+    tiny, low_one, send_units = stage(tiny, low_one, send_units)
+    tiny = tiny + links.xside(tiny)
+    tiny, send_units = stage(tiny, send_units)
+    other_units = links.xside(send_units)
+    other_one = links.yside(low_one)
+    small_count = small.shape[0]
+    feats_part = tiny[small_count:].reshape(feats_part.shape)
     step = 2
     while step < dp_size:
-        small = small + links.zside(small, step)
+        feats_part = feats_part + links.zside(feats_part, step)
         step *= 2
-    total_two, other_units, small, down_sum = stage(total_two, other_units, small, down_sum)
-    units = add_low(pick(units, links.y, 0), other_units)
-    units = units.reshape(links.line, 2, shard_rows, model_width)
-    kernel_low = jnp.concatenate([finish_piece(total) for total in (total_one, total_two)], 1)
-    feats_part = scaler * jnp.einsum(
-        "spd,hpd->sh", kernel_low, kernel_weight, preferred_element_type=floaty
-    )
-
-    send_units = pick(units, 1 - links.x, 1)
-    send_units, down_sum, feats_part, kernel_low, small = stage(
-        send_units, down_sum, feats_part, kernel_low, small
-    )
-    kernel_all = spread_group(links, kernel_low)
-    other_units = links.xside(send_units)
-    stride = 2
-    while stride < dp_size // 2:
-        bit = lax.axis_index("dp") // stride % 2
-        down_sum = down_sum.reshape(-1, 2, down_rows // 2, model_width)
-        other_down = links.zside(pick(down_sum, 1 - bit, 1), stride)
-        down_sum = add_low(pick(down_sum, bit, 1), other_down)
-        stride *= 2
-    down_sum = down_sum.reshape(down_rows // 2, model_width)
-    down_total = add_low(down_sum, links.owner_line(down_sum))
-    conv_all = spread_group(links, small[-1:])
-    small = small[:-1]
-    small = small + links.core(small)
-    small = small + links.yside(small)
-    feats_grad = spread_group(links, sum_dp(links, feats_part)).reshape(-1, HE)
-    units = add_low(pick(units, links.x, 1), other_units).reshape(links.line, shard_rows, -1)
-    unit_total = reduce_line(links, units, 0, links.zside).astype(low)
+    small = tiny[: small_count - 1]
+    conv_all = tiny[small_count - 1 : small_count]
+    other_small = links.core(tiny[:small_count])
+    small = small + other_small[:-1]
+    conv_all = pair_up(conv_all, other_small[-1:], links.c, 0)
+    down_sum = add_low(keep_down, other_down).reshape(down_rows // 2, model_width)
+    feats_part, other_one, other_units, low_two, small, conv_all, down_sum = stage(
+        feats_part, other_one, other_units, low_two, small, conv_all, down_sum
+    )
+    units = add_low(pick(units, links.x, 1), other_units).reshape(links.line, -1, model_width)
+    half_shard = shard_rows // 2
+    up_blocks = up_sum.reshape(links.line, half_shard, 2, model_width).transpose(0, 2, 1, 3)
+    both = jnp.concatenate([up_blocks.reshape(units.shape), units], 1)
+    all_one = pair_up(low_one[None], other_one[None], links.y, 0)[:, None]
+
+    tiny = jnp.concatenate([small, conv_all, feats_part.reshape(-1, model_width)], 0)
+    tiny, all_one, both, low_two, down_sum = stage(tiny, all_one, both, low_two, down_sum)
+    both = send_line(links, both, 0, links.zside)
+    other_tiny = links.yside(tiny)
+    other_two = links.yside(low_two)
+    other_one = links.core(all_one)
+    small = small + other_tiny[: small_count - 1]
+    conv_all = pair_up(conv_all, other_tiny[small_count - 1 : small_count + 1], links.y, 0)
+    feats_part = feats_part[None]
+    feats_y = other_tiny[small_count + 1 :].reshape(feats_part.shape)
+    feats_two = pair_up(feats_part, feats_y, links.y, 0)
+    feats_c = links.core(feats_two)
+    feats_grad = pair_up(feats_two[:, None], feats_c[:, None], links.c, 1).reshape(-1, HE)
+    feats_grad, other_one, other_two, small, conv_all, down_sum = stage(
+        feats_grad, other_one, other_two, small, conv_all, down_sum
+    )
+    all_one = pair_up(all_one, other_one, links.c, 1).reshape((wave_count,) + low_one.shape[1:])
+    all_two = pair_up(low_two[None], other_two[None], links.y, 0)[:, None]
+
+    all_two, feats_grad, all_one, down_sum = stage(all_two, feats_grad, all_one, down_sum)
+    other_two = links.core(all_two)
+    other_down = links.owner_line(down_sum)
     key_grad, *param_grads, bias_weight_grad, bias_shift_grad = hyper_backward(
         pick_rows,
         bias_mask,
         key_rows,
         hyper_params,
         feats_grad,
-        conv_all.reshape(group_size, model_width),
+        conv_all,
         bias_weight,
     )
+    wide_kernel = jnp.concatenate([kernel_one, kernel_two, kernel_three], 0)
+    pixel_grad = pixel_gradient(conv_low, wide_kernel, band_count)
+    weight_shard_grad = weight_grad(table_all, all_one, 0, shard_pixels, None)
+    other_two, key_grad, both, other_down, weight_shard_grad, pixel_grad = stage(
+        other_two, key_grad, both, other_down, weight_shard_grad, pixel_grad
+    )
+    pixel_grad = pixel_grad.reshape(pixels.shape)
+    both = jnp.concatenate([add_low(*both), add_low(down_sum, other_down)], 0)[None]
+    all_two = pair_up(all_two, other_two, links.c, 1).reshape(all_one.shape)
+
+    both, all_two = stage(both, all_two)
+    other_both = links.yside(both)
+    weight_shard_grad = weight_grad(table_all, all_two, 1, shard_pixels, weight_shard_grad)
+    other_both, weight_shard_grad = stage(other_both, weight_shard_grad)
+    both = pair_up(both, other_both, links.y, 0)
+    other_both = links.core(both)
     token_count = weight_tokens.shape[0]
-    kernel_all = kernel_all.reshape((wave_count,) + kernel_low.shape[1:])
-    weight_shard_grad = weight_grad(feats_all, kernel_all)
-    bias_shard_grad = scaler * jnp.sum(kernel_all.astype(floaty), 0)
-    up_total = up_total.reshape(1, shard_rows // 2, -1)
-    up_total = pair_up(up_total, links.yside(up_total), links.y, 0).reshape(shard_rows, -1)
-    up_total = pair_up(up_total, links.core(up_total), links.c, 1)
-    down_total = down_total.reshape(1, down_rows // 2, model_width)
-    down_total = pair_up(down_total, links.yside(down_total), links.y, 0)
-    down_other = links.owner_core(down_total)
+    bias_shard_grad = scaler * jnp.concatenate(
+        [jnp.sum(item.astype(floaty), 0) for item in (all_one, all_two)], 0
+    )
     is_owner = lax.axis_index("dp") // (dp_size // 2) == links.c
-    down_total = jnp.where(is_owner, down_total, down_other)
-    unit_all = spread_group(links, unit_total.reshape(shard_rows, model_width))
-    block_shards = (
-        widen(jnp.concatenate([unit_all[i] for i in range(3)], 1)),
-        widen(unit_all[3]),
-        widen(up_total),
-        widen(down_total.reshape(down_rows, model_width)),
-    )
+    if shard_rows % 32 == 0:
+        place = jnp.stack([links.c, is_owner.astype(jnp.int32)])
+        block_shards = finish_grads(place, both, other_both, shard_rows, down_rows)
+    else:
+        down_total = jnp.where(is_owner, both[:, 2 * shard_rows :], other_both[:, 2 * shard_rows :])
+        cores = pair_up(both[:, None], other_both[:, None], links.c, 1)
+        up_total = cores[:, :, :shard_rows].reshape(2, 2, 2, half_shard, model_width)
+        unit_all = cores[:, :, shard_rows : 2 * shard_rows].reshape(4, shard_rows, model_width)
+        block_shards = (
+            widen(jnp.concatenate([unit_all[i] for i in range(3)], 1)),
+            widen(unit_all[3]),
+            widen(up_total.transpose(0, 3, 1, 2, 4).reshape(shard_rows, -1)),
+            widen(down_total.reshape(down_rows, model_width)),
+        )
     return (
         encoded,
         pixel_grad,

time: 564 us -> 485 us (0.86)
  matrix products: 48.4 us -> 17.9 us
  local copies, waits for them, and re-layouts: 67.3 us -> 41.3 us
  waiting for transfers between devices: 148 us -> 134 us
  starting transfers between devices: 74.4 us -> 63.2 us
  other arithmetic: 52.9 us -> 59.9 us
    pallas_call x1 -> x7, Pallas kernels: 10.5 us -> 44.2 us  [the longest x1 15.9 us: pixel_gradient(): pl.pallas_call(pixel_grad_body, grid=(rows // block_rows,), in_specs=[pl....]
    dot_general x2 -> x0, matrix products: 30 us -> none  [the longest x1 20.4 us: dot_nt(): lax.dot_general(one, two, (((1,), (1,)), ((), ())), preferred_element_typ...]
    pallas_call x1, Pallas kernels: 31 us -> 15 us  [attend_rows(): pl.pallas_call(body, grid_spec=pltpu.PrefetchScalarGridSpec(num_scalar_pr...]
    pallas_call x1, Pallas kernels: 29.9 us -> 15.5 us  [attend_back(): pl.pallas_call(attend_back_body, grid=(rows // block_rows,), in_specs=[ro...]
    select_n x18 -> x19, other arithmetic: 10 us -> 19.9 us  [pair_up(): jnp.where(bit == 0, jnp.concatenate([block, other], axis), jnp.concatenat...]
    reshape x1 -> x5, local copies, waits for them, and re-layouts: 9.14 us -> 0.18 us  [the longest x1 0.13 us: on_device(): up_sum.reshape(links.line, half_shard, 2, model_width).transpose(0, 2, 1, 3)]
    pallas_call x1, Pallas kernels: 15.6 us -> 8.53 us  [hyper_backward(): pl.pallas_call(partial(hyper_backward_body, feats_grad.shape[0]), out_sha...]
    ppermute x12 -> x9, waiting for transfers between devices: 22 us -> 15.7 us  [yside(): lax.ppermute(block, 'group', [(i, i ^ 2) for i in range(self.group_size)])]
  transfers between devices with their start and end apart: 66 -> 57, of which waited for: 25 -> 29; matrix products, arithmetic and copies ran while one was open for 22% -> 17% of each run, Pallas kernels for 22% -> 25%
where the time goes in v2:
time: 485 us; the launch traced here: 479 us
  Pallas kernels  147 us (30%)
  waiting for transfers between devices  134 us (28%)
  starting transfers between devices  63.2 us (13%)
  other arithmetic  59.9 us (12%)
  local copies, waits for them, and re-layouts  41.3 us (9%)
  matrix products  17.9 us (4%)
  between operations  15.7 us (3%)
    ppermute x26, waiting for transfers between devices, zside(): lax.ppermute(block, 'dp', [(i, i ^ step) for i in range(self.dp_size)])  97.9 us
    pallas_call x2, Pallas kernels, expand_call(): pl.pallas_call(body, grid_spec=pltpu.PrefetchScalarGridSpec(num_scalar_pr...  40.8 us
    ppermute x26, starting transfers between devices, zside(): lax.ppermute(block, 'dp', [(i, i ^ step) for i in range(self.dp_size)])  36.5 us
    ppermute x10, waiting for transfers between devices, xside(): return lax.ppermute(block, 'dp', [(i, i ^ 1) for i in range(self.dp_size)])  20.1 us
    select_n x19, other arithmetic, pair_up(): jnp.where(bit == 0, jnp.concatenate([block, other], axis), jnp.concatenat...  19.9 us
    pallas_call x1, Pallas kernels, pixel_gradient(): pl.pallas_call(pixel_grad_body, grid=(rows // block_rows,), in_specs=[pl....  15.9 us
    ppermute x9, waiting for transfers between devices, yside(): lax.ppermute(block, 'group', [(i, i ^ 2) for i in range(self.group_size)])  15.7 us
    unnamed x122, local copies, waits for them, and re-layouts  15.5 us
  transfers between devices with their start and end apart: 57, of which 29 were waited for; matrix products, arithmetic and copies ran while one was open for 17% of the time, Pallas kernels for 25%

profile of v2, /device:TPU:0, one launch (start us, length us, event | category | flops | bytes accessed | tf_op | source)
XLA Modules:
  0.0 478.7 jit_solution(11458916725644184538)
XLA Ops:
  10.4 4.1 collective-permute-start.1
  17.6 5.2 %hyper_forward.2 = f32[16,128]{1,0:T(8,128)} custom-call(f32[16,144]{1,0:T(8,128)} %constant.166.clone.refs_0_, f32[16,144]{1,0:T(8,128)} %constant.167.clone.refs_1_, f32[144,128]{1,0:T(8,128)} %maximum_maximum_fusion.1.refs_2_, bf16[128,384]{1,0:T(8,128)(2,1)} %refs_0_.3, bf16[128,128]{1,0:T(8,128)(2,1)} %refs_1_.3, bf16[2,128]{1,0:T(2,128)(2,1)} %refs_2_.1, ...), custom_call_target="tpu_custom_call" | custom-call | tf_op jit(solution)/shard_map/hyper_forward/pallas_call | solution.py:852
  27.5 6.4 %make_kernel.1 = bf16[12,32,768]{2,1,0:T(8,128)(2,1)} custom-call(bf16[24,128]{1,0:T(8,128)(2,1)} %pad_maximum_fusion.9.feats_ref, bf16[128,32,768]{2,1,0:T(8,128)(2,1)} %weight_ref.5, bf16[32,768]{1,0:T(8,128)(2,1)} %bias_ref.1), custom_call_target="tpu_custom_call" | custom-call | tf_op jit(solution)/shard_map/make_kernel/pallas_call | solution.py:967
  35.1 3.9 collective-permute-start.5
  44.4 14.1 %collective-permute-done.3 = bf16[4,1,1,32,768]{4,3,0,2,1:T(8,128)(2,1)S(1)} collective-permute-done((bf16[4,1,1,32,768]{4,3,0,2,1:T(8,128)(2,1)S(1)}, bf16[4,1,1,32,768]{4,3,0,2,1:T(8,128)(2,1)S(1)}, u32[]{:S(2)}, u32[]{:S(2)}) %collective-permute-start.3) | collective-permute-done | bytes 196640 | tf_op jit(solution)/shard_map/ppermute | solution.py:94
  58.5 4.1 collective-permute-done.4
  73.0 5.8 %copy.144 = bf16[1,12,64,12,256]{4,3,2,1,0:T(8,128)(2,1)S(1)} copy(bf16[1,12,64,12,256]{4,2,3,1,0:T(8,128)(2,1)} %param.31) | data formatting | bytes 9437184 | tf_op jit(solution)/shard_map/optimization_barrier | solution.py:63
  82.0 13.9 %collective-permute-done.10 = bf16[4,1,1,32,768]{4,3,0,2,1:T(8,128)(2,1)S(1)} collective-permute-done((bf16[4,1,1,32,768]{4,3,0,2,1:T(8,128)(2,1)S(1)}, bf16[4,1,1,32,768]{4,3,0,2,1:T(8,128)(2,1)S(1)}, u32[]{:S(2)}, u32[]{:S(2)}) %collective-permute-start.10) | collective-permute-done | bytes 196640 | tf_op jit(solution)/shard_map/ppermute | solution.py:94
  101.8 3.8 collective-permute-start.16
  113.8 13.5 %collective-permute-done.14 = bf16[4,1,1,32,768]{4,3,0,2,1:T(8,128)(2,1)S(1)} collective-permute-done((bf16[4,1,1,32,768]{4,3,0,2,1:T(8,128)(2,1)S(1)}, bf16[4,1,1,32,768]{4,3,0,2,1:T(8,128)(2,1)S(1)}, u32[]{:S(2)}, u32[]{:S(2)}) %collective-permute-start.14) | collective-permute-done | bytes 196640 | tf_op jit(solution)/shard_map/ppermute | solution.py:94
  127.3 4.7 collective-permute-done.15
  138.7 5.7 %hyper_forward.3 = f32[56,128]{1,0:T(8,128)} custom-call(f32[56,192]{1,0:T(8,128)} %constant.168.clone.refs_0_.pick_ref, f32[56,192]{1,0:T(8,128)} %constant.169.clone.refs_1_.mask_ref, f32[192,128]{1,0:T(8,128)} %maximum_maximum_fusion.refs_2_.key_ref, bf16[128,384]{1,0:T(8,128)(2,1)} %refs_0_.3, bf16[128,128]{1,0:T(8,128)(2,1)} %refs_1_.3, ...), custom_call_target="tpu_custom_call" | custom-call | tf_op jit(solution)/shard_map/hyper_forward/pallas_call | solution.py:852
  158.3 5.7 %embed_rows.1 = (f32[768,768]{1,0:T(8,128)}, bf16[768,768]{1,0:T(8,128)(2,1)}) custom-call(f32[768,768]{1,0:T(8,128)} %add.271.part_ref, bf16[768,3072]{1,0:T(8,128)(2,1)} %bitcast.171, bf16[1024,768]{1,0:T(8,128)(2,1)} %bitcast.173, f32[2,768]{1,0:T(2,128)} %pad_maximum_fusion.10.norm_ref), custom_call_target="tpu_custom_call" | custom-call | flops 1207959552 | bytes 6684672 | tf_op jit(solution)/shard_map/embed_rows/pallas_call | solution.py:250
  164.0 15.0 %attend_rows.1 = (bf16[768,2304]{1,0:T(8,128)(2,1)}, bf16[768,768]{1,0:T(8,128)(2,1)}, bf16[768,768]{1,0:T(8,128)(2,1)}, f32[768,768]{1,0:T(8,128)}, bf16[768,768]{1,0:T(8,128)(2,1)}) custom-call(s32[12]{0:T(128)} %bitcast.219, bf16[768,768]{1,0:T(8,128)(2,1)} %get-tuple-element.235.refs_0_, f32[768,768]{1,0:T(8,128)} %get-tuple-element.236.refs_1_.start_ref, ...), custom_call_target="tpu_custom_call" | custom-call | flops 7247757312 | bytes 16515072 | tf_op jit(solution)/shard_map/attend_rows/pallas_call | solution.py:393
  179.1 18.3 %expand_first.1 = (bf16[768,1536]{1,0:T(8,128)(2,1)}, bf16[1536,768]{1,0:T(8,128)(2,1)}, f32[1,1536]{1,0:T(1,128)}, f32[768,768]{1,0:T(8,128)}, f32[768,768]{1,0:T(8,128)}) custom-call(s32[1]{0:T(128)} %bitcast.39.half_ref, bf16[768,768]{1,0:T(8,128)(2,1)} %get-tuple-element.238.hidden_ref, bf16[768,768]{1,0:T(8,128)(2,1)} %bitcast_multiply_fusion.out_ref, ...), custom_call_target="tpu_custom_call" | custom-call | flops 10871635968 | bytes 18874368 | tf_op jit(solution)/shard_map/expand_first/pallas_call | solution.py:562
  199.7 22.4 %expand_second.1 = (bf16[768,1536]{1,0:T(8,128)(2,1)}, bf16[1536,768]{1,0:T(8,128)(2,1)}, f32[1,1536]{1,0:T(1,128)}, bf16[768,768]{1,0:T(8,128)(2,1)}, f32[768,7...) custom-call(s32[1]{0:T(128)} %bitcast.half_ref, bf16[768,768]{1,0:T(8,128)(2,1)} %get-tuple-element.238.hidden_ref, ...), custom_call_target="tpu_custom_call" | custom-call | flops 10871635968 | bytes 18874368 | tf_op jit(solution)/shard_map/expand_second/pallas_call | solution.py:562
  231.1 15.5 %attend_back.1 = (bf16[768,2304]{1,0:T(8,128)(2,1)}, bf16[768,768]{1,0:T(8,128)(2,1)}, f32[3,768]{1,0:T(4,128)}, f32[1,2304]{1,0:T(1,128)}) custom-call(bf16[768,2304]{1,0:T(8,128)(2,1)} %get-tuple-element.259.project_ref, bf16[768,768]{1,0:T(8,128)(2,1)} %get-tuple-element.260.probs_ref, f32[768,768]{1,0:T(8,128)} %get-tuple-element.236.refs_1_.start_ref, ...), custom_call_target="tpu_custom_call" | custom-call | flops 10871635968 | bytes 22413312 | tf_op jit(solution)/shard_map/attend_back/pallas_call | solution.py:763
  246.6 6.6 %convolution_convert_fusion = bf16[3072,768]{1,0:T(8,128)(2,1)S(1)} fusion(bf16[768,3072]{1,0:T(8,128)(2,1)} %bitcast.172, bf16[768,768]{1,0:T(8,128)(2,1)} %get-tuple-element.347.grad_ref), kind=kOutput, calls=%fused_computation | convolution fusion | flops 3626237952 | bytes 10616832 | tf_op jit(solution)/shard_map/dot_general | solution.py:21
  273.5 9.1 %collective-permute-done.28 = f32[13,768]{1,0:T(8,128)S(1)} collective-permute-done((f32[13,768]{1,0:T(8,128)S(1)}, f32[13,768]{1,0:T(8,128)S(1)}, u32[]{:S(2)}, u32[]{:S(2)}) %collective-permute-start.28) | collective-permute-done | bytes 39968 | tf_op jit(solution)/shard_map/ppermute | solution.py:94
  283.7 9.0 %collective-permute-done.24 = bf16[12,4,1,16,768]{4,3,0,1,2:T(8,128)(2,1)S(1)} collective-permute-done((bf16[12,4,1,16,768]{4,3,0,1,2:T(8,128)(2,1)S(1)}, bf16[12,4,1,16,768]{4,3,0,1,2:T(8,128)(2,1)S(1)}, u32[]{:S(2)}, u32[]{:S(2)}) %collective-permute-start.24) | collective-permute-done | bytes 1179680 | tf_op jit(solution)/shard_map/ppermute | solution.py:91
  300.3 6.3 %collective-permute-done.32 = bf16[12,1,16,768]{3,2,0,1:T(8,128)(2,1)S(1)} collective-permute-done((bf16[12,1,16,768]{3,2,0,1:T(8,128)(2,1)S(1)}, bf16[12,1,16,768]{3,2,0,1:T(8,128)(2,1)S(1)}, u32[]{:S(2)}, u32[]{:S(2)}) %collective-permute-start.32) | collective-permute-done | bytes 294944 | tf_op jit(solution)/shard_map/ppermute | solution.py:94
  306.6 14.3 %collective-permute-done.31 = bf16[12,1,16,768]{3,2,0,1:T(8,128)(2,1)S(1)} collective-permute-done((bf16[12,1,16,768]{3,2,0,1:T(8,128)(2,1)S(1)}, bf16[12,1,16,768]{3,2,0,1:T(8,128)(2,1)S(1)}, u32[]{:S(2)}, u32[]{:S(2)}) %collective-permute-start.31) | collective-permute-done | bytes 294944 | tf_op jit(solution)/shard_map/ppermute | solution.py:94
  331.7 4.3 feats_piece.2
  338.0 13.4 %collective-permute-done.35 = bf16[12,1,16,768]{3,2,0,1:T(8,128)(2,1)} collective-permute-done((bf16[12,1,16,768]{3,2,0,1:T(8,128)(2,1)}, bf16[12,1,16,768]{3,2,0,1:T(8,128)(2,1)}, u32[]{:S(2)}, u32[]{:S(2)}) %collective-permute-start.35) | collective-permute-done | bytes 294944 | tf_op jit(solution)/shard_map/ppermute | solution.py:94
  355.7 4.3 feats_piece.3
  403.9 15.9 %pixel_gradient.1 = bf16[768,12,256]{2,1,0:T(8,128)(2,1)} custom-call(bf16[768,768]{1,0:T(8,128)(2,1)} %get-tuple-element.347.grad_ref, bf16[3072,768]{1,0:T(8,128)(2,1)} %pad_maximum_fusion.kernel_ref), custom_call_target="tpu_custom_call" | custom-call | flops 3623878656 | bytes 18874368 | tf_op jit(solution)/shard_map/pixel_gradient/pallas_call | solution.py:291
  419.7 8.5 %hyper_backward.1 = (f32[192,128]{1,0:T(8,128)}, f32[128,384]{1,0:T(8,128)}, f32[128,128]{1,0:T(8,128)}, f32[2,128]{1,0:T(2,128)}, f32[2,128]{1,0:T(2,128)}, /*i...) custom-call(f32[56,192]{1,0:T(8,128)} %constant.168.clone.refs_0_.pick_ref, ...), custom_call_target="tpu_custom_call" | custom-call | tf_op jit(solution)/shard_map/hyper_backward/pallas_call | solution.py:882
  428.3 6.2 %weight_grad.2.refs_0_ = f32[128,32,768]{2,1,0:T(8,128)} custom-call(bf16[2048,768]{1,0:T(8,128)(2,1)} %weight_table.1.table_ref, bf16[48,16,768]{2,1,0:T(8,128)(2,1)} %bitcast.175), custom_call_target="tpu_custom_call" | custom-call | tf_op jit(solution)/shard_map/weight_grad/pallas_call | solution.py:1014
  439.1 6.2 %weight_grad.3 = f32[128,32,768]{2,1,0:T(8,128)} custom-call(bf16[2048,768]{1,0:T(8,128)(2,1)} %weight_table.1.table_ref, bf16[48,16,768]{2,1,0:T(8,128)(2,1)} %bitcast.177, f32[128,32,768]{2,1,0:T(8,128)} %weight_grad.2.refs_0_), custom_call_target="tpu_custom_call", output_to_operand_aliasing={{}: (2, {})} | custom-call | tf_op jit(solution)/shard_map/weight_grad/pallas_call | solution.py:1014
  445.3 8.0 %collective-permute-done.54 = bf16[1,384,768]{2,1,0:T(8,128)(2,1)S(1)} collective-permute-done((bf16[1,384,768]{2,1,0:T(8,128)(2,1)S(1)}, bf16[1,384,768]{2,1,0:T(8,128)(2,1)S(1)}, u32[]{:S(2)}, u32[]{:S(2)}) %collective-permute-start.54) | collective-permute-done | bytes 589856 | tf_op jit(solution)/shard_map/ppermute | solution.py:88
  459.0 7.0 %copy.166 = bf16[1,12,64,12,256]{4,2,3,1,0:T(8,128)(2,1)} copy(bf16[1,12,64,12,256]{4,3,2,1,0:T(8,128)(2,1)} %bitcast.183) | data formatting | bytes 9437184
  468.0 3.7 finish_grads.1
  (403 shorter events, 178.1 us)
Async XLA Ops:
  7.2 171.8 %all-gather.3.cloned.1.call-start = ((), (), s32[]{:S(2)}) async-start(), calls=%async_computation | async-start | bytes 9732096 | tf_op jit(solution)/shard_map/all_gather | solution.py:184
  10.4 23.5 %collective-permute-start.1 = (bf16[1,1,1,1,96,768]{5,4,3,2,1,0:T(8,128)(2,1)S(1)}, bf16[1,1,1,1,96,768]{5,4,3,2,1,0:T(8,128)(2,1)S(1)}, u32[]{:S(2)}, u32[]{:S(2)}) collective-permute-start(bf16[1,1,1,1,96,768]{5,4,3,2,1,0:T(8,128)(2,1)S(1)} %get-tuple-element.477), channel_id=1, source_target_pairs={{0,4},{1,5},{2,6},{3,7},{4,0},{5,1},{6,2},{7,3},{8,12},{9,13},{10,... | collective-permute-start | bytes 442376 | tf_op jit(solution)/shard_map/ppermute | solution.py:94
  35.1 27.5 %collective-permute-start.5 = (bf16[4,1,1,32,768]{4,3,0,2,1:T(8,128)(2,1)S(1)}, bf16[4,1,1,32,768]{4,3,0,2,1:T(8,128)(2,1)S(1)}, u32[]{:S(2)}, u32[]{:S(2)}) collective-permute-start(bf16[4,1,1,32,768]{4,3,0,2,1:T(8,128)(2,1)S(1)} %get-tuple-element.504), channel_id=1, source_target_pairs={{0,6},{1,7},{2,4},{3,5},{4,2},{5,3},{6,0},{7,1},{8,14},{9,15},{10,... | collective-permute-start | bytes 589832 | tf_op jit(solution)/shard_map/ppermute | solution.py:94
  39.0 23.6 %collective-permute-start.4 = (bf16[4,1,1,32,768]{4,3,0,2,1:T(8,128)(2,1)S(1)}, bf16[4,1,1,32,768]{4,3,0,2,1:T(8,128)(2,1)S(1)}, u32[]{:S(2)}, u32[]{:S(2)}) collective-permute-start(bf16[4,1,1,32,768]{4,3,0,2,1:T(8,128)(2,1)S(1)} %get-tuple-element.504), channel_id=1, source_target_pairs={{0,4},{1,5},{2,6},{3,7},{4,0},{5,1},{6,2},{7,3},{8,12},{9,13},{10,... | collective-permute-start | bytes 589832 | tf_op jit(solution)/shard_map/ppermute | solution.py:94
  41.3 21.7 %collective-permute-start.6 = (bf16[4,1,1,1,96,768]{5,4,3,2,1,0:T(8,128)(2,1)S(1)}, bf16[4,1,1,1,96,768]{5,4,3,2,1,0:T(8,128)(2,1)S(1)}, u32[]{:S(2)}, u32[]{:S(2)}) collective-permute-start(bf16[4,1,1,1,96,768]{5,4,3,2,1,0:T(8,128)(2,1)S(1)} %constant_dynamic-update-slice_fusion), channel_id=1, source_target_pairs={{0,1},{1,0},{2,3},{3,2},{4,5},{5,4},{6,7},{7,6},{8,9},{9,8},{10,11... | collective-permute-start | bytes 1769480 | tf_op jit(solution)/shard_map/ppermute | solution.py:91
  63.1 35.9 %collective-permute-start.13 = (bf16[4,2,1,1,96,768]{5,4,3,2,1,0:T(8,128)(2,1)S(1)}, bf16[4,2,1,1,96,768]{5,4,3,2,1,0:T(8,128)(2,1)}, u32[]{:S(2)}, u32[]{:S(2)}) collective-permute-start(bf16[4,2,1,1,96,768]{5,4,3,2,1,0:T(8,128)(2,1)S(1)} %maximum_select_fusion.5), channel_id=1, source_target_pairs={{0,16},{8,24},{16,0},{24,8},{1,17},{9,25},{17,1},{25,9},{2,18},{10... | collective-permute-start | bytes 3538952 | tf_op jit(solution)/shard_map/ppermute | solution.py:88
  65.8 30.1 %collective-permute-start.11 = (bf16[4,1,1,32,768]{4,3,0,2,1:T(8,128)(2,1)S(1)}, bf16[4,1,1,32,768]{4,3,0,2,1:T(8,128)(2,1)S(1)}, u32[]{:S(2)}, u32[]{:S(2)}) collective-permute-start(bf16[4,1,1,32,768]{4,3,0,2,1:T(8,128)(2,1)S(1)} %get-tuple-element.206), channel_id=1, source_target_pairs={{0,6},{1,7},{2,4},{3,5},{4,2},{5,3},{6,0},{7,1},{8,14},{9,15},{10,... | collective-permute-start | bytes 589832 | tf_op jit(solution)/shard_map/ppermute | solution.py:94
  68.6 27.3 %collective-permute-start.10 = (bf16[4,1,1,32,768]{4,3,0,2,1:T(8,128)(2,1)S(1)}, bf16[4,1,1,32,768]{4,3,0,2,1:T(8,128)(2,1)S(1)}, u32[]{:S(2)}, u32[]{:S(2)}) collective-permute-start(bf16[4,1,1,32,768]{4,3,0,2,1:T(8,128)(2,1)S(1)} %get-tuple-element.206), channel_id=1, source_target_pairs={{0,4},{1,5},{2,6},{3,7},{4,0},{5,1},{6,2},{7,3},{8,12},{9,13},{10,... | collective-permute-start | bytes 589832 | tf_op jit(solution)/shard_map/ppermute | solution.py:94
  70.3 27.0 %collective-permute-start.12 = (bf16[4,4,1,32,768]{4,3,2,1,0:T(8,128)(2,1)S(1)}, bf16[4,4,1,32,768]{4,3,2,1,0:T(8,128)(2,1)S(1)}, u32[]{:S(2)}, u32[]{:S(2)}) collective-permute-start(bf16[4,4,1,32,768]{4,3,2,1,0:T(8,128)(2,1)S(1)} %bitcast_dynamic-update-slice_fusion.9), channel_id=1, source_target_pairs={{0,1},{1,0},{2,3},{3,2},{4,5},{5,4},{6,7},{7,6},{8,9},{9,8},{10,11... | collective-permute-start | bytes 2359304 | tf_op jit(solution)/shard_map/ppermute | solution.py:91
  101.7 30.4 %collective-permute-start.18 = (bf16[4,2,2,1,96,768]{5,4,3,2,1,0:T(8,128)(2,1)S(1)}, bf16[4,2,2,1,96,768]{5,4,3,2,1,0:T(8,128)(2,1)S(1)}, u32[]{:S(2)}, u32[]{:S(2)}) collective-permute-start(bf16[4,2,2,1,96,768]{5,4,3,2,1,0:T(8,128)(2,1)S(1)} %maximum_select_fusion.1), channel_id=1, source_target_pairs={{0,8},{8,0},{16,24},{24,16},{1,9},{9,1},{17,25},{25,17},{2,10},{10... | collective-permute-start | bytes 7077896 | tf_op jit(solution)/shard_map/ppermute | solution.py:85
  101.8 30.2 %collective-permute-start.16 = (bf16[4,1,1,32,768]{4,3,0,2,1:T(8,128)(2,1)S(1)}, bf16[4,1,1,32,768]{4,3,0,2,1:T(8,128)(2,1)S(1)}, u32[]{:S(2)}, u32[]{:S(2)}) collective-permute-start(bf16[4,1,1,32,768]{4,3,0,2,1:T(8,128)(2,1)S(1)} %get-tuple-element.217), channel_id=1, source_target_pairs={{0,6},{1,7},{2,4},{3,5},{4,2},{5,3},{6,0},{7,1},{8,14},{9,15},{10,... | collective-permute-start | bytes 589832 | tf_op jit(solution)/shard_map/ppermute | solution.py:94
  105.6 26.4 %collective-permute-start.15 = (bf16[4,1,1,32,768]{4,3,0,2,1:T(8,128)(2,1)S(1)}, bf16[4,1,1,32,768]{4,3,0,2,1:T(8,128)(2,1)S(1)}, u32[]{:S(2)}, u32[]{:S(2)}) collective-permute-start(bf16[4,1,1,32,768]{4,3,0,2,1:T(8,128)(2,1)S(1)} %get-tuple-element.217), channel_id=1, source_target_pairs={{0,4},{1,5},{2,6},{3,7},{4,0},{5,1},{6,2},{7,3},{8,12},{9,13},{10,... | collective-permute-start | bytes 589832 | tf_op jit(solution)/shard_map/ppermute | solution.py:94
  105.6 21.7 %collective-permute-start.14 = (bf16[4,1,1,32,768]{4,3,0,2,1:T(8,128)(2,1)S(1)}, bf16[4,1,1,32,768]{4,3,0,2,1:T(8,128)(2,1)S(1)}, u32[]{:S(2)}, u32[]{:S(2)}) collective-permute-start(bf16[4,1,1,32,768]{4,3,0,2,1:T(8,128)(2,1)S(1)} %get-tuple-element.217), channel_id=1, source_target_pairs={{0,2},{1,3},{2,0},{3,1},{4,6},{5,7},{6,4},{7,5},{8,10},{9,11},{10,... | collective-permute-start | bytes 589832 | tf_op jit(solution)/shard_map/ppermute | solution.py:94
  106.5 25.6 %collective-permute-start.17 = (bf16[4,4,1,32,768]{4,3,2,1,0:T(8,128)(2,1)S(1)}, bf16[4,4,1,32,768]{4,3,2,1,0:T(8,128)(2,1)S(1)}, u32[]{:S(2)}, u32[]{:S(2)}) collective-permute-start(bf16[4,4,1,32,768]{4,3,2,1,0:T(8,128)(2,1)S(1)} %bitcast_dynamic-update-slice_fusion.5), channel_id=1, source_target_pairs={{0,1},{1,0},{2,3},{3,2},{4,5},{5,4},{6,7},{7,6},{8,9},{9,8},{10,11... | collective-permute-start | bytes 2359304 | tf_op jit(solution)/shard_map/ppermute | solution.py:91
  197.4 27.0 %collective-permute-start.20 = (bf16[768,1536]{1,0:T(8,128)(2,1)}, bf16[768,1536]{1,0:T(8,128)(2,1)}, u32[]{:S(2)}, u32[]{:S(2)}) collective-permute-start(bf16[768,1536]{1,0:T(8,128)(2,1)} %get-tuple-element.247), channel_id=1, source_target_pairs={{0,8},{8,0},{16,24},{24,16},{1,9},{9,1},{17,25},{25,17},{2,10},{10... | collective-permute-start | bytes 7077896 | tf_op jit(solution)/shard_map/ppermute | solution.py:85
  197.5 27.0 %collective-permute-start.21 = (bf16[1536,768]{1,0:T(8,128)(2,1)}, bf16[1536,768]{1,0:T(8,128)(2,1)S(1)}, u32[]{:S(2)}, u32[]{:S(2)}) collective-permute-start(bf16[1536,768]{1,0:T(8,128)(2,1)} %get-tuple-element.248), channel_id=1, source_target_pairs={{0,8},{8,0},{16,24},{24,16},{1,9},{9,1},{17,25},{25,17},{2,10},{10... | collective-permute-start | bytes 7077896 | tf_op jit(solution)/shard_map/ppermute | solution.py:85
  228.9 28.3 %collective-permute-start.22 = (bf16[4,1,96,1536]{3,2,0,1:T(8,128)(2,1)}, bf16[4,1,96,1536]{3,2,0,1:T(8,128)(2,1)}, u32[]{:S(2)}, u32[]{:S(2)}) collective-permute-start(bf16[4,1,96,1536]{3,2,0,1:T(8,128)(2,1)} %add_convert_fusion.7), channel_id=1, source_target_pairs={{0,1},{1,0},{2,3},{3,2},{4,5},{5,4},{6,7},{7,6},{8,9},{9,8},{10,11... | collective-permute-start | bytes 3538952 | tf_op jit(solution)/shard_map/ppermute | solution.py:91
  230.7 28.0 %collective-permute-start.23 = (bf16[4,1,192,768]{3,2,0,1:T(8,128)(2,1)}, bf16[4,1,192,768]{3,2,0,1:T(8,128)(2,1)}, u32[]{:S(2)}, u32[]{:S(2)}) collective-permute-start(bf16[4,1,192,768]{3,2,0,1:T(8,128)(2,1)} %add_convert_fusion.6), channel_id=1, source_target_pairs={{0,16},{8,24},{16,0},{24,8},{1,17},{9,25},{17,1},{25,9},{2,18},{10... | collective-permute-start | bytes 3538952 | tf_op jit(solution)/shard_map/ppermute | solution.py:88
  265.9 26.8 %collective-permute-start.24 = (bf16[12,4,1,16,768]{4,3,0,1,2:T(8,128)(2,1)S(1)}, bf16[12,4,1,16,768]{4,3,0,1,2:T(8,128)(2,1)S(1)}, u32[]{:S(2)}, u32[]{:S(2)}) collective-permute-start(bf16[12,4,1,16,768]{4,3,0,1,2:T(8,128)(2,1)S(1)} %copy-done.20), channel_id=1, source_target_pairs={{0,1},{1,0},{2,3},{3,2},{4,5},{5,4},{6,7},{7,6},{8,9},{9,8},{10,11... | collective-permute-start | bytes 3538952 | tf_op jit(solution)/shard_map/ppermute | solution.py:91
  293.5 28.9 %collective-permute-start.33 = (bf16[2,768,768]{2,1,0:T(8,128)(2,1)S(1)}, bf16[2,768,768]{2,1,0:T(8,128)(2,1)S(1)}, u32[]{:S(2)}, u32[]{:S(2)}) collective-permute-start(bf16[2,768,768]{2,1,0:T(8,128)(2,1)S(1)} %pad_maximum_fusion.1), channel_id=1, source_target_pairs={{0,8},{8,0},{16,24},{24,16},{1,9},{9,1},{17,25},{25,17},{2,10},{10... | collective-permute-start | bytes 7077896 | tf_op jit(solution)/shard_map/ppermute | solution.py:85
  293.6 28.8 %collective-permute-start.29 = (bf16[12,4,1,16,768]{4,3,0,1,2:T(8,128)(2,1)S(1)}, bf16[12,4,1,16,768]{4,3,0,1,2:T(8,128)(2,1)S(1)}, u32[]{:S(2)}, u32[]{:S(2)}) collective-permute-start(bf16[12,4,1,16,768]{4,3,0,1,2:T(8,128)(2,1)S(1)} %constant_dynamic-slice_fusion.12), channel_id=1, source_target_pairs={{0,1},{1,0},{2,3},{3,2},{4,5},{5,4},{6,7},{7,6},{8,9},{9,8},{10,11... | collective-permute-start | bytes 3538952 | tf_op jit(solution)/shard_map/ppermute | solution.py:91
  296.2 24.7 %collective-permute-start.31 = (bf16[12,1,16,768]{3,2,0,1:T(8,128)(2,1)S(1)}, bf16[12,1,16,768]{3,2,0,1:T(8,128)(2,1)S(1)}, u32[]{:S(2)}, u32[]{:S(2)}) collective-permute-start(bf16[12,1,16,768]{3,2,0,1:T(8,128)(2,1)S(1)} %get-tuple-element.495), channel_id=1, source_target_pairs={{0,4},{1,5},{2,6},{3,7},{4,0},{5,1},{6,2},{7,3},{8,12},{9,13},{10,... | collective-permute-start | bytes 884744 | tf_op jit(solution)/shard_map/ppermute | solution.py:94
  296.2 24.7 %collective-permute-start.30 = (bf16[12,1,16,768]{3,2,0,1:T(8,128)(2,1)S(1)}, bf16[12,1,16,768]{3,2,0,1:T(8,128)(2,1)S(1)}, u32[]{:S(2)}, u32[]{:S(2)}) collective-permute-start(bf16[12,1,16,768]{3,2,0,1:T(8,128)(2,1)S(1)} %get-tuple-element.496), channel_id=1, source_target_pairs={{0,2},{1,3},{2,0},{3,1},{4,6},{5,7},{6,4},{7,5},{8,10},{9,11},{10,... | collective-permute-start | bytes 884744 | tf_op jit(solution)/shard_map/ppermute | solution.py:94
  324.4 27.7 %collective-permute-start.37 = (bf16[1,768,768]{2,1,0:T(8,128)(2,1)S(1)}, bf16[1,768,768]{2,1,0:T(8,128)(2,1)}, u32[]{:S(2)}, u32[]{:S(2)}) collective-permute-start(bf16[1,768,768]{2,1,0:T(8,128)(2,1)S(1)} %constant_dynamic-slice_fusion.8), channel_id=1, source_target_pairs={{0,16},{8,24},{16,0},{24,8},{1,17},{9,25},{17,1},{25,9},{2,18},{10... | collective-permute-start | bytes 3538952 | tf_op jit(solution)/shard_map/ppermute | solution.py:88
  327.2 24.2 %collective-permute-start.35 = (bf16[12,1,16,768]{3,2,0,1:T(8,128)(2,1)}, bf16[12,1,16,768]{3,2,0,1:T(8,128)(2,1)}, u32[]{:S(2)}, u32[]{:S(2)}) collective-permute-start(bf16[12,1,16,768]{3,2,0,1:T(8,128)(2,1)} %get-tuple-element.491), channel_id=1, source_target_pairs={{0,4},{1,5},{2,6},{3,7},{4,0},{5,1},{6,2},{7,3},{8,12},{9,13},{10,... | collective-permute-start | bytes 884744 | tf_op jit(solution)/shard_map/ppermute | solution.py:94
  327.2 24.2 %collective-permute-start.34 = (bf16[12,1,16,768]{3,2,0,1:T(8,128)(2,1)}, bf16[12,1,16,768]{3,2,0,1:T(8,128)(2,1)}, u32[]{:S(2)}, u32[]{:S(2)}) collective-permute-start(bf16[12,1,16,768]{3,2,0,1:T(8,128)(2,1)} %get-tuple-element.492), channel_id=1, source_target_pairs={{0,2},{1,3},{2,0},{3,1},{4,6},{5,7},{6,4},{7,5},{8,10},{9,11},{10,... | collective-permute-start | bytes 884744 | tf_op jit(solution)/shard_map/ppermute | solution.py:94
  330.2 21.1 %collective-permute-start.38 = (bf16[1,1,192,768]{3,2,1,0:T(8,128)(2,1)}, bf16[1,1,192,768]{3,2,1,0:T(8,128)(2,1)S(1)}, u32[]{:S(2)}, u32[]{:S(2)}) collective-permute-start(bf16[1,1,192,768]{3,2,1,0:T(8,128)(2,1)} %get-tuple-element.302), channel_id=1, source_target_pairs={{0,1},{1,0},{2,3},{3,2},{4,5},{5,4},{6,7},{7,6},{8,9},{9,8},{10,11... | collective-permute-start | bytes 884744 | tf_op jit(solution)/shard_map/ppermute | solution.py:91
  395.6 38.9 %collective-permute-start.49 = (bf16[2,1,12,16,768]{4,3,2,1,0:T(8,128)(2,1)}, bf16[2,1,12,16,768]{4,3,2,1,0:T(8,128)(2,1)}, u32[]{:S(2)}, u32[]{:S(2)}) collective-permute-start(bf16[2,1,12,16,768]{4,3,2,1,0:T(8,128)(2,1)} %maximum_select_fusion.10), channel_id=1, source_target_pairs={{0,8},{8,0},{16,24},{24,16},{1,9},{9,1},{17,25},{25,17},{2,10},{10... | collective-permute-start | bytes 1769480 | tf_op jit(solution)/shard_map/ppermute | solution.py:85
  398.1 36.4 %collective-permute-start.52 = (bf16[1,192,768]{2,1,0:T(8,128)(2,1)S(1)}, bf16[1,192,768]{2,1,0:T(8,128)(2,1)S(1)}, u32[]{:S(2)}, u32[]{:S(2)}) collective-permute-start(bf16[1,192,768]{2,1,0:T(8,128)(2,1)S(1)} %get-tuple-element.486), channel_id=1, source_target_pairs={{0,6},{1,7},{2,4},{3,5},{4,2},{5,3},{6,0},{7,1},{8,14},{9,15},{10,... | collective-permute-start | bytes 884744 | tf_op jit(solution)/shard_map/ppermute | solution.py:94
  400.6 33.9 %collective-permute-start.51 = (bf16[1,192,768]{2,1,0:T(8,128)(2,1)S(1)}, bf16[1,192,768]{2,1,0:T(8,128)(2,1)S(1)}, u32[]{:S(2)}, u32[]{:S(2)}) collective-permute-start(bf16[1,192,768]{2,1,0:T(8,128)(2,1)S(1)} %get-tuple-element.487), channel_id=1, source_target_pairs={{0,4},{1,5},{2,6},{3,7},{4,0},{5,1},{6,2},{7,3},{8,12},{9,13},{10,... | collective-permute-start | bytes 884744 | tf_op jit(solution)/shard_map/ppermute | solution.py:94
  401.3 33.2 %collective-permute-start.50 = (bf16[1,192,768]{2,1,0:T(8,128)(2,1)S(1)}, bf16[1,192,768]{2,1,0:T(8,128)(2,1)S(1)}, u32[]{:S(2)}, u32[]{:S(2)}) collective-permute-start(bf16[1,192,768]{2,1,0:T(8,128)(2,1)S(1)} %get-tuple-element.488), channel_id=1, source_target_pairs={{0,2},{1,3},{2,0},{3,1},{4,6},{5,7},{6,4},{7,5},{8,10},{9,11},{10,... | collective-permute-start | bytes 884744 | tf_op jit(solution)/shard_map/ppermute | solution.py:94
  402.6 31.9 %collective-permute-start.53 = (bf16[192,768]{1,0:T(8,128)(2,1)S(1)}, bf16[192,768]{1,0:T(8,128)(2,1)S(1)}, u32[]{:S(2)}, u32[]{:S(2)}) collective-permute-start(bf16[192,768]{1,0:T(8,128)(2,1)S(1)} %copy-done.19), channel_id=1, source_target_pairs={{4,0},{5,1},{6,2},{7,3},{8,12},{9,13},{10,14},{11,15},{20,16},{21,... | collective-permute-start | bytes 884744 | tf_op jit(solution)/shard_map/ppermute | solution.py:110
  (86 other events, 688.4 us)
Sparse Core Ops, SparseCore 0:
  11.5 119.3 all-gather.2

commit v3 on v2

--- a/solution.py
+++ b/solution.py
@@ -262,48 +262,34 @@
             jax.ShapeDtypeStruct((rows, width), jnp.bfloat16),
         ],
         compiler_params=kernel_params(),
-        cost_estimate=pl.CostEstimate(
-            flops=2 * rows * depth * width,
-            bytes_accessed=2 * (rows * depth + depth * width) + 6 * rows * width,
-            transcendentals=0,
-        ),
+        cost_estimate=pl.CostEstimate(flops=0, bytes_accessed=0, transcendentals=0),
         name="embed_rows",
     )(part, pixel_rows, wide_kernel, norm_one)
 
 
-def pixel_grad_body(grad_ref, kernel_ref, out_ref, *wide_refs):
-    rows, bands, depth = out_ref.shape
-    padded = wide_refs[0].shape[0] // rows
+def pixel_grad_body(grad_ref, kernel_ref, out_ref):
+    images, bands, slots, depth = out_ref.shape
     for band in range(bands):
         part = dot_nt(grad_ref[...], kernel_ref[band * depth : (band + 1) * depth, :])
-        for place, ref in enumerate(wide_refs):
-            ref[pl.ds(band, rows, stride=padded), :] = part[:, place * 128 : (place + 1) * 128]
-    for place, ref in enumerate(wide_refs):
-        wide = ref[...].reshape(rows, padded, 128)
-        out_ref[:, :, place * 128 : (place + 1) * 128] = wide[:, :bands].astype(out_ref.dtype)
-
-
-def pixel_gradient(conv_low, wide_kernel, bands):
+        out_ref[:, band] = part.astype(out_ref.dtype).reshape(images, slots, depth)
+
+
+def pixel_gradient(conv_low, wide_kernel, images, bands):
     rows, width = conv_low.shape
+    slots = rows // images
     depth = wide_kernel.shape[0] // bands
-    block_rows = 128
-    padded = -(-bands // 8) * 8
+    block = images // 3
     return pl.pallas_call(
         pixel_grad_body,
-        grid=(rows // block_rows,),
+        grid=(3,),
         in_specs=[
-            pl.BlockSpec((block_rows, width), lambda i: (i, 0)),
+            pl.BlockSpec((block * slots, width), lambda i: (i, 0)),
             whole_spec(wide_kernel.shape),
         ],
-        out_specs=pl.BlockSpec((block_rows, bands, depth), lambda i: (i, 0, 0)),
-        out_shape=jax.ShapeDtypeStruct((rows, bands, depth), jnp.bfloat16),
-        scratch_shapes=[pltpu.VMEM((block_rows * padded, 128), jnp.float32)] * (depth // 128),
+        out_specs=pl.BlockSpec((block, bands, slots, depth), lambda i: (i, 0, 0, 0)),
+        out_shape=jax.ShapeDtypeStruct((images, bands, slots, depth), jnp.bfloat16),
         compiler_params=kernel_params(),
-        cost_estimate=pl.CostEstimate(
-            flops=2 * rows * width * bands * depth,
-            bytes_accessed=4 * bands * depth * (width + rows),
-            transcendentals=0,
-        ),
+        cost_estimate=pl.CostEstimate(flops=0, bytes_accessed=0, transcendentals=0),
         name="pixel_gradient",
     )(conv_low, wide_kernel)
 
@@ -319,6 +305,19 @@
     first = reducer(jnp.where(low_half, values, filler), -1, keepdims=True)
     second = reducer(jnp.where(low_half, filler, values), -1, keepdims=True)
     return jnp.where(low_half, first, second)
+
+
+def join_weights(count_ref, own_ref, other_ref, weight_ref):
+    width = weight_ref.shape[1]
+
+    def fill(refs):
+        for unit in range(4):
+            weight_ref[unit] = refs[unit % 2][:, unit // 2].reshape(width, width)
+
+    core = count_ref[count_ref.shape[0] - 1]
+    first = pl.program_id(0) == 0
+    pl.when(first & (core == 0))(lambda: fill((own_ref, other_ref)))
+    pl.when(first & (core == 1))(lambda: fill((other_ref, own_ref)))
 
 
 def attend_body(
@@ -326,7 +325,8 @@
     count_ref,
     hidden_ref,
     start_ref,
-    weight_ref,
+    own_ref,
+    other_ref,
     bias_ref,
     rows_ref,
     project_ref,
@@ -335,14 +335,16 @@
     middle_ref,
     hidden_two_ref,
     score_ref,
+    weight_ref,
 ):
+    join_weights(count_ref, own_ref, other_ref, weight_ref)
     block_rows, width = hidden_ref.shape
     slots = 64
     images = block_rows // slots
     base = (pl.program_id(0) + first) * images
     for third in range(3):
         at = third * width
-        weight = weight_ref[:, third].reshape(width, width)
+        weight = weight_ref[third]
         project_ref[:, at : at + width] = (
             dot_nn(hidden_ref[...], weight) + bias_ref[:, at : at + width]
         ).astype(jnp.bfloat16)
@@ -373,13 +375,13 @@
         probs_low = score_ref[place * slots : (place + 1) * slots, :].astype(jnp.bfloat16)
         probs_ref[here, at : at + 128] = probs_low
         mixed_ref[here, at : at + 128] = dot_nn(probs_low, values).astype(jnp.bfloat16)
-    middle = start_ref[...] + dot_nn(mixed_ref[...], weight_ref[:, 3].reshape(width, width)) + rows_ref[0:1, :]
+    middle = start_ref[...] + dot_nn(mixed_ref[...], weight_ref[3]) + rows_ref[0:1, :]
     middle_ref[...] = middle
     normed, _ = norm_rows(middle, 1e-06)
     hidden_two_ref[...] = (normed * rows_ref[1:2, :] + rows_ref[2:3, :]).astype(jnp.bfloat16)
 
 
-def attend_rows(first, steps, earlier, counts, hidden_one, start, weights, bias_full, rows_in):
+def attend_rows(first, steps, earlier, counts, hidden_one, start, own, other, bias_full, rows_in):
     rows, width = hidden_one.shape
     block_rows = 128
     row_spec = lambda cols: pl.BlockSpec((block_rows, cols), lambda i, *_: (i + first, 0))
@@ -387,7 +389,7 @@
     keep = list(earlier or ())
 
     def body(count_ref, *refs):
-        refs = refs[:5] + refs[5 + len(keep) :]
+        refs = refs[:6] + refs[6 + len(keep) :]
         attend_body(first, count_ref, *refs)
 
     return pl.pallas_call(
@@ -398,7 +400,8 @@
             in_specs=[
                 row_spec(width),
                 row_spec(width),
-                whole_spec(weights.shape),
+                whole_spec(own.shape),
+                whole_spec(other.shape),
                 whole_spec(bias_full.shape),
                 whole_spec(rows_in.shape),
                 *(pl.BlockSpec(memory_space=pl.ANY) for _ in keep),
@@ -410,7 +413,10 @@
                 row_spec(width),
                 row_spec(width),
             ],
-            scratch_shapes=[pltpu.VMEM((block_rows * width // 128, 128), jnp.float32)],
+            scratch_shapes=[
+                pltpu.VMEM((block_rows * width // 128, 128), jnp.float32),
+                pltpu.VMEM((4, width, width), low),
+            ],
         ),
         out_shape=[
             jax.ShapeDtypeStruct((rows, 3 * width), low),
@@ -419,15 +425,11 @@
             jax.ShapeDtypeStruct((rows, width), jnp.float32),
             jax.ShapeDtypeStruct((rows, width), low),
         ],
-        input_output_aliases={6 + i: i for i in range(len(keep))},
+        input_output_aliases={7 + i: i for i in range(len(keep))},
         compiler_params=kernel_params(),
-        cost_estimate=pl.CostEstimate(
-            flops=16 * steps * block_rows * width * width,
-            bytes_accessed=8 * width * width + 20 * steps * block_rows * width,
-            transcendentals=rows * width,
-        ),
+        cost_estimate=pl.CostEstimate(flops=0, bytes_accessed=0, transcendentals=0),
         name="attend_rows",
-    )(counts, hidden_one, start, weights, bias_full, rows_in, *keep)
+    )(counts, hidden_one, start, own, other, bias_full, rows_in, *keep)
 
 
 def expand_step(hidden_ref, turned_ref, out_ref, up_ref, bias_ref, down_ref):
@@ -592,11 +594,7 @@
             *extra_outs,
         ],
         compiler_params=kernel_params(),
-        cost_estimate=pl.CostEstimate(
-            flops=12 * rows * width * width * steps,
-            bytes_accessed=8 * width * width * steps + 16 * rows * width,
-            transcendentals=2 * rows * width * steps,
-        ),
+        cost_estimate=pl.CostEstimate(flops=0, bytes_accessed=0, transcendentals=0),
         name=name,
     )(half, *ins)
 
@@ -662,12 +660,14 @@
 
 
 def attend_back_body(
+    count_ref,
     project_ref,
     probs_ref,
     start_ref,
     middle_grad_ref,
     middle_low_ref,
-    weight_ref,
+    own_ref,
+    other_ref,
     rows_ref,
     project_low_ref,
     conv_low_ref,
@@ -675,12 +675,13 @@
     third_ref,
     mixed_low,
     grad_ref,
+    weight_ref,
 ):
+    join_weights(count_ref, own_ref, other_ref, weight_ref)
     block_rows, width = start_ref.shape
     slots = 64
     low = jnp.bfloat16
-    wide_out = weight_ref[:, 3].reshape(width, width)
-    mixed_low[...] = dot_nt(middle_low_ref[...], wide_out).astype(low)
+    mixed_low[...] = dot_nt(middle_low_ref[...], weight_ref[3]).astype(low)
     lanes = lax.broadcasted_iota(jnp.int32, (slots, 128), 1)
     low_half = lanes < 64
 
@@ -720,11 +721,10 @@
             fold(dot_tn(score_low, queries)) * 0.125
         ).astype(low)
     project_low = project_low_ref[...]
-    grad = dot_nt(project_low[:, :width], weight_ref[:, 0].reshape(width, width))
+    grad = dot_nt(project_low[:, :width], weight_ref[0])
     for third in (1, 2):
         at = third * width
-        weight = weight_ref[:, third].reshape(width, width)
-        grad = grad + dot_nt(project_low[:, at : at + width], weight)
+        grad = grad + dot_nt(project_low[:, at : at + width], weight_ref[third])
     normed, inverse = norm_rows(start_ref[...], 1e-06)
     scaled = grad * rows_ref[0:1, :]
     start_grad = middle_grad_ref[...] + inverse * (
@@ -755,47 +755,48 @@
 
 
 def attend_back(
-    project, probs_low, start, middle_grad, middle_low, weights, rows_in, block_rows
+    counts, project, probs_low, start, middle_grad, middle_low, own, other, rows_in, block_rows
 ):
     rows, width = start.shape
-    row_spec = lambda cols: pl.BlockSpec((block_rows, cols), lambda i: (i, 0))
+    row_spec = lambda cols: pl.BlockSpec((block_rows, cols), lambda i, *_: (i, 0))
     low = jnp.bfloat16
     return pl.pallas_call(
         attend_back_body,
-        grid=(rows // block_rows,),
-        in_specs=[
-            row_spec(3 * width),
-            row_spec(width),
-            row_spec(width),
-            row_spec(width),
-            row_spec(width),
-            whole_spec(weights.shape),
-            whole_spec(rows_in.shape),
-        ],
-        out_specs=[
-            row_spec(3 * width),
-            row_spec(width),
-            whole_spec((3, width)),
-            whole_spec((1, 3 * width)),
-        ],
+        grid_spec=pltpu.PrefetchScalarGridSpec(
+            num_scalar_prefetch=1,
+            grid=(rows // block_rows,),
+            in_specs=[
+                row_spec(3 * width),
+                row_spec(width),
+                row_spec(width),
+                row_spec(width),
+                row_spec(width),
+                whole_spec(own.shape),
+                whole_spec(other.shape),
+                whole_spec(rows_in.shape),
+            ],
+            out_specs=[
+                row_spec(3 * width),
+                row_spec(width),
+                whole_spec((3, width)),
+                whole_spec((1, 3 * width)),
+            ],
+            scratch_shapes=[
+                pltpu.VMEM((block_rows, width), low),
+                pltpu.VMEM((block_rows * width // 128, 128), jnp.float32),
+                pltpu.VMEM((4, width, width), low),
+            ],
+        ),
         out_shape=[
             jax.ShapeDtypeStruct((rows, 3 * width), low),
             jax.ShapeDtypeStruct((rows, width), low),
             jax.ShapeDtypeStruct((3, width), jnp.float32),
             jax.ShapeDtypeStruct((1, 3 * width), jnp.float32),
         ],
-        scratch_shapes=[
-            pltpu.VMEM((block_rows, width), low),
-            pltpu.VMEM((block_rows * width // 128, 128), jnp.float32),
-        ],
         compiler_params=kernel_params(),
-        cost_estimate=pl.CostEstimate(
-            flops=24 * rows * width * width,
-            bytes_accessed=8 * width * width + 30 * rows * width,
-            transcendentals=0,
-        ),
+        cost_estimate=pl.CostEstimate(flops=0, bytes_accessed=0, transcendentals=0),
         name="attend_back",
-    )(project, probs_low, start, middle_grad, middle_low, weights, rows_in)
+    )(counts, project, probs_low, start, middle_grad, middle_low, own, other, rows_in)
 
 
 def dot_full(one, two, dims, precision=highest):
@@ -853,6 +854,7 @@
         hyper_forward_body,
         out_shape=jax.ShapeDtypeStruct((pick_rows.shape[0], key_rows.shape[1]), jnp.float32),
         compiler_params=kernel_params(),
+        cost_estimate=pl.CostEstimate(flops=0, bytes_accessed=0, transcendentals=0),
         name="hyper_forward",
     )(pick_rows, bias_mask, key_rows, *params)
 
@@ -888,6 +890,7 @@
             jax.ShapeDtypeStruct((1, bias_weight.shape[1]), jnp.float32),
         ],
         compiler_params=kernel_params(),
+        cost_estimate=pl.CostEstimate(flops=0, bytes_accessed=0, transcendentals=0),
         name="hyper_backward",
     )(pick_rows, bias_mask, key_rows, *params, feats_grad, conv_grad, bias_weight)
 
@@ -976,6 +979,7 @@
         out_shape=jax.ShapeDtypeStruct((bands, rows, width), jnp.bfloat16),
         scratch_shapes=[pltpu.VMEM((2 * bands * block, hidden * block), jnp.bfloat16)],
         compiler_params=kernel_params(),
+        cost_estimate=pl.CostEstimate(flops=0, bytes_accessed=0, transcendentals=0),
         name="make_kernel",
     )(feats, kernel_weight, kernel_bias)
 
@@ -992,6 +996,7 @@
         table_body,
         out_shape=jax.ShapeDtypeStruct(tuple(size * block for size in feats.shape), jnp.bfloat16),
         compiler_params=kernel_params(),
+        cost_estimate=pl.CostEstimate(flops=0, bytes_accessed=0, transcendentals=0),
         name="weight_table",
     )(feats)
 
@@ -1003,28 +1008,26 @@
     out_ref[...] = dot_nn(table_ref[...], grad).reshape(hidden, block, width)
 
 
-def weight_grad(table, piece, place, rows, out):
-    count, block, width = piece.shape
-    if block != 16:
-        part = jnp.einsum("hs,spd->hpd", table, piece, preferred_element_type=jnp.float32)
-        return part if out is None else jnp.concatenate([out, part], 1)
+def weight_grad(table, kernel_all):
+    count, rows, width = kernel_all.shape
+    block = 16
+    if rows % block:
+        return jnp.einsum("hs,spd->hpd", table, kernel_all, preferred_element_type=jnp.float32)
     hidden = table.shape[0] // block
     halves = 2
-    keep = [] if out is None else [out]
     return pl.pallas_call(
         weight_grad_body,
-        grid=(halves,),
+        grid=(rows // block, halves),
         in_specs=[
-            pl.BlockSpec((hidden * block // halves, count * block), lambda i: (i, 0)),
-            whole_spec(piece.shape),
-            *(pl.BlockSpec(memory_space=pl.ANY) for _ in keep),
+            pl.BlockSpec((hidden * block // halves, count * block), lambda i, j: (j, 0)),
+            pl.BlockSpec((count, block, width), lambda i, j: (0, i, 0)),
         ],
-        out_specs=pl.BlockSpec((hidden // halves, block, width), lambda i: (i, place, 0)),
+        out_specs=pl.BlockSpec((hidden // halves, block, width), lambda i, j: (j, i, 0)),
         out_shape=jax.ShapeDtypeStruct((hidden, rows, width), jnp.float32),
-        input_output_aliases={2: 0} if keep else {},
         compiler_params=kernel_params(),
+        cost_estimate=pl.CostEstimate(flops=0, bytes_accessed=0, transcendentals=0),
         name="weight_grad",
-    )(table, piece, *keep)
+    )(table, kernel_all)
 
 
 def feats_body(grad_ref, weight_ref, out_ref):
@@ -1061,6 +1064,7 @@
         out_specs=whole_spec((bands, hidden)),
         out_shape=jax.ShapeDtypeStruct((bands, hidden), jnp.float32),
         compiler_params=kernel_params(),
+        cost_estimate=pl.CostEstimate(flops=0, bytes_accessed=0, transcendentals=0),
         name="feats_piece",
     )(piece, kernel_weight)
 
@@ -1111,6 +1115,7 @@
             out(down_rows, width),
         ],
         compiler_params=kernel_params(),
+        cost_estimate=pl.CostEstimate(flops=0, bytes_accessed=0, transcendentals=0),
         name="finish_grads",
     )(place, own, other)
 
@@ -1219,9 +1224,11 @@
         line_three, other_two, other, embed_part, out_low, all_waves
     )
     kernel_two = pair_up(line_two, other_two, links.x, 2).reshape(depth, model_width)
-    weights = pair_up(block, other, links.c, 3).reshape(8, 4, -1, model_width)
-
-    line_three, weights, kernel_two, all_waves = stage(line_three, weights, kernel_two, all_waves)
+    own = block.reshape(8, 2, model_width // 8, model_width)
+    other = other.reshape(own.shape)
+    counts = jnp.concatenate([kept_count[0], links.c.reshape(1)])
+
+    line_three, kernel_two, all_waves = stage(line_three, kernel_two, all_waves)
     other_three = links.xside(line_three)
     embed_part = embed_part + dot_nn(pixel_rows[:, depth : 2 * depth], kernel_two)
     wave_all = jax.vmap(wave_embed)(all_waves)
@@ -1233,9 +1240,7 @@
     piece_count = 2
     piece_pixels = shard_pixels // piece_count
     table_all = weight_table(feats_all, piece_pixels)
-    other_three, embed_part, weights, table_all = stage(
-        other_three, embed_part, weights, table_all
-    )
+    other_three, embed_part, table_all = stage(other_three, embed_part, table_all)
     kernel_three = pair_up(line_three, other_three, links.x, 2).reshape(depth, model_width)
 
     gains = widen(norm_gains)
@@ -1250,10 +1255,11 @@
         0,
         6,
         None,
-        kept_count[0],
+        counts,
         hidden_one,
         start,
-        weights,
+        own,
+        other,
         bias_full,
         jnp.stack([widen(output_bias), gains[1], shifts[1]]),
     )
@@ -1297,7 +1303,7 @@
     other_up = links.xside(send_up)
     other_down = links.yside(send_down)
     project_low, conv_low, sums_one, third_sums = attend_back(
-        project, probs_low, start, middle_grad, middle_low, weights, gains[0:1], 256
+        counts, project, probs_low, start, middle_grad, middle_low, own, other, gains[0:1], 256
     )
     kernel_grad = contract_rows(pixel_rows, conv_low).astype(low)
     kernel_grad = kernel_grad.reshape(band_count, links.line, 2, shard_pixels, model_width)
@@ -1384,30 +1390,33 @@
 
     send_units = pick(units, 1 - links.y, 0)
     send_down, keep_down = halve_down(down_sum, 1)
-    ready, send_units, send_down, keep_down, total_one = stage(
-        ready, send_units, send_down, keep_down, total_one
+    ready, send_units, send_down, keep_down, total_one, conv_low = stage(
+        ready, send_units, send_down, keep_down, total_one, conv_low
     )
     total_two = send_line(links, ready, 1, links.zside)
     other_units = links.yside(send_units)
     other_down = links.xside(send_down)
     low_one = finish_piece(total_one)
     feats_one = feats_piece(low_one, kernel_weight, 0)
-    total_two, other_units, other_down, feats_one, low_one = stage(
-        total_two, other_units, other_down, feats_one, low_one
-    )
+    wide_kernel = jnp.concatenate([kernel_one, kernel_two, kernel_three], 0)
+    pixel_grad = pixel_gradient(conv_low, wide_kernel, image_count, band_count)
+    total_two, other_units, other_down, feats_one, low_one, pixel_grad = stage(
+        total_two, other_units, other_down, feats_one, low_one, pixel_grad
+    )
+    pixel_grad = pixel_grad.transpose(0, 2, 1, 3)[None]
     low_two = finish_piece(total_two)
 
-    low_two, feats_one = stage(low_two, feats_one)
     feats_part = feats_one + feats_piece(low_two, kernel_weight, 1)
+    tiny = jnp.concatenate([small, feats_part.reshape(-1, model_width)], 0)
+    tiny, units, other_units, low_two = stage(tiny, units, other_units, low_two)
+    tiny = tiny + links.xside(tiny)
     units = add_low(pick(units, links.y, 0), other_units)
     units = units.reshape(links.line, 2, shard_rows, model_width)
     send_units = pick(units, 1 - links.x, 1)
-    tiny = jnp.concatenate([small, feats_part.reshape(-1, model_width)], 0)
-    tiny, low_one, send_units = stage(tiny, low_one, send_units)
-    tiny = tiny + links.xside(tiny)
-    tiny, send_units = stage(tiny, send_units)
+    kernel_low = jnp.concatenate([low_one, low_two], 1)
+    tiny, send_units, kernel_low, units = stage(tiny, send_units, kernel_low, units)
     other_units = links.xside(send_units)
-    other_one = links.yside(low_one)
+    other_low = links.yside(kernel_low)
     small_count = small.shape[0]
     feats_part = tiny[small_count:].reshape(feats_part.shape)
     step = 2
@@ -1420,21 +1429,19 @@
     small = small + other_small[:-1]
     conv_all = pair_up(conv_all, other_small[-1:], links.c, 0)
     down_sum = add_low(keep_down, other_down).reshape(down_rows // 2, model_width)
-    feats_part, other_one, other_units, low_two, small, conv_all, down_sum = stage(
-        feats_part, other_one, other_units, low_two, small, conv_all, down_sum
+    feats_part, other_units, small, conv_all, down_sum = stage(
+        feats_part, other_units, small, conv_all, down_sum
     )
     units = add_low(pick(units, links.x, 1), other_units).reshape(links.line, -1, model_width)
     half_shard = shard_rows // 2
     up_blocks = up_sum.reshape(links.line, half_shard, 2, model_width).transpose(0, 2, 1, 3)
     both = jnp.concatenate([up_blocks.reshape(units.shape), units], 1)
-    all_one = pair_up(low_one[None], other_one[None], links.y, 0)[:, None]
 
     tiny = jnp.concatenate([small, conv_all, feats_part.reshape(-1, model_width)], 0)
-    tiny, all_one, both, low_two, down_sum = stage(tiny, all_one, both, low_two, down_sum)
+    tiny, both, down_sum = stage(tiny, both, down_sum)
     both = send_line(links, both, 0, links.zside)
+    other_down = links.owner_line(down_sum)
     other_tiny = links.yside(tiny)
-    other_two = links.yside(low_two)
-    other_one = links.core(all_one)
     small = small + other_tiny[: small_count - 1]
     conv_all = pair_up(conv_all, other_tiny[small_count - 1 : small_count + 1], links.y, 0)
     feats_part = feats_part[None]
@@ -1442,15 +1449,6 @@
     feats_two = pair_up(feats_part, feats_y, links.y, 0)
     feats_c = links.core(feats_two)
     feats_grad = pair_up(feats_two[:, None], feats_c[:, None], links.c, 1).reshape(-1, HE)
-    feats_grad, other_one, other_two, small, conv_all, down_sum = stage(
-        feats_grad, other_one, other_two, small, conv_all, down_sum
-    )
-    all_one = pair_up(all_one, other_one, links.c, 1).reshape((wave_count,) + low_one.shape[1:])
-    all_two = pair_up(low_two[None], other_two[None], links.y, 0)[:, None]
-
-    all_two, feats_grad, all_one, down_sum = stage(all_two, feats_grad, all_one, down_sum)
-    other_two = links.core(all_two)
-    other_down = links.owner_line(down_sum)
     key_grad, *param_grads, bias_weight_grad, bias_shift_grad = hyper_backward(
         pick_rows,
         bias_mask,
@@ -1460,26 +1458,25 @@
         conv_all,
         bias_weight,
     )
-    wide_kernel = jnp.concatenate([kernel_one, kernel_two, kernel_three], 0)
-    pixel_grad = pixel_gradient(conv_low, wide_kernel, band_count)
-    weight_shard_grad = weight_grad(table_all, all_one, 0, shard_pixels, None)
-    other_two, key_grad, both, other_down, weight_shard_grad, pixel_grad = stage(
-        other_two, key_grad, both, other_down, weight_shard_grad, pixel_grad
-    )
-    pixel_grad = pixel_grad.reshape(pixels.shape)
+    kernel_all = pair_up(kernel_low[None], other_low[None], links.y, 0)[:, None]
+    both, other_down, key_grad, kernel_all, small = stage(
+        both, other_down, key_grad, kernel_all, small
+    )
     both = jnp.concatenate([add_low(*both), add_low(down_sum, other_down)], 0)[None]
-    all_two = pair_up(all_two, other_two, links.c, 1).reshape(all_one.shape)
-
-    both, all_two = stage(both, all_two)
+
+    both, kernel_all = stage(both, kernel_all)
     other_both = links.yside(both)
-    weight_shard_grad = weight_grad(table_all, all_two, 1, shard_pixels, weight_shard_grad)
-    other_both, weight_shard_grad = stage(other_both, weight_shard_grad)
+    other_all = links.core(kernel_all)
+    kernel_all = pair_up(kernel_all, other_all, links.c, 1)
+    kernel_all = kernel_all.reshape((wave_count,) + kernel_low.shape[1:])
+    weight_shard_grad = weight_grad(table_all, kernel_all)
+    bias_shard_grad = scaler * jnp.sum(kernel_all.astype(floaty), 0)
+    token_count = weight_tokens.shape[0]
+    other_both, weight_shard_grad, bias_shard_grad = stage(
+        other_both, weight_shard_grad, bias_shard_grad
+    )
     both = pair_up(both, other_both, links.y, 0)
     other_both = links.core(both)
-    token_count = weight_tokens.shape[0]
-    bias_shard_grad = scaler * jnp.concatenate(
-        [jnp.sum(item.astype(floaty), 0) for item in (all_one, all_two)], 0
-    )
     is_owner = lax.axis_index("dp") // (dp_size // 2) == links.c
     if shard_rows % 32 == 0:
         place = jnp.stack([links.c, is_owner.astype(jnp.int32)])

time: 485 us -> 458 us (0.944)
  other arithmetic: 59.9 us -> 48.5 us
  Pallas kernels: 147 us -> 141 us
  waiting for transfers between devices: 134 us -> 129 us
    select_n x19 -> x15, other arithmetic: 19.9 us -> 8.94 us  [pair_up(): jnp.where(bit == 0, jnp.concatenate([block, other], axis), jnp.concatenat...]
    ppermute x9 -> x8, waiting for transfers between devices: 15.7 us -> 6.27 us  [yside(): lax.ppermute(block, 'group', [(i, i ^ 2) for i in range(self.group_size)])]
    pallas_call x4 -> x3, Pallas kernels: 43.8 us -> 35.8 us  [the longest x1 16.4 us: attend_back(): pl.pallas_call(attend_back_body, grid_spec=pltpu.PrefetchScalarGridSpec(n...]
    unnamed x122 -> x105, local copies, waits for them, and re-layouts: 15.5 us -> 11 us
  transfers between devices with their start and end apart: 57 -> 55, of which waited for: 29 -> 26; matrix products, arithmetic and copies ran while one was open for 17% -> 18% of each run, Pallas kernels for 25% -> 25%
where the time goes in v3:
time: 458 us; the launch traced here: 453 us
  Pallas kernels  141 us (31%)
  waiting for transfers between devices  129 us (28%)
  starting transfers between devices  60.6 us (13%)
  other arithmetic  48.5 us (11%)
  local copies, waits for them, and re-layouts  40.9 us (9%)
  matrix products  17.8 us (4%)
  between operations  15.7 us (3%)
    ppermute x26, waiting for transfers between devices, zside(): lax.ppermute(block, 'dp', [(i, i ^ step) for i in range(self.dp_size)])  101 us
    pallas_call x2, Pallas kernels, expand_call(): pl.pallas_call(body, grid_spec=pltpu.PrefetchScalarGridSpec(num_scalar_pr...  41.2 us
    ppermute x26, starting transfers between devices, zside(): lax.ppermute(block, 'dp', [(i, i ^ step) for i in range(self.dp_size)])  35.6 us
    ppermute x10, waiting for transfers between devices, xside(): return lax.ppermute(block, 'dp', [(i, i ^ 1) for i in range(self.dp_size)])  16.7 us
    pallas_call x1, Pallas kernels, attend_back(): pl.pallas_call(attend_back_body, grid_spec=pltpu.PrefetchScalarGridSpec(n...  16.4 us
    convert_element_type x12, other arithmetic, add_low(): return total.astype(jnp.bfloat16)  15.7 us
    pallas_call x1, Pallas kernels, attend_rows(): pl.pallas_call(body, grid_spec=pltpu.PrefetchScalarGridSpec(num_scalar_pr...  15.5 us
    ppermute x10, starting transfers between devices, xside(): return lax.ppermute(block, 'dp', [(i, i ^ 1) for i in range(self.dp_size)])  14.2 us
  transfers between devices with their start and end apart: 55, of which 26 were waited for; matrix products, arithmetic and copies ran while one was open for 18% of the time, Pallas kernels for 25%

profile of v3, /device:TPU:0, one launch (start us, length us, event | category | flops | bytes accessed | tf_op | source)
XLA Modules:
  0.0 452.9 jit_solution(13453705558658051879)
XLA Ops:
  10.4 4.1 collective-permute-start.1
  17.6 5.2 %hyper_forward.2 = f32[16,128]{1,0:T(8,128)} custom-call(f32[16,144]{1,0:T(8,128)} %constant.166.clone.refs_0_, f32[16,144]{1,0:T(8,128)} %constant.167.clone.refs_1_, f32[144,128]{1,0:T(8,128)} %maximum_maximum_fusion.1.refs_2_, bf16[128,384]{1,0:T(8,128)(2,1)} %refs_0_.3, bf16[128,128]{1,0:T(8,128)(2,1)} %refs_1_.3, bf16[2,128]{1,0:T(2,128)(2,1)} %refs_2_.1, ...), custom_call_target="tpu_custom_call" | custom-call | tf_op jit(solution)/shard_map/hyper_forward/pallas_call | solution.py:853
  27.5 6.7 %make_kernel.1 = bf16[12,32,768]{2,1,0:T(8,128)(2,1)} custom-call(bf16[24,128]{1,0:T(8,128)(2,1)} %pad_maximum_fusion.10.feats_ref, bf16[128,32,768]{2,1,0:T(8,128)(2,1)} %weight_ref.5, bf16[32,768]{1,0:T(8,128)(2,1)} %bias_ref.1), custom_call_target="tpu_custom_call" | custom-call | tf_op jit(solution)/shard_map/make_kernel/pallas_call | solution.py:970
  35.5 3.9 collective-permute-start.5
  44.7 14.9 %collective-permute-done.3 = bf16[4,1,1,32,768]{4,3,0,2,1:T(8,128)(2,1)S(1)} collective-permute-done((bf16[4,1,1,32,768]{4,3,0,2,1:T(8,128)(2,1)S(1)}, bf16[4,1,1,32,768]{4,3,0,2,1:T(8,128)(2,1)S(1)}, u32[]{:S(2)}, u32[]{:S(2)}) %collective-permute-start.3) | collective-permute-done | bytes 196640 | tf_op jit(solution)/shard_map/ppermute | solution.py:94
  72.4 5.8 %copy.140 = bf16[1,12,64,12,256]{4,3,2,1,0:T(8,128)(2,1)S(1)} copy(bf16[1,12,64,12,256]{4,2,3,1,0:T(8,128)(2,1)} %param.31) | data formatting | bytes 9437184 | tf_op jit(solution)/shard_map/optimization_barrier | solution.py:63
  81.5 14.8 %collective-permute-done.10 = bf16[4,1,1,32,768]{4,3,0,2,1:T(8,128)(2,1)S(1)} collective-permute-done((bf16[4,1,1,32,768]{4,3,0,2,1:T(8,128)(2,1)S(1)}, bf16[4,1,1,32,768]{4,3,0,2,1:T(8,128)(2,1)S(1)}, u32[]{:S(2)}, u32[]{:S(2)}) %collective-permute-start.10) | collective-permute-done | bytes 196640 | tf_op jit(solution)/shard_map/ppermute | solution.py:94
  96.4 3.8 collective-permute-done.13
  103.8 3.6 collective-permute-start.16
  115.7 12.5 %collective-permute-done.14 = bf16[4,1,1,32,768]{4,3,0,2,1:T(8,128)(2,1)S(1)} collective-permute-done((bf16[4,1,1,32,768]{4,3,0,2,1:T(8,128)(2,1)S(1)}, bf16[4,1,1,32,768]{4,3,0,2,1:T(8,128)(2,1)S(1)}, u32[]{:S(2)}, u32[]{:S(2)}) %collective-permute-start.14) | collective-permute-done | bytes 196640 | tf_op jit(solution)/shard_map/ppermute | solution.py:94
  128.3 5.0 %collective-permute-done.15 = bf16[4,1,1,32,768]{4,3,0,2,1:T(8,128)(2,1)S(1)} collective-permute-done((bf16[4,1,1,32,768]{4,3,0,2,1:T(8,128)(2,1)S(1)}, bf16[4,1,1,32,768]{4,3,0,2,1:T(8,128)(2,1)S(1)}, u32[]{:S(2)}, u32[]{:S(2)}) %collective-permute-start.15) | collective-permute-done | bytes 196640 | tf_op jit(solution)/shard_map/ppermute | solution.py:94
  138.2 5.9 %hyper_forward.3 = f32[56,128]{1,0:T(8,128)} custom-call(f32[56,192]{1,0:T(8,128)} %constant.168.clone.refs_0_.pick_ref, f32[56,192]{1,0:T(8,128)} %constant.169.clone.refs_1_.mask_ref, f32[192,128]{1,0:T(8,128)} %maximum_maximum_fusion.refs_2_.key_ref, bf16[128,384]{1,0:T(8,128)(2,1)} %refs_0_.3, bf16[128,128]{1,0:T(8,128)(2,1)} %refs_1_.3, ...), custom_call_target="tpu_custom_call" | custom-call | tf_op jit(solution)/shard_map/hyper_forward/pallas_call | solution.py:853
  145.7 3.8 weight_table.1.table_ref
  157.7 5.7 %embed_rows.1 = (f32[768,768]{1,0:T(8,128)}, bf16[768,768]{1,0:T(8,128)(2,1)}) custom-call(f32[768,768]{1,0:T(8,128)} %add.271.part_ref, bf16[768,3072]{1,0:T(8,128)(2,1)} %bitcast.175, bf16[1024,768]{1,0:T(8,128)(2,1)} %bitcast.177, f32[2,768]{1,0:T(2,128)} %pad_maximum_fusion.11.norm_ref), custom_call_target="tpu_custom_call" | custom-call | tf_op jit(solution)/shard_map/embed_rows/pallas_call | solution.py:250
  163.4 15.5 %attend_rows.1 = (bf16[768,2304]{1,0:T(8,128)(2,1)}, bf16[768,768]{1,0:T(8,128)(2,1)}, bf16[768,768]{1,0:T(8,128)(2,1)}, f32[768,768]{1,0:T(8,128)}, bf16[768,768]{1,0:T(8,128)(2,1)}) custom-call(s32[13]{0:T(128)} %pad_add_fusion.count_ref, bf16[768,768]{1,0:T(8,128)(2,1)} %get-tuple-element.220.refs_0_, f32[768,768]{1,0:T(8,128)} %get-tuple-element.221.refs_1_.start_ref, ...), custom_call_target="tpu_custom_call" | custom-call | tf_op jit(solution)/shard_map/attend_rows/pallas_call | solution.py:395
  178.9 18.6 %expand_first.1 = (bf16[768,1536]{1,0:T(8,128)(2,1)}, bf16[1536,768]{1,0:T(8,128)(2,1)}, f32[1,1536]{1,0:T(1,128)}, f32[768,768]{1,0:T(8,128)}, f32[768,768]{1,0:T(8,128)}) custom-call(s32[1]{0:T(128)} %bitcast.40.half_ref, bf16[768,768]{1,0:T(8,128)(2,1)} %get-tuple-element.223.hidden_ref, bf16[768,768]{1,0:T(8,128)(2,1)} %bitcast_multiply_fusion.out_ref, ...), custom_call_target="tpu_custom_call" | custom-call | tf_op jit(solution)/shard_map/expand_first/pallas_call | solution.py:564
  199.8 22.6 %expand_second.1 = (bf16[768,1536]{1,0:T(8,128)(2,1)}, bf16[1536,768]{1,0:T(8,128)(2,1)}, f32[1,1536]{1,0:T(1,128)}, bf16[768,768]{1,0:T(8,128)(2,1)}, f32[768,7...) custom-call(s32[1]{0:T(128)} %bitcast.half_ref, bf16[768,768]{1,0:T(8,128)(2,1)} %get-tuple-element.223.hidden_ref, ...), custom_call_target="tpu_custom_call" | custom-call | tf_op jit(solution)/shard_map/expand_second/pallas_call | solution.py:564
  231.2 16.4 %attend_back.1 = (bf16[768,2304]{1,0:T(8,128)(2,1)}, bf16[768,768]{1,0:T(8,128)(2,1)}, f32[3,768]{1,0:T(4,128)}, f32[1,2304]{1,0:T(1,128)}) custom-call(s32[13]{0:T(128)} %pad_add_fusion.count_ref, bf16[768,2304]{1,0:T(8,128)(2,1)} %get-tuple-element.244.project_ref, bf16[768,768]{1,0:T(8,128)(2,1)} %get-tuple-element.245.probs_ref, ...), custom_call_target="tpu_custom_call" | custom-call | tf_op jit(solution)/shard_map/attend_back/pallas_call | solution.py:763
  247.6 6.6 %convolution_convert_fusion = bf16[3072,768]{1,0:T(8,128)(2,1)S(1)} fusion(bf16[768,3072]{1,0:T(8,128)(2,1)} %bitcast.176, bf16[768,768]{1,0:T(8,128)(2,1)} %get-tuple-element.292.grad_ref), kind=kOutput, calls=%fused_computation | convolution fusion | flops 3626237952 | bytes 10616832 | tf_op jit(solution)/shard_map/dot_general | solution.py:21
  274.0 9.0 %collective-permute-done.28 = f32[13,768]{1,0:T(8,128)S(1)} collective-permute-done((f32[13,768]{1,0:T(8,128)S(1)}, f32[13,768]{1,0:T(8,128)S(1)}, u32[]{:S(2)}, u32[]{:S(2)}) %collective-permute-start.28) | collective-permute-done | bytes 39968 | tf_op jit(solution)/shard_map/ppermute | solution.py:94
  284.1 8.9 %collective-permute-done.24 = bf16[12,4,1,16,768]{4,3,0,1,2:T(8,128)(2,1)S(1)} collective-permute-done((bf16[12,4,1,16,768]{4,3,0,1,2:T(8,128)(2,1)S(1)}, bf16[12,4,1,16,768]{4,3,0,1,2:T(8,128)(2,1)S(1)}, u32[]{:S(2)}, u32[]{:S(2)}) %collective-permute-start.24) | collective-permute-done | bytes 1179680 | tf_op jit(solution)/shard_map/ppermute | solution.py:91
  299.6 7.1 %collective-permute-done.32 = bf16[12,1,16,768]{3,2,0,1:T(8,128)(2,1)S(1)} collective-permute-done((bf16[12,1,16,768]{3,2,0,1:T(8,128)(2,1)S(1)}, bf16[12,1,16,768]{3,2,0,1:T(8,128)(2,1)S(1)}, u32[]{:S(2)}, u32[]{:S(2)}) %collective-permute-start.32) | collective-permute-done | bytes 294944 | tf_op jit(solution)/shard_map/ppermute | solution.py:94
  306.7 14.4 %collective-permute-done.31 = bf16[12,1,16,768]{3,2,0,1:T(8,128)(2,1)S(1)} collective-permute-done((bf16[12,1,16,768]{3,2,0,1:T(8,128)(2,1)S(1)}, bf16[12,1,16,768]{3,2,0,1:T(8,128)(2,1)S(1)}, u32[]{:S(2)}, u32[]{:S(2)}) %collective-permute-start.31) | collective-permute-done | bytes 294944 | tf_op jit(solution)/shard_map/ppermute | solution.py:94
  335.5 4.3 feats_piece.2
  339.8 7.9 %pixel_gradient.1 = bf16[12,12,64,256]{3,2,1,0:T(8,128)(2,1)} custom-call(bf16[768,768]{1,0:T(8,128)(2,1)} %get-tuple-element.292.grad_ref, bf16[3072,768]{1,0:T(8,128)(2,1)} %pad_maximum_fusion.kernel_ref), custom_call_target="tpu_custom_call" | custom-call | tf_op jit(solution)/shard_map/pixel_gradient/pallas_call | solution.py:282
  347.7 5.5 %collective-permute-done.35 = bf16[12,1,16,768]{3,2,0,1:T(8,128)(2,1)} collective-permute-done((bf16[12,1,16,768]{3,2,0,1:T(8,128)(2,1)}, bf16[12,1,16,768]{3,2,0,1:T(8,128)(2,1)}, u32[]{:S(2)}, u32[]{:S(2)}) %collective-permute-start.35) | collective-permute-done | bytes 294944 | tf_op jit(solution)/shard_map/ppermute | solution.py:94
  355.4 4.3 feats_piece.3
  374.4 5.0 %collective-permute-done.42 = bf16[4,1,96,768]{3,2,0,1:T(8,128)(2,1)} collective-permute-done((bf16[4,1,96,768]{3,2,0,1:T(8,128)(2,1)}, bf16[4,1,96,768]{3,2,0,1:T(8,128)(2,1)}, u32[]{:S(2)}, u32[]{:S(2)}) %collective-permute-start.42) | collective-permute-done | bytes 589856 | tf_op jit(solution)/shard_map/ppermute | solution.py:91
  391.6 8.5 %hyper_backward.1 = (f32[192,128]{1,0:T(8,128)}, f32[128,384]{1,0:T(8,128)}, f32[128,128]{1,0:T(8,128)}, f32[2,128]{1,0:T(2,128)}, f32[2,128]{1,0:T(2,128)}, /*i...) custom-call(f32[56,192]{1,0:T(8,128)} %constant.168.clone.refs_0_.pick_ref, ...), custom_call_target="tpu_custom_call" | custom-call | tf_op jit(solution)/shard_map/hyper_backward/pallas_call | solution.py:884
  400.1 11.8 %collective-permute-done.45 = bf16[1,192,768]{2,1,0:T(8,128)(2,1)} collective-permute-done((bf16[1,192,768]{2,1,0:T(8,128)(2,1)}, bf16[1,192,768]{2,1,0:T(8,128)(2,1)}, u32[]{:S(2)}, u32[]{:S(2)}) %collective-permute-start.45) | collective-permute-done | bytes 294944 | tf_op jit(solution)/shard_map/ppermute | solution.py:94
  421.1 11.5 %weight_grad.1 = f32[128,32,768]{2,1,0:T(8,128)} custom-call(bf16[2048,768]{1,0:T(8,128)(2,1)} %weight_table.1.table_ref, bf16[48,32,768]{2,1,0:T(8,128)(2,1)} %bitcast.179), custom_call_target="tpu_custom_call" | custom-call | tf_op jit(solution)/shard_map/weight_grad/pallas_call | solution.py:1018
  442.1 3.7 finish_grads.1
  (378 shorter events, 160.0 us)
Async XLA Ops:
  7.2 171.6 %all-gather.3.cloned.1.call-start = ((), (), s32[]{:S(2)}) async-start(), calls=%async_computation | async-start | bytes 9732096 | tf_op jit(solution)/shard_map/all_gather | solution.py:184
  10.4 23.9 %collective-permute-start.1 = (bf16[1,1,1,1,96,768]{5,4,2,1,0,3:T(8,128)(2,1)S(1)}, bf16[1,1,1,1,96,768]{5,4,2,1,0,3:T(8,128)(2,1)S(1)}, u32[]{:S(2)}, u32[]{:S(2)}) collective-permute-start(bf16[1,1,1,1,96,768]{5,4,2,1,0,3:T(8,128)(2,1)S(1)} %get-tuple-element.357), channel_id=1, source_target_pairs={{0,4},{1,5},{2,6},{3,7},{4,0},{5,1},{6,2},{7,3},{8,12},{9,13},{10,... | collective-permute-start | bytes 442376 | tf_op jit(solution)/shard_map/ppermute | solution.py:94
  35.5 27.3 %collective-permute-start.5 = (bf16[4,1,1,32,768]{4,3,0,2,1:T(8,128)(2,1)S(1)}, bf16[4,1,1,32,768]{4,3,0,2,1:T(8,128)(2,1)S(1)}, u32[]{:S(2)}, u32[]{:S(2)}) collective-permute-start(bf16[4,1,1,32,768]{4,3,0,2,1:T(8,128)(2,1)S(1)} %get-tuple-element.384), channel_id=1, source_target_pairs={{0,6},{1,7},{2,4},{3,5},{4,2},{5,3},{6,0},{7,1},{8,14},{9,15},{10,... | collective-permute-start | bytes 589832 | tf_op jit(solution)/shard_map/ppermute | solution.py:94
  39.3 23.4 %collective-permute-start.4 = (bf16[4,1,1,32,768]{4,3,0,2,1:T(8,128)(2,1)S(1)}, bf16[4,1,1,32,768]{4,3,0,2,1:T(8,128)(2,1)S(1)}, u32[]{:S(2)}, u32[]{:S(2)}) collective-permute-start(bf16[4,1,1,32,768]{4,3,0,2,1:T(8,128)(2,1)S(1)} %get-tuple-element.384), channel_id=1, source_target_pairs={{0,4},{1,5},{2,6},{3,7},{4,0},{5,1},{6,2},{7,3},{8,12},{9,13},{10,... | collective-permute-start | bytes 589832 | tf_op jit(solution)/shard_map/ppermute | solution.py:94
  39.4 20.3 %collective-permute-start.3 = (bf16[4,1,1,32,768]{4,3,0,2,1:T(8,128)(2,1)S(1)}, bf16[4,1,1,32,768]{4,3,0,2,1:T(8,128)(2,1)S(1)}, u32[]{:S(2)}, u32[]{:S(2)}) collective-permute-start(bf16[4,1,1,32,768]{4,3,0,2,1:T(8,128)(2,1)S(1)} %get-tuple-element.384), channel_id=1, source_target_pairs={{0,2},{1,3},{2,0},{3,1},{4,6},{5,7},{6,4},{7,5},{8,10},{9,11},{10,... | collective-permute-start | bytes 589832 | tf_op jit(solution)/shard_map/ppermute | solution.py:94
  41.7 21.7 %collective-permute-start.6 = (bf16[4,1,1,1,96,768]{5,4,2,1,0,3:T(8,128)(2,1)S(1)}, bf16[4,1,1,1,96,768]{5,4,2,1,0,3:T(8,128)(2,1)S(1)}, u32[]{:S(2)}, u32[]{:S(2)}) collective-permute-start(bf16[4,1,1,1,96,768]{5,4,2,1,0,3:T(8,128)(2,1)S(1)} %constant_dynamic-update-slice_fusion), channel_id=1, source_target_pairs={{0,1},{1,0},{2,3},{3,2},{4,5},{5,4},{6,7},{7,6},{8,9},{9,8},{10,11... | collective-permute-start | bytes 1769480 | tf_op jit(solution)/shard_map/ppermute | solution.py:91
  63.4 36.8 %collective-permute-start.13 = (bf16[4,2,1,1,96,768]{5,4,2,1,0,3:T(8,128)(2,1)S(1)}, bf16[4,2,1,1,96,768]{5,4,2,1,0,3:T(8,128)(2,1)}, u32[]{:S(2)}, u32[]{:S(2)}) collective-permute-start(bf16[4,2,1,1,96,768]{5,4,2,1,0,3:T(8,128)(2,1)S(1)} %maximum_select_fusion.5), channel_id=1, source_target_pairs={{0,16},{8,24},{16,0},{24,8},{1,17},{9,25},{17,1},{25,9},{2,18},{10... | collective-permute-start | bytes 3538952 | tf_op jit(solution)/shard_map/ppermute | solution.py:88
  66.0 30.3 %collective-permute-start.11 = (bf16[4,1,1,32,768]{4,3,0,2,1:T(8,128)(2,1)S(1)}, bf16[4,1,1,32,768]{4,3,0,2,1:T(8,128)(2,1)S(1)}, u32[]{:S(2)}, u32[]{:S(2)}) collective-permute-start(bf16[4,1,1,32,768]{4,3,0,2,1:T(8,128)(2,1)S(1)} %get-tuple-element.193), channel_id=1, source_target_pairs={{0,6},{1,7},{2,4},{3,5},{4,2},{5,3},{6,0},{7,1},{8,14},{9,15},{10,... | collective-permute-start | bytes 589832 | tf_op jit(solution)/shard_map/ppermute | solution.py:94
  68.9 27.4 %collective-permute-start.10 = (bf16[4,1,1,32,768]{4,3,0,2,1:T(8,128)(2,1)S(1)}, bf16[4,1,1,32,768]{4,3,0,2,1:T(8,128)(2,1)S(1)}, u32[]{:S(2)}, u32[]{:S(2)}) collective-permute-start(bf16[4,1,1,32,768]{4,3,0,2,1:T(8,128)(2,1)S(1)} %get-tuple-element.193), channel_id=1, source_target_pairs={{0,4},{1,5},{2,6},{3,7},{4,0},{5,1},{6,2},{7,3},{8,12},{9,13},{10,... | collective-permute-start | bytes 589832 | tf_op jit(solution)/shard_map/ppermute | solution.py:94
  70.5 25.9 %collective-permute-start.12 = (bf16[4,4,1,32,768]{4,3,2,1,0:T(8,128)(2,1)S(1)}, bf16[4,4,1,32,768]{4,3,2,1,0:T(8,128)(2,1)S(1)}, u32[]{:S(2)}, u32[]{:S(2)}) collective-permute-start(bf16[4,4,1,32,768]{4,3,2,1,0:T(8,128)(2,1)S(1)} %bitcast_dynamic-update-slice_fusion.9), channel_id=1, source_target_pairs={{0,1},{1,0},{2,3},{3,2},{4,5},{5,4},{6,7},{7,6},{8,9},{9,8},{10,11... | collective-permute-start | bytes 2359304 | tf_op jit(solution)/shard_map/ppermute | solution.py:91
  103.0 30.3 %collective-permute-start.18 = (bf16[4,2,2,1,96,768]{5,4,2,1,0,3:T(8,128)(2,1)S(1)}, bf16[4,2,2,1,96,768]{5,4,2,1,0,3:T(8,128)(2,1)S(1)}, u32[]{:S(2)}, u32[]{:S(2)}) collective-permute-start(bf16[4,2,2,1,96,768]{5,4,2,1,0,3:T(8,128)(2,1)S(1)} %maximum_select_fusion), channel_id=1, source_target_pairs={{0,8},{8,0},{16,24},{24,16},{1,9},{9,1},{17,25},{25,17},{2,10},{10... | collective-permute-start | bytes 7077896 | tf_op jit(solution)/shard_map/ppermute | solution.py:85
  103.8 29.4 %collective-permute-start.16 = (bf16[4,1,1,32,768]{4,3,0,2,1:T(8,128)(2,1)S(1)}, bf16[4,1,1,32,768]{4,3,0,2,1:T(8,128)(2,1)S(1)}, u32[]{:S(2)}, u32[]{:S(2)}) collective-permute-start(bf16[4,1,1,32,768]{4,3,0,2,1:T(8,128)(2,1)S(1)} %get-tuple-element.204), channel_id=1, source_target_pairs={{0,6},{1,7},{2,4},{3,5},{4,2},{5,3},{6,0},{7,1},{8,14},{9,15},{10,... | collective-permute-start | bytes 589832 | tf_op jit(solution)/shard_map/ppermute | solution.py:94
  107.4 25.8 %collective-permute-start.15 = (bf16[4,1,1,32,768]{4,3,0,2,1:T(8,128)(2,1)S(1)}, bf16[4,1,1,32,768]{4,3,0,2,1:T(8,128)(2,1)S(1)}, u32[]{:S(2)}, u32[]{:S(2)}) collective-permute-start(bf16[4,1,1,32,768]{4,3,0,2,1:T(8,128)(2,1)S(1)} %get-tuple-element.204), channel_id=1, source_target_pairs={{0,4},{1,5},{2,6},{3,7},{4,0},{5,1},{6,2},{7,3},{8,12},{9,13},{10,... | collective-permute-start | bytes 589832 | tf_op jit(solution)/shard_map/ppermute | solution.py:94
  107.4 20.8 %collective-permute-start.14 = (bf16[4,1,1,32,768]{4,3,0,2,1:T(8,128)(2,1)S(1)}, bf16[4,1,1,32,768]{4,3,0,2,1:T(8,128)(2,1)S(1)}, u32[]{:S(2)}, u32[]{:S(2)}) collective-permute-start(bf16[4,1,1,32,768]{4,3,0,2,1:T(8,128)(2,1)S(1)} %get-tuple-element.204), channel_id=1, source_target_pairs={{0,2},{1,3},{2,0},{3,1},{4,6},{5,7},{6,4},{7,5},{8,10},{9,11},{10,... | collective-permute-start | bytes 589832 | tf_op jit(solution)/shard_map/ppermute | solution.py:94
  108.5 24.8 %collective-permute-start.17 = (bf16[4,4,1,32,768]{4,3,2,1,0:T(8,128)(2,1)S(1)}, bf16[4,4,1,32,768]{4,3,2,1,0:T(8,128)(2,1)S(1)}, u32[]{:S(2)}, u32[]{:S(2)}) collective-permute-start(bf16[4,4,1,32,768]{4,3,2,1,0:T(8,128)(2,1)S(1)} %bitcast_dynamic-update-slice_fusion.5), channel_id=1, source_target_pairs={{0,1},{1,0},{2,3},{3,2},{4,5},{5,4},{6,7},{7,6},{8,9},{9,8},{10,11... | collective-permute-start | bytes 2359304 | tf_op jit(solution)/shard_map/ppermute | solution.py:91
  197.5 27.2 %collective-permute-start.20 = (bf16[768,1536]{1,0:T(8,128)(2,1)}, bf16[768,1536]{1,0:T(8,128)(2,1)}, u32[]{:S(2)}, u32[]{:S(2)}) collective-permute-start(bf16[768,1536]{1,0:T(8,128)(2,1)} %get-tuple-element.232), channel_id=1, source_target_pairs={{0,8},{8,0},{16,24},{24,16},{1,9},{9,1},{17,25},{25,17},{2,10},{10... | collective-permute-start | bytes 7077896 | tf_op jit(solution)/shard_map/ppermute | solution.py:85
  197.6 27.2 %collective-permute-start.21 = (bf16[1536,768]{1,0:T(8,128)(2,1)}, bf16[1536,768]{1,0:T(8,128)(2,1)S(1)}, u32[]{:S(2)}, u32[]{:S(2)}) collective-permute-start(bf16[1536,768]{1,0:T(8,128)(2,1)} %get-tuple-element.233), channel_id=1, source_target_pairs={{0,8},{8,0},{16,24},{24,16},{1,9},{9,1},{17,25},{25,17},{2,10},{10... | collective-permute-start | bytes 7077896 | tf_op jit(solution)/shard_map/ppermute | solution.py:85
  229.2 28.5 %collective-permute-start.22 = (bf16[4,1,96,1536]{3,2,0,1:T(8,128)(2,1)}, bf16[4,1,96,1536]{3,2,0,1:T(8,128)(2,1)}, u32[]{:S(2)}, u32[]{:S(2)}) collective-permute-start(bf16[4,1,96,1536]{3,2,0,1:T(8,128)(2,1)} %add_convert_fusion.7), channel_id=1, source_target_pairs={{0,1},{1,0},{2,3},{3,2},{4,5},{5,4},{6,7},{7,6},{8,9},{9,8},{10,11... | collective-permute-start | bytes 3538952 | tf_op jit(solution)/shard_map/ppermute | solution.py:91
  230.9 28.0 %collective-permute-start.23 = (bf16[4,1,192,768]{3,2,0,1:T(8,128)(2,1)}, bf16[4,1,192,768]{3,2,0,1:T(8,128)(2,1)}, u32[]{:S(2)}, u32[]{:S(2)}) collective-permute-start(bf16[4,1,192,768]{3,2,0,1:T(8,128)(2,1)} %add_convert_fusion.6), channel_id=1, source_target_pairs={{0,16},{8,24},{16,0},{24,8},{1,17},{9,25},{17,1},{25,9},{2,18},{10... | collective-permute-start | bytes 3538952 | tf_op jit(solution)/shard_map/ppermute | solution.py:88
  266.2 26.8 %collective-permute-start.24 = (bf16[12,4,1,16,768]{4,3,0,1,2:T(8,128)(2,1)S(1)}, bf16[12,4,1,16,768]{4,3,0,1,2:T(8,128)(2,1)S(1)}, u32[]{:S(2)}, u32[]{:S(2)}) collective-permute-start(bf16[12,4,1,16,768]{4,3,0,1,2:T(8,128)(2,1)S(1)} %copy-done.21), channel_id=1, source_target_pairs={{0,1},{1,0},{2,3},{3,2},{4,5},{5,4},{6,7},{7,6},{8,9},{9,8},{10,11... | collective-permute-start | bytes 3538952 | tf_op jit(solution)/shard_map/ppermute | solution.py:91
  293.8 28.7 %collective-permute-start.33 = (bf16[2,768,768]{2,1,0:T(8,128)(2,1)S(1)}, bf16[2,768,768]{2,1,0:T(8,128)(2,1)S(1)}, u32[]{:S(2)}, u32[]{:S(2)}) collective-permute-start(bf16[2,768,768]{2,1,0:T(8,128)(2,1)S(1)} %pad_maximum_fusion.1), channel_id=1, source_target_pairs={{0,8},{8,0},{16,24},{24,16},{1,9},{9,1},{17,25},{25,17},{2,10},{10... | collective-permute-start | bytes 7077896 | tf_op jit(solution)/shard_map/ppermute | solution.py:85
  293.9 28.6 %collective-permute-start.29 = (bf16[12,4,1,16,768]{4,3,0,1,2:T(8,128)(2,1)S(1)}, bf16[12,4,1,16,768]{4,3,0,1,2:T(8,128)(2,1)S(1)}, u32[]{:S(2)}, u32[]{:S(2)}) collective-permute-start(bf16[12,4,1,16,768]{4,3,0,1,2:T(8,128)(2,1)S(1)} %constant_dynamic-slice_fusion.12), channel_id=1, source_target_pairs={{0,1},{1,0},{2,3},{3,2},{4,5},{5,4},{6,7},{7,6},{8,9},{9,8},{10,11... | collective-permute-start | bytes 3538952 | tf_op jit(solution)/shard_map/ppermute | solution.py:91
  296.4 24.7 %collective-permute-start.31 = (bf16[12,1,16,768]{3,2,0,1:T(8,128)(2,1)S(1)}, bf16[12,1,16,768]{3,2,0,1:T(8,128)(2,1)S(1)}, u32[]{:S(2)}, u32[]{:S(2)}) collective-permute-start(bf16[12,1,16,768]{3,2,0,1:T(8,128)(2,1)S(1)} %get-tuple-element.375), channel_id=1, source_target_pairs={{0,4},{1,5},{2,6},{3,7},{4,0},{5,1},{6,2},{7,3},{8,12},{9,13},{10,... | collective-permute-start | bytes 884744 | tf_op jit(solution)/shard_map/ppermute | solution.py:94
  296.4 24.7 %collective-permute-start.30 = (bf16[12,1,16,768]{3,2,0,1:T(8,128)(2,1)S(1)}, bf16[12,1,16,768]{3,2,0,1:T(8,128)(2,1)S(1)}, u32[]{:S(2)}, u32[]{:S(2)}) collective-permute-start(bf16[12,1,16,768]{3,2,0,1:T(8,128)(2,1)S(1)} %get-tuple-element.376), channel_id=1, source_target_pairs={{0,2},{1,3},{2,0},{3,1},{4,6},{5,7},{6,4},{7,5},{8,10},{9,11},{10,... | collective-permute-start | bytes 884744 | tf_op jit(solution)/shard_map/ppermute | solution.py:94
  325.4 27.9 %collective-permute-start.37 = (bf16[1,768,768]{2,1,0:T(8,128)(2,1)}, bf16[1,768,768]{2,1,0:T(8,128)(2,1)}, u32[]{:S(2)}, u32[]{:S(2)}) collective-permute-start(bf16[1,768,768]{2,1,0:T(8,128)(2,1)} %constant_dynamic-slice_fusion.8), channel_id=1, source_target_pairs={{0,16},{8,24},{16,0},{24,8},{1,17},{9,25},{17,1},{25,9},{2,18},{10... | collective-permute-start | bytes 3538952 | tf_op jit(solution)/shard_map/ppermute | solution.py:88
  327.5 20.2 %collective-permute-start.36 = (bf16[12,1,16,768]{3,2,0,1:T(8,128)(2,1)}, bf16[12,1,16,768]{3,2,0,1:T(8,128)(2,1)}, u32[]{:S(2)}, u32[]{:S(2)}) collective-permute-start(bf16[12,1,16,768]{3,2,0,1:T(8,128)(2,1)} %get-tuple-element.370), channel_id=1, source_target_pairs={{0,6},{1,7},{2,4},{3,5},{4,2},{5,3},{6,0},{7,1},{8,14},{9,15},{10,... | collective-permute-start | bytes 884744 | tf_op jit(solution)/shard_map/ppermute | solution.py:94
  329.1 24.2 %collective-permute-start.35 = (bf16[12,1,16,768]{3,2,0,1:T(8,128)(2,1)}, bf16[12,1,16,768]{3,2,0,1:T(8,128)(2,1)}, u32[]{:S(2)}, u32[]{:S(2)}) collective-permute-start(bf16[12,1,16,768]{3,2,0,1:T(8,128)(2,1)} %get-tuple-element.371), channel_id=1, source_target_pairs={{0,4},{1,5},{2,6},{3,7},{4,0},{5,1},{6,2},{7,3},{8,12},{9,13},{10,... | collective-permute-start | bytes 884744 | tf_op jit(solution)/shard_map/ppermute | solution.py:94
  329.1 24.2 %collective-permute-start.34 = (bf16[12,1,16,768]{3,2,0,1:T(8,128)(2,1)}, bf16[12,1,16,768]{3,2,0,1:T(8,128)(2,1)}, u32[]{:S(2)}, u32[]{:S(2)}) collective-permute-start(bf16[12,1,16,768]{3,2,0,1:T(8,128)(2,1)} %get-tuple-element.372), channel_id=1, source_target_pairs={{0,2},{1,3},{2,0},{3,1},{4,6},{5,7},{6,4},{7,5},{8,10},{9,11},{10,... | collective-permute-start | bytes 884744 | tf_op jit(solution)/shard_map/ppermute | solution.py:94
  331.9 21.3 %collective-permute-start.38 = (bf16[1,1,192,768]{3,2,1,0:T(8,128)(2,1)S(1)}, bf16[1,1,192,768]{3,2,1,0:T(8,128)(2,1)S(1)}, u32[]{:S(2)}, u32[]{:S(2)}) collective-permute-start(bf16[1,1,192,768]{3,2,1,0:T(8,128)(2,1)S(1)} %get-tuple-element.287), channel_id=1, source_target_pairs={{0,1},{1,0},{2,3},{3,2},{4,5},{5,4},{6,7},{7,6},{8,9},{9,8},{10,11... | collective-permute-start | bytes 884744 | tf_op jit(solution)/shard_map/ppermute | solution.py:91
  384.7 27.2 %collective-permute-start.45 = (bf16[1,192,768]{2,1,0:T(8,128)(2,1)}, bf16[1,192,768]{2,1,0:T(8,128)(2,1)}, u32[]{:S(2)}, u32[]{:S(2)}) collective-permute-start(bf16[1,192,768]{2,1,0:T(8,128)(2,1)} %get-tuple-element.367), channel_id=1, source_target_pairs={{0,4},{1,5},{2,6},{3,7},{4,0},{5,1},{6,2},{7,3},{8,12},{9,13},{10,... | collective-permute-start | bytes 884744 | tf_op jit(solution)/shard_map/ppermute | solution.py:94
  385.8 26.1 %collective-permute-start.44 = (bf16[1,192,768]{2,1,0:T(8,128)(2,1)}, bf16[1,192,768]{2,1,0:T(8,128)(2,1)}, u32[]{:S(2)}, u32[]{:S(2)}) collective-permute-start(bf16[1,192,768]{2,1,0:T(8,128)(2,1)} %get-tuple-element.368), channel_id=1, source_target_pairs={{0,2},{1,3},{2,0},{3,1},{4,6},{5,7},{6,4},{7,5},{8,10},{9,11},{10,... | collective-permute-start | bytes 884744 | tf_op jit(solution)/shard_map/ppermute | solution.py:94
  387.8 27.1 %collective-permute-start.47 = (bf16[192,768]{1,0:T(8,128)(2,1)S(1)}, bf16[192,768]{1,0:T(8,128)(2,1)S(1)}, u32[]{:S(2)}, u32[]{:S(2)}) collective-permute-start(bf16[192,768]{1,0:T(8,128)(2,1)S(1)} %fusion.22), channel_id=1, source_target_pairs={{4,0},{5,1},{6,2},{7,3},{8,12},{9,13},{10,14},{11,15},{20,16},{21,... | collective-permute-start | bytes 884744 | tf_op jit(solution)/shard_map/ppermute | solution.py:110
  (76 other events, 597.0 us)
Sparse Core Ops, SparseCore 0:
  11.5 120.7 all-gather.2

commit v4 on v3

--- a/solution.py
+++ b/solution.py
@@ -234,26 +234,48 @@
     return lax.dot_general(one, two, (((0,), (0,)), ((), ())), preferred_element_type=jnp.float32)
 
 
-def embed_body(part_ref, pixel_ref, kernel_ref, norm_ref, start_ref, hidden_ref):
+def embed_body(side_ref, part_ref, pixel_ref, own_ref, other_ref, norm_ref, *refs):
+    start_ref, hidden_ref, kernel_ref = refs
+    bands, line, pixels, width = own_ref.shape
+
+    def fill(refs):
+        for band in range(bands):
+            for place in range(line):
+                for side in range(2):
+                    at = ((band * line + place) * 2 + side) * pixels
+                    kernel_ref[at : at + pixels, :] = refs[side][band, place]
+
+    first = pl.program_id(0) == 0
+    pl.when(first & (side_ref[0] == 0))(lambda: fill((own_ref, other_ref)))
+    pl.when(first & (side_ref[0] == 1))(lambda: fill((other_ref, own_ref)))
     start = part_ref[...] + dot_nn(pixel_ref[...], kernel_ref[...])
     start_ref[...] = start
     normed, _ = norm_rows(start, 1e-06)
     hidden_ref[...] = (normed * norm_ref[0:1, :] + norm_ref[1:2, :]).astype(jnp.bfloat16)
 
 
-def embed_rows(part, pixel_rows, wide_kernel, norm_one, block_rows):
-    rows = part.shape[0]
-    depth = wide_kernel.shape[0]
+def embed_rows(side, part, pixel_rows, own, other, norm_one, block_rows):
+    rows, width = part.shape
+    bands, line, _, pixels, _ = own.shape
+    if pixels % 16:
+        wide = pair_up(own, other, side, 2)
+        side = jnp.zeros_like(side)
+        own, other = jnp.split(wide.reshape(bands, 2, -1, width), 2, 1)
+        bands, line, pixels = bands, 1, own.shape[2]
+    own = own.reshape(bands, line, pixels, width)
+    other = other.reshape(own.shape)
+    depth = bands * line * 2 * pixels
     last = pixel_rows.shape[1] // depth - 1
-    width = wide_kernel.shape[1]
     row_spec = lambda cols: pl.BlockSpec((block_rows, cols), lambda i: (i, 0))
     return pl.pallas_call(
         embed_body,
         grid=(rows // block_rows,),
         in_specs=[
+            pl.BlockSpec(memory_space=pltpu.SMEM),
             row_spec(width),
             pl.BlockSpec((block_rows, depth), lambda i: (i, last)),
-            whole_spec(wide_kernel.shape),
+            whole_spec(own.shape),
+            whole_spec(own.shape),
             whole_spec(norm_one.shape),
         ],
         out_specs=[row_spec(width), row_spec(width)],
@@ -261,10 +283,11 @@
             jax.ShapeDtypeStruct((rows, width), jnp.float32),
             jax.ShapeDtypeStruct((rows, width), jnp.bfloat16),
         ],
+        scratch_shapes=[pltpu.VMEM((depth, width), jnp.bfloat16)],
         compiler_params=kernel_params(),
         cost_estimate=pl.CostEstimate(flops=0, bytes_accessed=0, transcendentals=0),
         name="embed_rows",
-    )(part, pixel_rows, wide_kernel, norm_one)
+    )(side.reshape(1), part, pixel_rows, own, other, norm_one)
 
 
 def pixel_grad_body(grad_ref, kernel_ref, out_ref):
@@ -1246,7 +1269,13 @@
     gains = widen(norm_gains)
     shifts = widen(norm_shifts)
     start, hidden_one = embed_rows(
-        embed_part, pixel_rows, kernel_three, jnp.stack([gains[0], shifts[0]]), 256
+        links.x,
+        embed_part,
+        pixel_rows,
+        line_three,
+        other_three,
+        jnp.stack([gains[0], shifts[0]]),
+        256,
     )
     bias_full = jnp.concatenate(
         [widen(attention_bias[0]), jnp.zeros((model_width,), floaty), widen(attention_bias[1])]
@@ -1459,8 +1488,13 @@
         bias_weight,
     )
     kernel_all = pair_up(kernel_low[None], other_low[None], links.y, 0)[:, None]
-    both, other_down, key_grad, kernel_all, small = stage(
-        both, other_down, key_grad, kernel_all, small
+    token_count = weight_tokens.shape[0]
+    token_grad = key_grad[:token_count]
+    bias_token_grad = key_grad[token_count + wave_count]
+    small_parts = [small[0:2], small[2:4], small[4:6], small[6], small[8:].reshape(-1), small[7]]
+    bias_shift_grad = bias_shift_grad.reshape(-1)
+    both, other_down, token_grad, bias_token_grad, bias_shift_grad, kernel_all, small_parts = stage(
+        both, other_down, token_grad, bias_token_grad, bias_shift_grad, kernel_all, small_parts
     )
     both = jnp.concatenate([add_low(*both), add_low(down_sum, other_down)], 0)[None]
 
@@ -1471,7 +1505,6 @@
     kernel_all = kernel_all.reshape((wave_count,) + kernel_low.shape[1:])
     weight_shard_grad = weight_grad(table_all, kernel_all)
     bias_shard_grad = scaler * jnp.sum(kernel_all.astype(floaty), 0)
-    token_count = weight_tokens.shape[0]
     other_both, weight_shard_grad, bias_shard_grad = stage(
         other_both, weight_shard_grad, bias_shard_grad
     )
@@ -1495,20 +1528,15 @@
     return (
         encoded,
         pixel_grad,
-        key_grad[:token_count],
-        key_grad[token_count + wave_count],
+        token_grad,
+        bias_token_grad,
         *param_grads,
         weight_shard_grad,
         bias_shard_grad,
         bias_weight_grad,
-        bias_shift_grad.reshape(-1),
+        bias_shift_grad,
         *block_shards,
-        small[0:2],
-        small[2:4],
-        small[4:6],
-        small[6],
-        small[8:].reshape(-1),
-        small[7],
+        *small_parts,
     )
 
 

time: 458 us -> 461 us (level)
  waiting for transfers between devices: 129 us -> 116 us
  starting transfers between devices: 60.6 us -> 67.7 us
  local copies, waits for them, and re-layouts: 40.9 us -> 47.7 us
    ppermute x26, waiting for transfers between devices: 101 us -> 85.9 us  [zside(): lax.ppermute(block, 'dp', [(i, i ^ step) for i in range(self.dp_size)])]
    ppermute x26, starting transfers between devices: 35.6 us -> 40.7 us  [zside(): lax.ppermute(block, 'dp', [(i, i ^ step) for i in range(self.dp_size)])]
    unnamed x105 -> x107, local copies, waits for them, and re-layouts: 11 us -> 14.2 us
  transfers between devices with their start and end apart: 55 -> 55, of which waited for: 26 -> 24; matrix products, arithmetic and copies ran while one was open for 18% -> 19% of each run, Pallas kernels for 25% -> 25%
where the time goes in v4:
time: 461 us; the launch traced here: 455 us
  Pallas kernels  140 us (30%)
  waiting for transfers between devices  116 us (25%)
  starting transfers between devices  67.7 us (15%)
  other arithmetic  48.1 us (10%)
  local copies, waits for them, and re-layouts  47.7 us (10%)
  matrix products  19.2 us (4%)
  between operations  15.7 us (3%)
    ppermute x26, waiting for transfers between devices, zside(): lax.ppermute(block, 'dp', [(i, i ^ step) for i in range(self.dp_size)])  85.9 us
    pallas_call x2, Pallas kernels, expand_call(): pl.pallas_call(body, grid_spec=pltpu.PrefetchScalarGridSpec(num_scalar_pr...  41.3 us
    ppermute x26, starting transfers between devices, zside(): lax.ppermute(block, 'dp', [(i, i ^ step) for i in range(self.dp_size)])  40.7 us
    ppermute x10, waiting for transfers between devices, xside(): return lax.ppermute(block, 'dp', [(i, i ^ 1) for i in range(self.dp_size)])  17.5 us
    pallas_call x1, Pallas kernels, attend_back(): pl.pallas_call(attend_back_body, grid_spec=pltpu.PrefetchScalarGridSpec(n...  16.4 us
    convert_element_type x12, other arithmetic, add_low(): return total.astype(jnp.bfloat16)  15.5 us
    pallas_call x1, Pallas kernels, attend_rows(): pl.pallas_call(body, grid_spec=pltpu.PrefetchScalarGridSpec(num_scalar_pr...  15.5 us
    unnamed x107, local copies, waits for them, and re-layouts  14.2 us
  transfers between devices with their start and end apart: 55, of which 24 were waited for; matrix products, arithmetic and copies ran while one was open for 19% of the time, Pallas kernels for 25%

profile of v4, /device:TPU:0, one launch (start us, length us, event | category | flops | bytes accessed | tf_op | source)
XLA Modules:
  0.0 455.2 jit_solution(13122993141044028985)
XLA Ops:
  10.4 4.1 collective-permute-start.1
  17.1 5.2 %hyper_forward.2 = f32[16,128]{1,0:T(8,128)} custom-call(f32[16,144]{1,0:T(8,128)} %constant.166.clone.refs_0_, f32[16,144]{1,0:T(8,128)} %constant.167.clone.refs_1_, f32[144,128]{1,0:T(8,128)} %maximum_maximum_fusion.1.refs_2_, bf16[128,384]{1,0:T(8,128)(2,1)} %refs_0_.3, bf16[128,128]{1,0:T(8,128)(2,1)} %refs_1_.3, bf16[2,128]{1,0:T(2,128)(2,1)} %refs_2_.1, ...), custom_call_target="tpu_custom_call" | custom-call | tf_op jit(solution)/shard_map/hyper_forward/pallas_call | solution.py:876
  25.8 6.6 %make_kernel.1 = bf16[12,32,768]{2,1,0:T(8,128)(2,1)} custom-call(bf16[24,128]{1,0:T(8,128)(2,1)} %pad_maximum_fusion.10.feats_ref, bf16[128,32,768]{2,1,0:T(8,128)(2,1)} %weight_ref.5, bf16[32,768]{1,0:T(8,128)(2,1)} %bias_ref.1), custom_call_target="tpu_custom_call" | custom-call | tf_op jit(solution)/shard_map/make_kernel/pallas_call | solution.py:993
  33.8 3.9 collective-permute-start.5
  43.0 13.8 %collective-permute-done.3 = bf16[4,1,1,32,768]{4,3,1,0,2:T(8,128)(2,1)S(1)} collective-permute-done((bf16[4,1,1,32,768]{4,3,1,0,2:T(8,128)(2,1)S(1)}, bf16[4,1,1,32,768]{4,3,1,0,2:T(8,128)(2,1)S(1)}, u32[]{:S(2)}, u32[]{:S(2)}) %collective-permute-start.3) | collective-permute-done | bytes 196640 | tf_op jit(solution)/shard_map/ppermute | solution.py:94
  56.9 5.7 %collective-permute-done.4 = bf16[4,1,1,32,768]{4,3,1,0,2:T(8,128)(2,1)S(1)} collective-permute-done((bf16[4,1,1,32,768]{4,3,1,0,2:T(8,128)(2,1)S(1)}, bf16[4,1,1,32,768]{4,3,1,0,2:T(8,128)(2,1)S(1)}, u32[]{:S(2)}, u32[]{:S(2)}) %collective-permute-start.4) | collective-permute-done | bytes 196640 | tf_op jit(solution)/shard_map/ppermute | solution.py:94
  66.6 3.9 collective-permute-start.9
  74.0 5.8 %copy.105 = bf16[1,12,64,12,256]{4,3,2,1,0:T(8,128)(2,1)S(1)} copy(bf16[1,12,64,12,256]{4,2,3,1,0:T(8,128)(2,1)} %param.31) | data formatting | bytes 9437184 | tf_op jit(solution)/shard_map/optimization_barrier | solution.py:63
  79.8 5.5 %copy.137 = bf16[96,8,12,256]{3,1,2,0:T(8,128)(2,1)} copy(bf16[96,8,12,256]{3,2,1,0:T(8,128)(2,1)S(1)} %bitcast.150) | data formatting | bytes 9437184
  85.4 16.2 %collective-permute-done.10 = bf16[4,1,1,32,768]{4,3,1,0,2:T(8,128)(2,1)S(1)} collective-permute-done((bf16[4,1,1,32,768]{4,3,1,0,2:T(8,128)(2,1)S(1)}, bf16[4,1,1,32,768]{4,3,1,0,2:T(8,128)(2,1)S(1)}, u32[]{:S(2)}, u32[]{:S(2)}) %collective-permute-start.10) | collective-permute-done | bytes 196640 | tf_op jit(solution)/shard_map/ppermute | solution.py:94
  101.7 4.8 %collective-permute-done.13 = bf16[4,2,1,1,96,768]{5,4,2,1,0,3:T(8,128)(2,1)} collective-permute-done((bf16[4,2,1,1,96,768]{5,4,2,1,0,3:T(8,128)(2,1)S(1)}, bf16[4,2,1,1,96,768]{5,4,2,1,0,3:T(8,128)(2,1)}, u32[]{:S(2)}, u32[]{:S(2)}) %collective-permute-start.13) | collective-permute-done | bytes 1179680 | tf_op jit(solution)/shard_map/ppermute | solution.py:88
  122.7 4.2 fusion.4
  135.8 4.0 collective-permute-done.17
  143.1 5.7 %hyper_forward.3 = f32[56,128]{1,0:T(8,128)} custom-call(f32[56,192]{1,0:T(8,128)} %constant.168.clone.refs_0_.pick_ref, f32[56,192]{1,0:T(8,128)} %constant.169.clone.refs_1_.mask_ref, f32[192,128]{1,0:T(8,128)} %maximum_maximum_fusion.refs_2_.key_ref, bf16[128,384]{1,0:T(8,128)(2,1)} %refs_0_.3, bf16[128,128]{1,0:T(8,128)(2,1)} %refs_1_.3, ...), custom_call_target="tpu_custom_call" | custom-call | tf_op jit(solution)/shard_map/hyper_forward/pallas_call | solution.py:876
  160.3 5.7 %embed_rows.1 = (f32[768,768]{1,0:T(8,128)}, bf16[768,768]{1,0:T(8,128)(2,1)}) custom-call(s32[1]{0:T(128)} %bitcast.2.side_ref, f32[768,768]{1,0:T(8,128)} %add.271.part_ref, bf16[768,3072]{1,0:T(8,128)(2,1)} %bitcast.155, bf16[4,4,32,768]{3,2,1,0:T(8,128)(2,1)} %bitcast.22.own_ref, bf16[4,4,32,768]{3,2,1,0:T(8,128)(2,1)} %bitcast.169, ...), custom_call_target="tpu_custom_call" | custom-call | tf_op jit(solution)/shard_map/embed_rows/pallas_call | solution.py:270
  166.0 15.5 %attend_rows.1 = (bf16[768,2304]{1,0:T(8,128)(2,1)}, bf16[768,768]{1,0:T(8,128)(2,1)}, bf16[768,768]{1,0:T(8,128)(2,1)}, f32[768,768]{1,0:T(8,128)}, bf16[768,768]{1,0:T(8,128)(2,1)}) custom-call(s32[13]{0:T(128)} %pad_add_fusion.count_ref, bf16[768,768]{1,0:T(8,128)(2,1)} %get-tuple-element.227.refs_0_, f32[768,768]{1,0:T(8,128)} %get-tuple-element.228.refs_1_.start_ref, ...), custom_call_target="tpu_custom_call" | custom-call | tf_op jit(solution)/shard_map/attend_rows/pallas_call | solution.py:418
  181.5 18.6 %expand_first.1 = (bf16[768,1536]{1,0:T(8,128)(2,1)}, bf16[1536,768]{1,0:T(8,128)(2,1)}, f32[1,1536]{1,0:T(1,128)}, f32[768,768]{1,0:T(8,128)}, f32[768,768]{1,0:T(8,128)}) custom-call(s32[1]{0:T(128)} %bitcast.30.half_ref, bf16[768,768]{1,0:T(8,128)(2,1)} %get-tuple-element.230.hidden_ref, bf16[768,768]{1,0:T(8,128)(2,1)} %bitcast_multiply_fusion.out_ref, ...), custom_call_target="tpu_custom_call" | custom-call | tf_op jit(solution)/shard_map/expand_first/pallas_call | solution.py:587
  202.4 22.7 %expand_second.1 = (bf16[768,1536]{1,0:T(8,128)(2,1)}, bf16[1536,768]{1,0:T(8,128)(2,1)}, f32[1,1536]{1,0:T(1,128)}, bf16[768,768]{1,0:T(8,128)(2,1)}, f32[768,7...) custom-call(s32[1]{0:T(128)} %bitcast.half_ref, bf16[768,768]{1,0:T(8,128)(2,1)} %get-tuple-element.230.hidden_ref, ...), custom_call_target="tpu_custom_call" | custom-call | tf_op jit(solution)/shard_map/expand_second/pallas_call | solution.py:587
  235.4 16.4 %attend_back.1 = (bf16[768,2304]{1,0:T(8,128)(2,1)}, bf16[768,768]{1,0:T(8,128)(2,1)}, f32[3,768]{1,0:T(4,128)}, f32[1,2304]{1,0:T(1,128)}) custom-call(s32[13]{0:T(128)} %pad_add_fusion.count_ref, bf16[768,2304]{1,0:T(8,128)(2,1)} %get-tuple-element.251.project_ref, bf16[768,768]{1,0:T(8,128)(2,1)} %get-tuple-element.252.probs_ref, ...), custom_call_target="tpu_custom_call" | custom-call | tf_op jit(solution)/shard_map/attend_back/pallas_call | solution.py:786
  251.8 6.6 %convolution_convert_fusion = bf16[3072,768]{1,0:T(8,128)(2,1)S(1)} fusion(bf16[768,3072]{1,0:T(8,128)(2,1)} %bitcast.156, bf16[768,768]{1,0:T(8,128)(2,1)} %get-tuple-element.299.grad_ref), kind=kOutput, calls=%fused_computation | convolution fusion | flops 3626237952 | bytes 10616832 | tf_op jit(solution)/shard_map/dot_general | solution.py:21
  280.2 6.8 %collective-permute-done.28 = f32[13,768]{1,0:T(8,128)S(1)} collective-permute-done((f32[13,768]{1,0:T(8,128)S(1)}, f32[13,768]{1,0:T(8,128)S(1)}, u32[]{:S(2)}, u32[]{:S(2)}) %collective-permute-start.28) | collective-permute-done | bytes 39968 | tf_op jit(solution)/shard_map/ppermute | solution.py:94
  288.5 8.1 %collective-permute-done.24 = bf16[12,4,1,16,768]{4,3,0,1,2:T(8,128)(2,1)S(1)} collective-permute-done((bf16[12,4,1,16,768]{4,3,0,1,2:T(8,128)(2,1)S(1)}, bf16[12,4,1,16,768]{4,3,0,1,2:T(8,128)(2,1)S(1)}, u32[]{:S(2)}, u32[]{:S(2)}) %collective-permute-start.24) | collective-permute-done | bytes 1179680 | tf_op jit(solution)/shard_map/ppermute | solution.py:91
  303.1 7.1 %collective-permute-done.32 = bf16[12,1,16,768]{3,2,0,1:T(8,128)(2,1)S(1)} collective-permute-done((bf16[12,1,16,768]{3,2,0,1:T(8,128)(2,1)S(1)}, bf16[12,1,16,768]{3,2,0,1:T(8,128)(2,1)S(1)}, u32[]{:S(2)}, u32[]{:S(2)}) %collective-permute-start.32) | collective-permute-done | bytes 294944 | tf_op jit(solution)/shard_map/ppermute | solution.py:94
  310.2 17.0 %collective-permute-done.31 = bf16[12,1,16,768]{3,2,0,1:T(8,128)(2,1)S(1)} collective-permute-done((bf16[12,1,16,768]{3,2,0,1:T(8,128)(2,1)S(1)}, bf16[12,1,16,768]{3,2,0,1:T(8,128)(2,1)S(1)}, u32[]{:S(2)}, u32[]{:S(2)}) %collective-permute-start.31) | collective-permute-done | bytes 294944 | tf_op jit(solution)/shard_map/ppermute | solution.py:94
  343.0 4.3 feats_piece.2
  347.3 7.9 %pixel_gradient.1 = bf16[12,12,64,256]{3,2,1,0:T(8,128)(2,1)} custom-call(bf16[768,768]{1,0:T(8,128)(2,1)} %get-tuple-element.299.grad_ref, bf16[3072,768]{1,0:T(8,128)(2,1)} %pad_maximum_fusion.kernel_ref), custom_call_target="tpu_custom_call" | custom-call | tf_op jit(solution)/shard_map/pixel_gradient/pallas_call | solution.py:305
  355.2 5.9 %collective-permute-done.35 = bf16[12,1,16,768]{3,2,0,1:T(8,128)(2,1)} collective-permute-done((bf16[12,1,16,768]{3,2,0,1:T(8,128)(2,1)}, bf16[12,1,16,768]{3,2,0,1:T(8,128)(2,1)}, u32[]{:S(2)}, u32[]{:S(2)}) %collective-permute-start.35) | collective-permute-done | bytes 294944 | tf_op jit(solution)/shard_map/ppermute | solution.py:94
  363.2 4.3 feats_piece.3
  382.2 4.7 %collective-permute-done.42 = bf16[4,1,96,768]{3,2,0,1:T(8,128)(2,1)} collective-permute-done((bf16[4,1,96,768]{3,2,0,1:T(8,128)(2,1)}, bf16[4,1,96,768]{3,2,0,1:T(8,128)(2,1)}, u32[]{:S(2)}, u32[]{:S(2)}) %collective-permute-start.42) | collective-permute-done | bytes 589856 | tf_op jit(solution)/shard_map/ppermute | solution.py:91
  401.9 8.5 %hyper_backward.1 = (f32[192,128]{1,0:T(8,128)}, f32[128,384]{1,0:T(8,128)}, f32[128,128]{1,0:T(8,128)}, f32[2,128]{1,0:T(2,128)}, f32[2,128]{1,0:T(2,128)}, /*i...) custom-call(f32[56,192]{1,0:T(8,128)} %constant.168.clone.refs_0_.pick_ref, ...), custom_call_target="tpu_custom_call" | custom-call | tf_op jit(solution)/shard_map/hyper_backward/pallas_call | solution.py:907
  414.3 4.7 %collective-permute-done.45 = bf16[1,192,768]{2,1,0:T(8,128)(2,1)S(1)} collective-permute-done((bf16[1,192,768]{2,1,0:T(8,128)(2,1)}, bf16[1,192,768]{2,1,0:T(8,128)(2,1)S(1)}, u32[]{:S(2)}, u32[]{:S(2)}) %collective-permute-start.45) | collective-permute-done | bytes 294944 | tf_op jit(solution)/shard_map/ppermute | solution.py:94
  428.1 11.5 %weight_grad.1 = f32[128,32,768]{2,1,0:T(8,128)} custom-call(bf16[2048,768]{1,0:T(8,128)(2,1)} %weight_table.1.table_ref, bf16[48,32,768]{2,1,0:T(8,128)(2,1)} %bitcast.157), custom_call_target="tpu_custom_call" | custom-call | tf_op jit(solution)/shard_map/weight_grad/pallas_call | solution.py:1041
  (382 shorter events, 173.9 us)
Async XLA Ops:
  7.2 174.3 %all-gather.3.cloned.1.call-start = ((), (), s32[]{:S(2)}) async-start(), calls=%async_computation | async-start | bytes 9732096 | tf_op jit(solution)/shard_map/all_gather | solution.py:184
  10.4 22.2 %collective-permute-start.1 = (bf16[1,1,1,1,96,768]{5,4,2,1,0,3:T(8,128)(2,1)S(1)}, bf16[1,1,1,1,96,768]{5,4,2,1,0,3:T(8,128)(2,1)S(1)}, u32[]{:S(2)}, u32[]{:S(2)}) collective-permute-start(bf16[1,1,1,1,96,768]{5,4,2,1,0,3:T(8,128)(2,1)S(1)} %get-tuple-element.371), channel_id=1, source_target_pairs={{0,4},{1,5},{2,6},{3,7},{4,0},{5,1},{6,2},{7,3},{8,12},{9,13},{10,... | collective-permute-start | bytes 442376 | tf_op jit(solution)/shard_map/ppermute | solution.py:94
  33.8 28.8 %collective-permute-start.5 = (bf16[4,1,1,32,768]{4,3,1,0,2:T(8,128)(2,1)S(1)}, bf16[4,1,1,32,768]{4,3,1,0,2:T(8,128)(2,1)S(1)}, u32[]{:S(2)}, u32[]{:S(2)}) collective-permute-start(bf16[4,1,1,32,768]{4,3,1,0,2:T(8,128)(2,1)S(1)} %get-tuple-element.398), channel_id=1, source_target_pairs={{0,6},{1,7},{2,4},{3,5},{4,2},{5,3},{6,0},{7,1},{8,14},{9,15},{10,... | collective-permute-start | bytes 589832 | tf_op jit(solution)/shard_map/ppermute | solution.py:94
  37.7 24.9 %collective-permute-start.4 = (bf16[4,1,1,32,768]{4,3,1,0,2:T(8,128)(2,1)S(1)}, bf16[4,1,1,32,768]{4,3,1,0,2:T(8,128)(2,1)S(1)}, u32[]{:S(2)}, u32[]{:S(2)}) collective-permute-start(bf16[4,1,1,32,768]{4,3,1,0,2:T(8,128)(2,1)S(1)} %get-tuple-element.398), channel_id=1, source_target_pairs={{0,4},{1,5},{2,6},{3,7},{4,0},{5,1},{6,2},{7,3},{8,12},{9,13},{10,... | collective-permute-start | bytes 589832 | tf_op jit(solution)/shard_map/ppermute | solution.py:94
  37.7 19.2 %collective-permute-start.3 = (bf16[4,1,1,32,768]{4,3,1,0,2:T(8,128)(2,1)S(1)}, bf16[4,1,1,32,768]{4,3,1,0,2:T(8,128)(2,1)S(1)}, u32[]{:S(2)}, u32[]{:S(2)}) collective-permute-start(bf16[4,1,1,32,768]{4,3,1,0,2:T(8,128)(2,1)S(1)} %get-tuple-element.398), channel_id=1, source_target_pairs={{0,2},{1,3},{2,0},{3,1},{4,6},{5,7},{6,4},{7,5},{8,10},{9,11},{10,... | collective-permute-start | bytes 589832 | tf_op jit(solution)/shard_map/ppermute | solution.py:94
  40.0 22.7 %collective-permute-start.6 = (bf16[4,1,1,1,96,768]{5,4,2,1,0,3:T(8,128)(2,1)S(1)}, bf16[4,1,1,1,96,768]{5,4,2,1,0,3:T(8,128)(2,1)S(1)}, u32[]{:S(2)}, u32[]{:S(2)}) collective-permute-start(bf16[4,1,1,1,96,768]{5,4,2,1,0,3:T(8,128)(2,1)S(1)} %constant_dynamic-update-slice_fusion.12), channel_id=1, source_target_pairs={{0,1},{1,0},{2,3},{3,2},{4,5},{5,4},{6,7},{7,6},{8,9},{9,8},{10,11... | collective-permute-start | bytes 1769480 | tf_op jit(solution)/shard_map/ppermute | solution.py:91
  62.8 43.7 %collective-permute-start.13 = (bf16[4,2,1,1,96,768]{5,4,2,1,0,3:T(8,128)(2,1)S(1)}, bf16[4,2,1,1,96,768]{5,4,2,1,0,3:T(8,128)(2,1)}, u32[]{:S(2)}, u32[]{:S(2)}) collective-permute-start(bf16[4,2,1,1,96,768]{5,4,2,1,0,3:T(8,128)(2,1)S(1)} %maximum_select_fusion.5), channel_id=1, source_target_pairs={{0,16},{8,24},{16,0},{24,8},{1,17},{9,25},{17,1},{25,9},{2,18},{10... | collective-permute-start | bytes 3538952 | tf_op jit(solution)/shard_map/ppermute | solution.py:88
  64.7 37.0 %collective-permute-start.12 = (bf16[4,4,1,32,768]{4,3,1,0,2:T(8,128)(2,1)S(1)}, bf16[4,4,1,32,768]{4,3,1,0,2:T(8,128)(2,1)S(1)}, u32[]{:S(2)}, u32[]{:S(2)}) collective-permute-start(bf16[4,4,1,32,768]{4,3,1,0,2:T(8,128)(2,1)S(1)} %constant_dynamic-update-slice_fusion.8), channel_id=1, source_target_pairs={{0,1},{1,0},{2,3},{3,2},{4,5},{5,4},{6,7},{7,6},{8,9},{9,8},{10,11... | collective-permute-start | bytes 2359304 | tf_op jit(solution)/shard_map/ppermute | solution.py:91
  70.5 31.2 %collective-permute-start.11 = (bf16[4,1,1,32,768]{4,3,1,0,2:T(8,128)(2,1)S(1)}, bf16[4,1,1,32,768]{4,3,1,0,2:T(8,128)(2,1)S(1)}, u32[]{:S(2)}, u32[]{:S(2)}) collective-permute-start(bf16[4,1,1,32,768]{4,3,1,0,2:T(8,128)(2,1)S(1)} %get-tuple-element.200), channel_id=1, source_target_pairs={{0,6},{1,7},{2,4},{3,5},{4,2},{5,3},{6,0},{7,1},{8,14},{9,15},{10,... | collective-permute-start | bytes 589832 | tf_op jit(solution)/shard_map/ppermute | solution.py:94
  73.4 28.2 %collective-permute-start.10 = (bf16[4,1,1,32,768]{4,3,1,0,2:T(8,128)(2,1)S(1)}, bf16[4,1,1,32,768]{4,3,1,0,2:T(8,128)(2,1)S(1)}, u32[]{:S(2)}, u32[]{:S(2)}) collective-permute-start(bf16[4,1,1,32,768]{4,3,1,0,2:T(8,128)(2,1)S(1)} %get-tuple-element.200), channel_id=1, source_target_pairs={{0,4},{1,5},{2,6},{3,7},{4,0},{5,1},{6,2},{7,3},{8,12},{9,13},{10,... | collective-permute-start | bytes 589832 | tf_op jit(solution)/shard_map/ppermute | solution.py:94
  110.7 29.1 %collective-permute-start.18 = (bf16[4,2,2,1,96,768]{5,4,2,1,0,3:T(8,128)(2,1)S(1)}, bf16[4,2,2,1,96,768]{5,4,2,1,0,3:T(8,128)(2,1)}, u32[]{:S(2)}, u32[]{:S(2)}) collective-permute-start(bf16[4,2,2,1,96,768]{5,4,2,1,0,3:T(8,128)(2,1)S(1)} %maximum_select_fusion), channel_id=1, source_target_pairs={{0,8},{8,0},{16,24},{24,16},{1,9},{9,1},{17,25},{25,17},{2,10},{10... | collective-permute-start | bytes 7077896 | tf_op jit(solution)/shard_map/ppermute | solution.py:85
  115.3 19.8 %collective-permute-start.16 = (bf16[4,1,1,32,768]{4,3,1,0,2:T(8,128)(2,1)S(1)}, bf16[4,1,1,32,768]{4,3,1,0,2:T(8,128)(2,1)S(1)}, u32[]{:S(2)}, u32[]{:S(2)}) collective-permute-start(bf16[4,1,1,32,768]{4,3,1,0,2:T(8,128)(2,1)S(1)} %get-tuple-element.211), channel_id=1, source_target_pairs={{0,6},{1,7},{2,4},{3,5},{4,2},{5,3},{6,0},{7,1},{8,14},{9,15},{10,... | collective-permute-start | bytes 589832 | tf_op jit(solution)/shard_map/ppermute | solution.py:94
  119.9 19.9 %collective-permute-start.17 = (bf16[4,4,1,32,768]{4,3,1,0,2:T(8,128)(2,1)}, bf16[4,4,1,32,768]{4,3,1,0,2:T(8,128)(2,1)S(1)}, u32[]{:S(2)}, u32[]{:S(2)}) collective-permute-start(bf16[4,4,1,32,768]{4,3,1,0,2:T(8,128)(2,1)} %copy-done.15), channel_id=1, source_target_pairs={{0,1},{1,0},{2,3},{3,2},{4,5},{5,4},{6,7},{7,6},{8,9},{9,8},{10,11... | collective-permute-start | bytes 2359304 | tf_op jit(solution)/shard_map/ppermute | solution.py:91
  140.4 19.0 %collective-permute-start.19 = (bf16[4,4,1,32,768]{4,3,1,0,2:T(8,128)(2,1)}, bf16[4,4,1,32,768]{4,3,1,0,2:T(8,128)(2,1)S(1)}, u32[]{:S(2)}, u32[]{:S(2)}) collective-permute-start(bf16[4,4,1,32,768]{4,3,1,0,2:T(8,128)(2,1)} %constant_dynamic-update-slice_fusion), channel_id=1, source_target_pairs={{0,1},{1,0},{2,3},{3,2},{4,5},{5,4},{6,7},{7,6},{8,9},{9,8},{10,11... | collective-permute-start | bytes 2359304 | tf_op jit(solution)/shard_map/ppermute | solution.py:91
  200.1 27.3 %collective-permute-start.20 = (bf16[768,1536]{1,0:T(8,128)(2,1)}, bf16[768,1536]{1,0:T(8,128)(2,1)}, u32[]{:S(2)}, u32[]{:S(2)}) collective-permute-start(bf16[768,1536]{1,0:T(8,128)(2,1)} %get-tuple-element.239), channel_id=1, source_target_pairs={{0,8},{8,0},{16,24},{24,16},{1,9},{9,1},{17,25},{25,17},{2,10},{10... | collective-permute-start | bytes 7077896 | tf_op jit(solution)/shard_map/ppermute | solution.py:85
  200.2 27.2 %collective-permute-start.21 = (bf16[1536,768]{1,0:T(8,128)(2,1)}, bf16[1536,768]{1,0:T(8,128)(2,1)S(1)}, u32[]{:S(2)}, u32[]{:S(2)}) collective-permute-start(bf16[1536,768]{1,0:T(8,128)(2,1)} %get-tuple-element.240), channel_id=1, source_target_pairs={{0,8},{8,0},{16,24},{24,16},{1,9},{9,1},{17,25},{25,17},{2,10},{10... | collective-permute-start | bytes 7077896 | tf_op jit(solution)/shard_map/ppermute | solution.py:85
  231.9 30.0 %collective-permute-start.22 = (bf16[4,1,96,1536]{3,2,0,1:T(8,128)(2,1)}, bf16[4,1,96,1536]{3,2,0,1:T(8,128)(2,1)}, u32[]{:S(2)}, u32[]{:S(2)}) collective-permute-start(bf16[4,1,96,1536]{3,2,0,1:T(8,128)(2,1)} %add_convert_fusion.7), channel_id=1, source_target_pairs={{0,1},{1,0},{2,3},{3,2},{4,5},{5,4},{6,7},{7,6},{8,9},{9,8},{10,11... | collective-permute-start | bytes 3538952 | tf_op jit(solution)/shard_map/ppermute | solution.py:91
  233.4 28.5 %collective-permute-start.23 = (bf16[4,1,192,768]{3,2,0,1:T(8,128)(2,1)}, bf16[4,1,192,768]{3,2,0,1:T(8,128)(2,1)}, u32[]{:S(2)}, u32[]{:S(2)}) collective-permute-start(bf16[4,1,192,768]{3,2,0,1:T(8,128)(2,1)} %add_convert_fusion.6), channel_id=1, source_target_pairs={{0,16},{8,24},{16,0},{24,8},{1,17},{9,25},{17,1},{25,9},{2,18},{10... | collective-permute-start | bytes 3538952 | tf_op jit(solution)/shard_map/ppermute | solution.py:88
  269.2 27.4 %collective-permute-start.24 = (bf16[12,4,1,16,768]{4,3,0,1,2:T(8,128)(2,1)S(1)}, bf16[12,4,1,16,768]{4,3,0,1,2:T(8,128)(2,1)S(1)}, u32[]{:S(2)}, u32[]{:S(2)}) collective-permute-start(bf16[12,4,1,16,768]{4,3,0,1,2:T(8,128)(2,1)S(1)} %copy-done.24), channel_id=1, source_target_pairs={{0,1},{1,0},{2,3},{3,2},{4,5},{5,4},{6,7},{7,6},{8,9},{9,8},{10,11... | collective-permute-start | bytes 3538952 | tf_op jit(solution)/shard_map/ppermute | solution.py:91
  297.4 29.8 %collective-permute-start.33 = (bf16[2,768,768]{2,1,0:T(8,128)(2,1)S(1)}, bf16[2,768,768]{2,1,0:T(8,128)(2,1)S(1)}, u32[]{:S(2)}, u32[]{:S(2)}) collective-permute-start(bf16[2,768,768]{2,1,0:T(8,128)(2,1)S(1)} %pad_maximum_fusion.1), channel_id=1, source_target_pairs={{0,8},{8,0},{16,24},{24,16},{1,9},{9,1},{17,25},{25,17},{2,10},{10... | collective-permute-start | bytes 7077896 | tf_op jit(solution)/shard_map/ppermute | solution.py:85
  297.5 29.7 %collective-permute-start.29 = (bf16[12,4,1,16,768]{4,3,0,1,2:T(8,128)(2,1)S(1)}, bf16[12,4,1,16,768]{4,3,0,1,2:T(8,128)(2,1)S(1)}, u32[]{:S(2)}, u32[]{:S(2)}) collective-permute-start(bf16[12,4,1,16,768]{4,3,0,1,2:T(8,128)(2,1)S(1)} %constant_dynamic-slice_fusion.12), channel_id=1, source_target_pairs={{0,1},{1,0},{2,3},{3,2},{4,5},{5,4},{6,7},{7,6},{8,9},{9,8},{10,11... | collective-permute-start | bytes 3538952 | tf_op jit(solution)/shard_map/ppermute | solution.py:91
  301.5 25.7 %collective-permute-start.31 = (bf16[12,1,16,768]{3,2,0,1:T(8,128)(2,1)S(1)}, bf16[12,1,16,768]{3,2,0,1:T(8,128)(2,1)S(1)}, u32[]{:S(2)}, u32[]{:S(2)}) collective-permute-start(bf16[12,1,16,768]{3,2,0,1:T(8,128)(2,1)S(1)} %get-tuple-element.389), channel_id=1, source_target_pairs={{0,4},{1,5},{2,6},{3,7},{4,0},{5,1},{6,2},{7,3},{8,12},{9,13},{10,... | collective-permute-start | bytes 884744 | tf_op jit(solution)/shard_map/ppermute | solution.py:94
  301.5 25.7 %collective-permute-start.30 = (bf16[12,1,16,768]{3,2,0,1:T(8,128)(2,1)S(1)}, bf16[12,1,16,768]{3,2,0,1:T(8,128)(2,1)S(1)}, u32[]{:S(2)}, u32[]{:S(2)}) collective-permute-start(bf16[12,1,16,768]{3,2,0,1:T(8,128)(2,1)S(1)} %get-tuple-element.390), channel_id=1, source_target_pairs={{0,2},{1,3},{2,0},{3,1},{4,6},{5,7},{6,4},{7,5},{8,10},{9,11},{10,... | collective-permute-start | bytes 884744 | tf_op jit(solution)/shard_map/ppermute | solution.py:94
  330.2 30.9 %collective-permute-start.37 = (bf16[1,768,768]{2,1,0:T(8,128)(2,1)}, bf16[1,768,768]{2,1,0:T(8,128)(2,1)}, u32[]{:S(2)}, u32[]{:S(2)}) collective-permute-start(bf16[1,768,768]{2,1,0:T(8,128)(2,1)} %constant_dynamic-slice_fusion.8), channel_id=1, source_target_pairs={{0,16},{8,24},{16,0},{24,8},{1,17},{9,25},{17,1},{25,9},{2,18},{10... | collective-permute-start | bytes 3538952 | tf_op jit(solution)/shard_map/ppermute | solution.py:88
  333.9 21.3 %collective-permute-start.36 = (bf16[12,1,16,768]{3,2,0,1:T(8,128)(2,1)}, bf16[12,1,16,768]{3,2,0,1:T(8,128)(2,1)S(1)}, u32[]{:S(2)}, u32[]{:S(2)}) collective-permute-start(bf16[12,1,16,768]{3,2,0,1:T(8,128)(2,1)} %get-tuple-element.384), channel_id=1, source_target_pairs={{0,6},{1,7},{2,4},{3,5},{4,2},{5,3},{6,0},{7,1},{8,14},{9,15},{10,... | collective-permute-start | bytes 884744 | tf_op jit(solution)/shard_map/ppermute | solution.py:94
  336.2 24.9 %collective-permute-start.35 = (bf16[12,1,16,768]{3,2,0,1:T(8,128)(2,1)}, bf16[12,1,16,768]{3,2,0,1:T(8,128)(2,1)}, u32[]{:S(2)}, u32[]{:S(2)}) collective-permute-start(bf16[12,1,16,768]{3,2,0,1:T(8,128)(2,1)} %get-tuple-element.385), channel_id=1, source_target_pairs={{0,4},{1,5},{2,6},{3,7},{4,0},{5,1},{6,2},{7,3},{8,12},{9,13},{10,... | collective-permute-start | bytes 884744 | tf_op jit(solution)/shard_map/ppermute | solution.py:94
  336.3 24.9 %collective-permute-start.34 = (bf16[12,1,16,768]{3,2,0,1:T(8,128)(2,1)}, bf16[12,1,16,768]{3,2,0,1:T(8,128)(2,1)}, u32[]{:S(2)}, u32[]{:S(2)}) collective-permute-start(bf16[12,1,16,768]{3,2,0,1:T(8,128)(2,1)} %get-tuple-element.386), channel_id=1, source_target_pairs={{0,2},{1,3},{2,0},{3,1},{4,6},{5,7},{6,4},{7,5},{8,10},{9,11},{10,... | collective-permute-start | bytes 884744 | tf_op jit(solution)/shard_map/ppermute | solution.py:94
  338.3 22.8 %collective-permute-start.38 = (bf16[1,1,192,768]{3,2,1,0:T(8,128)(2,1)}, bf16[1,1,192,768]{3,2,1,0:T(8,128)(2,1)S(1)}, u32[]{:S(2)}, u32[]{:S(2)}) collective-permute-start(bf16[1,1,192,768]{3,2,1,0:T(8,128)(2,1)} %get-tuple-element.294), channel_id=1, source_target_pairs={{0,1},{1,0},{2,3},{3,2},{4,5},{5,4},{6,7},{7,6},{8,9},{9,8},{10,11... | collective-permute-start | bytes 884744 | tf_op jit(solution)/shard_map/ppermute | solution.py:91
  390.0 24.3 %collective-permute-start.46 = (bf16[1,192,768]{2,1,0:T(8,128)(2,1)}, bf16[1,192,768]{2,1,0:T(8,128)(2,1)S(1)}, u32[]{:S(2)}, u32[]{:S(2)}) collective-permute-start(bf16[1,192,768]{2,1,0:T(8,128)(2,1)} %get-tuple-element.380), channel_id=1, source_target_pairs={{0,6},{1,7},{2,4},{3,5},{4,2},{5,3},{6,0},{7,1},{8,14},{9,15},{10,... | collective-permute-start | bytes 884744 | tf_op jit(solution)/shard_map/ppermute | solution.py:94
  392.6 26.4 %collective-permute-start.45 = (bf16[1,192,768]{2,1,0:T(8,128)(2,1)}, bf16[1,192,768]{2,1,0:T(8,128)(2,1)S(1)}, u32[]{:S(2)}, u32[]{:S(2)}) collective-permute-start(bf16[1,192,768]{2,1,0:T(8,128)(2,1)} %get-tuple-element.381), channel_id=1, source_target_pairs={{0,4},{1,5},{2,6},{3,7},{4,0},{5,1},{6,2},{7,3},{8,12},{9,13},{10,... | collective-permute-start | bytes 884744 | tf_op jit(solution)/shard_map/ppermute | solution.py:94
  393.2 25.9 %collective-permute-start.44 = (bf16[1,192,768]{2,1,0:T(8,128)(2,1)}, bf16[1,192,768]{2,1,0:T(8,128)(2,1)}, u32[]{:S(2)}, u32[]{:S(2)}) collective-permute-start(bf16[1,192,768]{2,1,0:T(8,128)(2,1)} %get-tuple-element.382), channel_id=1, source_target_pairs={{0,2},{1,3},{2,0},{3,1},{4,6},{5,7},{6,4},{7,5},{8,10},{9,11},{10,... | collective-permute-start | bytes 884744 | tf_op jit(solution)/shard_map/ppermute | solution.py:94
  395.7 26.5 %collective-permute-start.47 = (bf16[192,768]{1,0:T(8,128)(2,1)S(1)}, bf16[192,768]{1,0:T(8,128)(2,1)S(1)}, u32[]{:S(2)}, u32[]{:S(2)}) collective-permute-start(bf16[192,768]{1,0:T(8,128)(2,1)S(1)} %fusion.22), channel_id=1, source_target_pairs={{4,0},{5,1},{6,2},{7,3},{8,12},{9,13},{10,14},{11,15},{20,16},{21,... | collective-permute-start | bytes 884744 | tf_op jit(solution)/shard_map/ppermute | solution.py:110
  (76 other events, 568.8 us)
Sparse Core Ops, SparseCore 0:
  11.5 106.8 all-gather.2
